TPU v7x, 128 devices: a whole 4x4x4 slice. The times are simulated.
128 devices in a mesh: segment: 4 (over z), seq: 32 (over x, y, core).
Axes of the slice: x: 4, y: 4, z: 4, core: 2. Of those that a mesh axis runs over, the one named last changes fastest.
Arguments:
- queries: bfloat16 [4, 16384, 8192], P('segment', 'seq'), may hold values from -40 to 40
- keys_in: bfloat16 [4, 16384, 1024], P('segment', 'seq'), may hold values from -6 to 6
- values_in: bfloat16 [4, 16384, 1024], P('segment', 'seq'), may hold values from -6 to 6
- random_blocks: int32 [4, 256, 3], P('segment', 'seq'), may hold values from 0 to 255, as said below
- global_blocks: int32 [4, 2], P('segment'), may hold values from 0 to 255
Outputs:
- handed: bfloat16 [4, 16384, 8192], P('segment', 'seq')
Inputs may be any that keep to these rules, and one draw needn't show every extreme that they name: random_blocks[s, j] are block numbers; the rows of one device of seq name at most 1 block lying on any single device of seq, and in every section one device of seq is named exactly once by the rows of every device.
All inputs are finite; a program needn't handle non-finite values.
Results may differ from a plain program's by a relative error of at most 0.0049.
Values may be sent and summed in bfloat16 or wider, within the bound.
No kernel may reach another device: no remote copies, remote signals or barrier semaphores. Data moves between devices by JAX's collectives and lax.ppermute only.
A program may use at most 128 MiB of HBM per device.

v0:
```python
import jax
import jax.numpy as jnp
from jax import lax
from jax.sharding import PartitionSpec as P

HEAD = 128
BLOCK = 64
GLOB = 2
RAND = 3


def padded_2(x, sides, width):
    for axis, dim in sides:
        size, length = (lax.axis_size(axis), x.shape[dim])
        up = [(i, (i + 1) % size) for i in range(size - 1)]
        down = [(j, i) for i, j in up]
        last = lax.slice_in_dim(x, length - width, length, axis=dim)
        leading = lax.slice_in_dim(x, 0, width, axis=dim)
        before = lax.ppermute(last, axis, up)
        after = lax.ppermute(leading, axis, down)
        x = jnp.concatenate([before, x, after], axis=dim)
    return x


def shifted(x, axis, by):
    length = lax.axis_size(axis)
    return lax.ppermute(x, axis, [(i, (i + by) % length) for i in range(length)])


def slot_table(owners, local, ranks, number_of_strings, cap):
    match_owner = (
        owners[None, None, :] == jnp.arange(number_of_strings, dtype=jnp.int32)[:, None, None]
    )
    match_rank = ranks[None, None, :] == jnp.arange(cap, dtype=jnp.int32)[None, :, None]
    picked = jnp.where(match_owner & match_rank & True, local[None, None, :], 0)
    return jnp.sum(picked, axis=-1)


def rank_among(owners):
    count = owners.shape[0]
    same = owners[:, None] == owners[None, :]
    earlier = jnp.arange(count)[None, :] < jnp.arange(count)[:, None]
    return jnp.sum(same & earlier, axis=1)


def per_device(queries, keys_in, values_in, random_blocks, global_blocks):
    tok = queries.shape[1]
    kvw = keys_in.shape[2]
    kvh = kvw // HEAD
    group = queries.shape[2] // kvw
    blk_dev = tok // BLOCK
    number_of_strings = lax.axis_size("seq")
    me = lax.axis_index("seq")
    nblk = blk_dev * number_of_strings
    wanted = blk_dev * RAND
    cap = max(1, (wanted + number_of_strings - 1) // number_of_strings)
    width = 2 * kvw
    joined = jnp.concatenate([keys_in[0], values_in[0]], axis=-1)
    local_blocks = joined.reshape(blk_dev, BLOCK, width)
    padded = padded_2(joined, (("seq", 0),), BLOCK)
    padded_blocks = padded.reshape(blk_dev + 2, BLOCK, width)
    window = jnp.stack([padded_blocks[:-2], padded_blocks[1:-1], padded_blocks[2:]], axis=1)
    global_row = global_blocks[0]
    offset = global_row - me * blk_dev
    mine = (offset >= 0) & (offset < blk_dev)
    chosen = local_blocks[jnp.clip(offset, 0, blk_dev - 1)]
    contrib = jnp.where(mine[:, None, None], chosen.astype(jnp.float32), 0.0)
    global_kv = lax.psum(contrib.astype(jnp.bfloat16), "seq")
    requests = random_blocks[0].reshape(wanted)
    owners = requests // blk_dev
    local = requests % blk_dev
    ranks = rank_among(owners)
    table = slot_table(owners, local, ranks, number_of_strings, cap)
    asked = lax.all_to_all(table, "seq", split_axis=0, concat_axis=0, tiled=True)
    outgoing = local_blocks[asked.reshape(number_of_strings * cap)].reshape(
        number_of_strings, cap, BLOCK, width
    )
    incoming = lax.all_to_all(outgoing, "seq", split_axis=0, concat_axis=0, tiled=True)
    fetched = incoming.reshape(number_of_strings * cap, BLOCK, width)[owners * cap + ranks]
    fetched = fetched.reshape(blk_dev, RAND, BLOCK, width)
    global_wide = jnp.broadcast_to(global_kv[None], (blk_dev, GLOB, BLOCK, width))
    all_keys = jnp.concatenate([window, global_wide, fetched], axis=1)
    keys_total = all_keys.shape[1] * BLOCK
    all_keys = all_keys.reshape(blk_dev, keys_total, width)
    rows_global = me * blk_dev + jnp.arange(blk_dev, dtype=jnp.int32)
    valid = jnp.concatenate(
        [
            (rows_global >= 1)[:, None],
            jnp.ones((blk_dev, 1), bool),
            (rows_global + 1 < nblk)[:, None],
            jnp.ones((blk_dev, GLOB + RAND), bool),
        ],
        axis=1,
    )
    mask = jnp.repeat(valid, BLOCK, axis=1)
    query_blocks = queries[0].reshape(blk_dev, BLOCK, kvh, group, HEAD)
    scale = 1.0 / HEAD**0.5
    results = []
    for head_kv in range(kvh):
        query_portion = query_blocks[:, :, head_kv]
        key_portion = all_keys[:, :, head_kv * HEAD : (head_kv + 1) * HEAD]
        value_portion = all_keys[:, :, kvw + head_kv * HEAD : kvw + (head_kv + 1) * HEAD]
        scores = (
            jnp.einsum(
                "uoic,ufc->uiof", query_portion, key_portion, preferred_element_type=jnp.float32
            )
            * scale
        )
        scores = jnp.where(mask[:, None, None, :], scores, -jnp.inf)
        top = jnp.max(scores, axis=-1, keepdims=True)
        expo = jnp.exp(scores - top)
        attention_probs = (expo / jnp.sum(expo, axis=-1, keepdims=True)).astype(jnp.bfloat16)
        result = jnp.einsum(
            "xuys,xsi->xyui", attention_probs, value_portion, preferred_element_type=jnp.float32
        )
        result = result.astype(jnp.bfloat16).reshape(tok, group * HEAD)
        results.append(result[None])
    combined = jnp.concatenate(results, axis=-1)
    combined = shifted(combined, "segment", 1)
    return combined


def solution(mesh):
    in_specs = (
        P("segment", "seq", None),
        P("segment", "seq", None),
        P("segment", "seq", None),
        P("segment", "seq", None),
        P("segment", None),
    )
    out_specs = P("segment", "seq", None)
    return jax.shard_map(
        per_device, mesh=mesh, in_specs=in_specs, out_specs=out_specs, check_vma=False
    )
```

profile of v0, /device:TPU:8, one launch (start us, length us, event | category | flops | bytes accessed | tf_op | source)
XLA Modules:
  0.0 534.8 jit_solution(8999148159508215032)
XLA Ops:
  8.4 7.5 %all-to-all-start = ((s32[32,1,1]{2,1,0:T(1,128)}), s32[32,1,1]{2,1,0:T(1,128)S(1)}, u32[]{:S(2)}, u32[]{:S(2)}) async-start(s32[32,1,1]{2,1,0:T(1,128)} %copy.83), calls=%async_computation | async-start | bytes 32768 | tf_op jit(solution)/shard_map/all_to_all | solution.py:74
  15.9 1.7 pad_maximum_fusion.4
  18.3 3.7 all-to-all-done
  22.7 5.2 gather_fusion.1
  27.8 6.2 %all-to-all-start.1 = ((bf16[32,1,64,2048]{3,2,1,0:T(8,128)(2,1)}), bf16[32,1,64,2048]{3,2,1,0:T(8,128)(2,1)}, u32[]{:S(2)}, u32[]{:S(2)}) async-start(bf16[32,1,64,2048]{3,2,1,0:T(8,128)(2,1)} %bitcast.266), calls=%async_computation.1 | async-start | bytes 16777216 | tf_op jit(solution)/shard_map/all_to_all | solution.py:78
  34.0 1.7 pad_maximum_fusion.5
  35.8 2.0 collective-permute-start
  37.8 3.5 collective-permute-start.1
  41.4 9.3 %copy.127 = bf16[64,8,64,128]{3,2,1,0:T(8,128)(2,1)} copy(bf16[64,8,64,128]{3,1,2,0:T(8,128)(2,1)} %bitcast.277) | data formatting | bytes 16777216
  51.2 7.2 %fusion.118 = (bf16[8,64,1,8,128]{4,3,2,1,0:T(8,128)(2,1)}, bf16[8,64,1,8,128]{4,3,2,1,0:T(8,128)(2,1)}, bf16[8,64,1,8,128]{4,3,2,1,0:T(8,128)(2,1)}, bf16[8,64,...) fusion(bf16[8,64,8,8,128]{4,3,2,1,0:T(8,128)(2,1)} %bitcast.267), kind=kLoop, calls=%fused_computation.207 | loop fusion | bytes 16777216 | tf_op jit(solution)/shard_map/slice | solution.py:100
  58.4 1.4 gather_fusion
  59.8 2.1 select_convert_fusion
  61.9 76.1 %collective-permute-done = bf16[64,2048]{1,0:T(8,128)(2,1)} collective-permute-done((bf16[64,2048]{1,0:T(8,128)(2,1)}, bf16[64,2048]{1,0:T(8,128)(2,1)}, u32[]{:S(2)}, u32[]{:S(2)}) %collective-permute-start) | collective-permute-done | bytes 262176 | tf_op jit(solution)/shard_map/ppermute | solution.py:19
  138.0 5.0 pad_maximum_fusion
  143.1 1.5 constant_dynamic-update-slice_fusion.2
  144.6 1.5 maximum_dynamic-update-slice_fusion
  146.1 1.6 constant_dynamic-update-slice_fusion.1
  147.6 67.2 %all-reduce.2.cloned.1.call-done = bf16[2,64,2048]{2,1,0:T(8,128)(2,1)} async-done(((bf16[2,64,2048]{2,1,0:T(8,128)(2,1)}), bf16[2,64,2048]{2,1,0:T(8,128)(2,1)}) %all-reduce.2.cloned.1.call-update) | async-done | bytes 524304 | tf_op jit(solution)/shard_map/psum | solution.py:68
  214.8 3.5 broadcast_dynamic-update-slice_fusion
  218.3 7.9 %gather_fusion.2 = bf16[24,64,2048]{2,1,0:T(8,128)(2,1)} fusion(bf16[32,64,2048]{2,1,0:T(8,128)(2,1)} %bitcast.18, s32[1024]{0:T(1024)S(1)} %pad_clamp_fusion), kind=kCustom, calls=%fused_computation.2 | custom fusion | bytes 12583008 | tf_op jit(solution)/shard_map/gather | solution.py:79
  226.2 6.6 %constant_dynamic-update-slice_fusion = bf16[8,8,64,2048]{3,2,1,0:T(8,128)(2,1)} fusion(bf16[8,8,64,2048]{3,2,1,0:T(8,128)(2,1)} %broadcast_dynamic-update-slice_fusion, bf16[8,3,64,2048]{3,2,1,0:T(8,128)(2,1)} %bitcast.268), kind=kLoop, calls=%fused_computation.149 | loop fusion | bytes 12582912 | tf_op jit(solution)/shard_map/concatenate | solution.py:82
  232.8 2.5 fusion.88
  235.3 3.1 fusion.126
  238.4 2.9 fusion.87
  242.6 2.5 fusion.89
  245.1 3.1 fusion.125
  248.2 3.0 fusion.86
  251.2 1.7 copy.100
  252.9 1.7 broadcast_in_dim_reshape.38
  254.6 2.5 fusion.90
  257.1 3.1 fusion.124
  260.2 3.0 fusion.85
  263.2 1.7 copy.98
  264.9 2.3 broadcast_in_dim_reshape.37
  267.2 2.5 fusion.91
  269.7 3.1 fusion.123
  272.8 3.0 fusion.84
  275.8 1.7 copy.96
  277.5 2.3 broadcast_in_dim_reshape.36
  279.8 2.5 fusion.92
  282.3 3.1 fusion.122
  285.4 3.0 fusion.83
  288.4 1.7 copy.94
  290.1 2.3 broadcast_in_dim_reshape.35
  292.4 2.5 fusion.93
  294.9 3.1 fusion.121
  298.1 3.2 fusion.82
  301.2 1.7 copy.92
  302.9 2.3 broadcast_in_dim_reshape.34
  305.2 2.5 fusion.94
  307.7 3.1 fusion.120
  310.9 3.0 fusion.81
  313.9 1.7 copy.90
  315.5 2.3 broadcast_in_dim_reshape.33
  317.9 2.5 fusion.95
  320.4 3.1 fusion.119
  323.5 2.9 fusion.80
  326.4 1.7 copy.88
  328.1 2.3 broadcast_in_dim_reshape.32
  330.4 1.4 constant_dynamic-update-slice_fusion.10
  331.8 1.3 constant_dynamic-update-slice_fusion.9
  336.2 1.6 collective-permute-start.2
  337.8 182.2 %collective-permute-done.2 = bf16[1,512,8192]{2,1,0:T(8,128)(2,1)} collective-permute-done((bf16[1,512,8192]{2,1,0:T(8,128)(2,1)S(1)}, bf16[1,512,8192]{2,1,0:T(8,128)(2,1)}, u32[]{:S(2)}, u32[]{:S(2)}) %collective-permute-start.2) | collective-permute-done | bytes 8388640 | tf_op jit(solution)/shard_map/ppermute | solution.py:27
  520.0 7.8 %copy.157 = bf16[1,512,8192]{2,1,0:T(8,128)(2,1)} copy(bf16[1,512,8192]{2,1,0:T(8,128)(2,1)} %collective-permute-done.2) | data formatting | bytes 16777216
  (60 shorter events, 8.0 us)
Async XLA Ops:
  8.4 13.6 %all-to-all-start = ((s32[32,1,1]{2,1,0:T(1,128)}), s32[32,1,1]{2,1,0:T(1,128)S(1)}, u32[]{:S(2)}, u32[]{:S(2)}) async-start(s32[32,1,1]{2,1,0:T(1,128)} %copy.83), calls=%async_computation | async-start | bytes 32768 | tf_op jit(solution)/shard_map/all_to_all | solution.py:74
  27.8 6.2 %copy-start = (bf16[1,512,1024]{2,1,0:T(8,128)(2,1)S(1)}, bf16[1,512,1024]{2,1,0:T(8,128)(2,1)}, u32[]{:S(2)}) copy-start(bf16[1,512,1024]{2,1,0:T(8,128)(2,1)} %param.7) | copy-start | bytes 3145732
  27.8 190.5 %all-to-all-start.1 = ((bf16[32,1,64,2048]{3,2,1,0:T(8,128)(2,1)}), bf16[32,1,64,2048]{3,2,1,0:T(8,128)(2,1)}, u32[]{:S(2)}, u32[]{:S(2)}) async-start(bf16[32,1,64,2048]{3,2,1,0:T(8,128)(2,1)} %bitcast.266), calls=%async_computation.1 | async-start | bytes 16777216 | tf_op jit(solution)/shard_map/all_to_all | solution.py:78
  34.0 180.8 %all-reduce.2.cloned.1.call-start = ((), (), s32[]{:S(2)}) async-start(), calls=%async_computation.2 | async-start | bytes 1048576 | tf_op jit(solution)/shard_map/psum | solution.py:68
  35.8 102.3 %collective-permute-start = (bf16[64,2048]{1,0:T(8,128)(2,1)}, bf16[64,2048]{1,0:T(8,128)(2,1)}, u32[]{:S(2)}, u32[]{:S(2)}) collective-permute-start(bf16[64,2048]{1,0:T(8,128)(2,1)} %get-tuple-element.16), channel_id=1, source_target_pairs={{0,1},{1,2},{2,3},{3,4},{4,5},{5,6},{6,7},{7,8},{8,9},{9,10},{10,1... | collective-permute-start | bytes 786440 | tf_op jit(solution)/shard_map/ppermute | solution.py:19
  37.8 100.2 %collective-permute-start.1 = (bf16[64,2048]{1,0:T(8,128)(2,1)S(1)}, bf16[64,2048]{1,0:T(8,128)(2,1)}, u32[]{:S(2)}, u32[]{:S(2)}) collective-permute-start(bf16[64,2048]{1,0:T(8,128)(2,1)S(1)} %get-tuple-element.15), channel_id=1, source_target_pairs={{1,0},{2,1},{3,2},{4,3},{5,4},{6,5},{7,6},{8,7},{9,8},{10,9},{11,1... | collective-permute-start | bytes 786440 | tf_op jit(solution)/shard_map/ppermute | solution.py:20
  41.4 9.8 %copy-start.12 = (s32[1,2]{1,0:T(1,128)S(1)}, s32[1,2]{1,0:T(1,128)}, u32[]{:S(2)}) copy-start(s32[1,2]{1,0:T(1,128)} %param.9) | copy-start | bytes 28
  59.8 84.8 %copy-start.1 = (bf16[1,512,1024]{2,1,0:T(8,128)(2,1)S(1)}, bf16[1,512,1024]{2,1,0:T(8,128)(2,1)}, u32[]{:S(2)}) copy-start(bf16[1,512,1024]{2,1,0:T(8,128)(2,1)} %param.6) | copy-start | bytes 3145732
  226.2 6.6 %copy-start.9 = (bf16[8,64,1,8,128]{4,3,2,1,0:T(8,128)(2,1)S(1)}, bf16[8,64,1,8,128]{4,3,2,1,0:T(8,128)(2,1)}, u32[]{:S(2)}) copy-start(bf16[8,64,1,8,128]{4,3,2,1,0:T(8,128)(2,1)} %get-tuple-element.5) | copy-start | bytes 3145732
  238.4 4.2 copy-start.8
  248.2 6.4 %copy-start.7 = (bf16[8,64,1,8,128]{4,3,2,1,0:T(8,128)(2,1)S(1)}, bf16[8,64,1,8,128]{4,3,2,1,0:T(8,128)(2,1)}, u32[]{:S(2)}) copy-start(bf16[8,64,1,8,128]{4,3,2,1,0:T(8,128)(2,1)} %get-tuple-element.7) | copy-start | bytes 3145732
  260.2 7.0 %copy-start.6 = (bf16[8,64,1,8,128]{4,3,2,1,0:T(8,128)(2,1)S(1)}, bf16[8,64,1,8,128]{4,3,2,1,0:T(8,128)(2,1)}, u32[]{:S(2)}) copy-start(bf16[8,64,1,8,128]{4,3,2,1,0:T(8,128)(2,1)} %get-tuple-element.8) | copy-start | bytes 3145732
  272.8 7.0 %copy-start.5 = (bf16[8,64,1,8,128]{4,3,2,1,0:T(8,128)(2,1)S(1)}, bf16[8,64,1,8,128]{4,3,2,1,0:T(8,128)(2,1)}, u32[]{:S(2)}) copy-start(bf16[8,64,1,8,128]{4,3,2,1,0:T(8,128)(2,1)} %get-tuple-element.9) | copy-start | bytes 3145732
  285.4 7.0 %copy-start.4 = (bf16[8,64,1,8,128]{4,3,2,1,0:T(8,128)(2,1)S(1)}, bf16[8,64,1,8,128]{4,3,2,1,0:T(8,128)(2,1)}, u32[]{:S(2)}) copy-start(bf16[8,64,1,8,128]{4,3,2,1,0:T(8,128)(2,1)} %get-tuple-element.10) | copy-start | bytes 3145732
  298.0 7.2 %copy-start.3 = (bf16[8,64,1,8,128]{4,3,2,1,0:T(8,128)(2,1)S(1)}, bf16[8,64,1,8,128]{4,3,2,1,0:T(8,128)(2,1)}, u32[]{:S(2)}) copy-start(bf16[8,64,1,8,128]{4,3,2,1,0:T(8,128)(2,1)} %get-tuple-element.11) | copy-start | bytes 3145732
  310.9 7.0 %copy-start.2 = (bf16[8,64,1,8,128]{4,3,2,1,0:T(8,128)(2,1)S(1)}, bf16[8,64,1,8,128]{4,3,2,1,0:T(8,128)(2,1)}, u32[]{:S(2)}) copy-start(bf16[8,64,1,8,128]{4,3,2,1,0:T(8,128)(2,1)} %get-tuple-element.12) | copy-start | bytes 3145732
  326.4 9.5 %copy-start.10 = (bf16[1,512,1024]{2,1,0:T(8,128)(2,1)S(1)}, bf16[1,512,1024]{2,1,0:T(8,128)(2,1)}, u32[]{:S(2)}) copy-start(bf16[1,512,1024]{2,1,0:T(8,128)(2,1)} %broadcast_in_dim_reshape.37) | copy-start | bytes 3145732
  330.4 5.4 %copy-start.11 = (bf16[1,512,1024]{2,1,0:T(8,128)(2,1)S(1)}, bf16[1,512,1024]{2,1,0:T(8,128)(2,1)}, u32[]{:S(2)}) copy-start(bf16[1,512,1024]{2,1,0:T(8,128)(2,1)} %broadcast_in_dim_reshape.36) | copy-start | bytes 3145732
  336.2 183.8 %collective-permute-start.2 = (bf16[1,512,8192]{2,1,0:T(8,128)(2,1)S(1)}, bf16[1,512,8192]{2,1,0:T(8,128)(2,1)}, u32[]{:S(2)}, u32[]{:S(2)}) collective-permute-start(bf16[1,512,8192]{2,1,0:T(8,128)(2,1)S(1)} %constant_dynamic-update-slice_fusion.3), channel_id=1, source_target_pairs={{0,32},{32,64},{64,96},{96,0},{1,33},{33,65},{65,97},{97,1},{2,34}... | collective-permute-start | bytes 25165832 | tf_op jit(solution)/shard_map/ppermute | solution.py:27
Sparse Core Ops, SparseCore 0:
  62.1 152.7 all-reduce.1
where the time goes:
time: 540 us; the launch traced here: 535 us
  waiting for transfers between devices  329 us (61%)
  local copies, waits for them, and re-layouts  88.2 us (16%)
  matrix products  43.6 us (8%)
  other arithmetic  38.9 us (7%)
  starting transfers between devices  20.9 us (4%)
  between operations  14.1 us (3%)
    ppermute x1, waiting for transfers between devices, shifted(): lax.ppermute(x, axis, [(i, (i + by) % length) for i in range(length)])  182 us
    ppermute x1, waiting for transfers between devices, padded_2(): before = lax.ppermute(last, axis, up)  76.1 us
    psum x1, waiting for transfers between devices, per_device(): global_kv = lax.psum(contrib.astype(jnp.bfloat16), 'seq')  67.2 us
    unnamed x39, local copies, waits for them, and re-layouts  30.1 us
    sub x8, other arithmetic, per_device(): expo = jnp.exp(scores - top)  25.1 us
    dot_general x8, matrix products, per_device(): jnp.einsum('xuys,xsi->xyui', attention_probs, value_portion, preferred_el...  23.8 us
    dot_general x8, matrix products, per_device(): jnp.einsum('uoic,ufc->uiof', query_portion, key_portion, preferred_elemen...  19.8 us
    another operation x8, local copies, waits for them, and re-layouts, per_device(): results.append(result[None])  16.1 us
  transfers between devices with their start and end apart: 6, of which 4 were waited for; matrix products, arithmetic and copies ran while one was open for 7% of the time, Pallas kernels for 0%

commit v1 on v0

v1 whole, which is shorter than its diff:
```python
import math

import jax
import jax.numpy as jnp
from jax import lax
from jax.experimental import pallas as pl
from jax.experimental.pallas import tpu as pltpu
from jax.sharding import PartitionSpec as P

HEAD = 128
BLOCK = 64
GLOB = 2
RAND = 3
ROWS = 512
BLOCKS = ROWS // BLOCK
GROUP = 8
PAIR = 2
TILES = 2 * PAIR
CHUNKS = 4
DEVS = 32
PIECE = 16
KEYS = 512
SLOT = TILES * BLOCK + PIECE
QW = GROUP * HEAD
BF = jnp.bfloat16
SCALE = math.log2(math.e) / math.sqrt(HEAD)
VMEM_BYTES = 48 << 20


def along(x, axis, by):
    n = lax.axis_size(axis)
    return lax.ppermute(x, axis, [(i, (i + by) % n) for i in range(n)])


def exchange(x):
    return lax.all_to_all(x, "seq", split_axis=0, concat_axis=0, tiled=True)


def params():
    return pltpu.CompilerParams(vmem_limit_bytes=VMEM_BYTES)


def first_message(owners, local, near, keys, values):
    def body(own, loc, near_ref, k0, k1, v0, v1, out):
        for i in range(DEVS):
            g, t, part = i // 16, (i % 16) // 4, i % 4
            src = ((k0, k1), (v0, v1))[t // PAIR][g]
            for c in range(CHUNKS):
                head = PAIR * c + t % PAIR
                out[i, c * PIECE : (c + 1) * PIECE] = src[
                    part * PIECE : (part + 1) * PIECE, head * HEAD : (head + 1) * HEAD
                ]
        out[:, CHUNKS * PIECE :] = jnp.zeros((DEVS, PIECE, HEAD), BF)
        for r in range(BLOCKS * RAND):
            out[own[r], CHUNKS * PIECE :] = jnp.full((PIECE, HEAD), loc[r], jnp.int32).astype(
                jnp.float32
            ).astype(BF)

    def spec(g):
        return pl.BlockSpec((BLOCK, keys.shape[1]), lambda i, own, loc, near: (near[g], 0))

    return pl.pallas_call(
        body,
        grid_spec=pltpu.PrefetchScalarGridSpec(
            num_scalar_prefetch=3,
            grid=(1,),
            in_specs=[spec(0), spec(1), spec(0), spec(1)],
            out_specs=pl.BlockSpec((DEVS, (CHUNKS + 1) * PIECE, HEAD), lambda i, *_: (0, 0, 0)),
        ),
        out_shape=jax.ShapeDtypeStruct((DEVS, (CHUNKS + 1) * PIECE, HEAD), BF),
        compiler_params=params(),
    )(owners, local, near, keys, keys, values, values)


def pack(asked, k, k_at, v, v_at, piece):
    step = 8

    def body(ask, k_ref, v_ref, p_ref, out):
        base = pl.program_id(0) * step
        for d in range(step):
            rows = pl.ds(pl.multiple_of(ask[base + d] * BLOCK, BLOCK), BLOCK)
            for t in range(TILES):
                src = (k_ref, v_ref)[t // PAIR]
                at = (t % PAIR) * HEAD
                out[d, t * BLOCK : (t + 1) * BLOCK] = src[rows, at : at + HEAD]
            out[d, TILES * BLOCK :] = p_ref[...]

    return pl.pallas_call(
        body,
        grid_spec=pltpu.PrefetchScalarGridSpec(
            num_scalar_prefetch=1,
            grid=(DEVS // step,),
            in_specs=[
                pl.BlockSpec((ROWS, PAIR * HEAD), lambda i, *_: (0, k_at)),
                pl.BlockSpec((ROWS, PAIR * HEAD), lambda i, *_: (0, v_at)),
                pl.BlockSpec((PIECE, HEAD), lambda i, *_: (0, 0)),
            ],
            out_specs=pl.BlockSpec((step, SLOT, HEAD), lambda i, *_: (i, 0, 0)),
        ),
        out_shape=jax.ShapeDtypeStruct((DEVS, SLOT, HEAD), BF),
        compiler_params=params(),
    )(asked, k, v, piece)


def attention(slots, flags, q, q_at, k, k_at, v, v_at, before, after, hk_at, hv_at, got, out=None, out_at=0, width=None):
    def body(slot, flag, q_ref, k_ref, v_ref, kb, vb, ka, va, rk, rv, gl, *rest):
        o_ref, kpad, vpad, kcat, vcat = rest[-5:]
        h = pl.program_id(0)
        for pad, own, b, a in ((kpad, k_ref, kb, ka), (vpad, v_ref, vb, va)):
            pad[0:BLOCK] = b[...]
            pad[BLOCK : BLOCK + ROWS] = own[...]
            pad[BLOCK + ROWS :] = a[...]
        for buf in range(2):
            for g in range(GLOB):
                for part in range(4):
                    at = 3 * BLOCK + g * BLOCK + part * PIECE
                    kcat[buf, at : at + PIECE] = gl[g * 16 + h * 4 + part]
                    vcat[buf, at : at + PIECE, 0:HEAD] = gl[g * 16 + (PAIR + h) * 4 + part]
            vcat[buf, :, HEAD:] = jnp.ones((KEYS, HEAD), BF)
        for j in range(BLOCKS):
            buf = j % 2
            kcat[buf, 0 : 3 * BLOCK] = kpad[j * BLOCK : (j + 3) * BLOCK]
            vcat[buf, 0 : 3 * BLOCK, 0:HEAD] = vpad[j * BLOCK : (j + 3) * BLOCK]
            for r in range(RAND):
                s = slot[j * RAND + r]
                at = (3 + GLOB + r) * BLOCK
                kcat[buf, at : at + BLOCK] = rk[s]
                vcat[buf, at : at + BLOCK, 0:HEAD] = rv[s]
            rows = slice(j * BLOCK, (j + 1) * BLOCK)
            part_heads = 2
            for u in range(GROUP // part_heads):
                heads = range(u * part_heads, (u + 1) * part_heads)
                qq = jnp.concatenate([q_ref[rows, g * HEAD : (g + 1) * HEAD] for g in heads], axis=0)
                s = lax.dot_general(
                    qq, kcat[buf], (((1,), (1,)), ((), ())), preferred_element_type=jnp.float32
                )
                if j == 0 or j == BLOCKS - 1:
                    col = lax.broadcasted_iota(jnp.int32, (1, KEYS), 1)
                    if j == 0:
                        hide = (col < BLOCK) & (flag[0] == 0)
                    else:
                        hide = (col >= 2 * BLOCK) & (col < 3 * BLOCK) & (flag[1] == 0)
                    s = jnp.where(hide, -jnp.inf, s)
                top = jnp.max(s, axis=-1, keepdims=True)
                e = jnp.exp2((s - top) * SCALE).astype(BF)
                o = lax.dot_general(
                    e, vcat[buf], (((1,), (0,)), ((), ())), preferred_element_type=jnp.float32
                )
                o = (o[:, :HEAD] / o[:, HEAD:]).astype(BF)
                for n, g in enumerate(heads):
                    o_ref[rows, g * HEAD : (g + 1) * HEAD] = o[n * BLOCK : (n + 1) * BLOCK]

    def col(shape, at):
        return pl.BlockSpec(shape, lambda h, *_: (0, at + h))

    in_specs = [
        col((ROWS, QW), q_at),
        col((ROWS, HEAD), k_at),
        col((ROWS, HEAD), v_at),
        col((BLOCK, HEAD), hk_at),
        col((BLOCK, HEAD), hv_at),
        col((BLOCK, HEAD), hk_at),
        col((BLOCK, HEAD), hv_at),
        pl.BlockSpec((DEVS, BLOCK, HEAD), lambda h, *_: (0, h, 0)),
        pl.BlockSpec((DEVS, BLOCK, HEAD), lambda h, *_: (0, PAIR + h, 0)),
        pl.BlockSpec((DEVS, PIECE, HEAD), lambda h, *_: (0, TILES * BLOCK // PIECE, 0)),
    ]
    operands = [slots, flags, q, k, v, before, before, after, after, got, got, got]
    aliases = {}
    if out is not None:
        in_specs.append(pl.BlockSpec(memory_space=pl.ANY))
        aliases = {len(operands): 0}
        operands.append(out)
    return pl.pallas_call(
        body,
        grid_spec=pltpu.PrefetchScalarGridSpec(
            num_scalar_prefetch=2,
            grid=(PAIR,),
            in_specs=in_specs,
            out_specs=pl.BlockSpec((ROWS, QW), lambda h, *_: (0, out_at + h)),
            scratch_shapes=[
                pltpu.VMEM((ROWS + 2 * BLOCK, HEAD), BF),
                pltpu.VMEM((ROWS + 2 * BLOCK, HEAD), BF),
                pltpu.VMEM((2, KEYS, HEAD), BF),
                pltpu.VMEM((2, KEYS, 2 * HEAD), BF),
            ],
        ),
        out_shape=jax.ShapeDtypeStruct((ROWS, width or PAIR * QW), BF),
        input_output_aliases=aliases,
        compiler_params=params(),
    )(*operands)


def place(part, out, at):
    step = ROWS // 4

    def body(p_ref, _, o_ref):
        o_ref[...] = p_ref[...]

    return pl.pallas_call(
        body,
        grid=(4,),
        in_specs=[
            pl.BlockSpec((step, part.shape[1]), lambda i: (i, 0)),
            pl.BlockSpec(memory_space=pl.ANY),
        ],
        out_specs=pl.BlockSpec((step, part.shape[1]), lambda i: (i, at)),
        out_shape=jax.ShapeDtypeStruct(out.shape, BF),
        input_output_aliases={1: 0},
        compiler_params=params(),
    )(part, out)


def per_device(queries, keys_in, values_in, random_blocks, global_blocks):
    q, keys, values = queries[0], keys_in[0], values_in[0]
    me = lax.axis_index("seq")
    half = 2 * PAIR * HEAD

    near_q = along(q[:, 2 * PAIR * QW : 3 * PAIR * QW], "segment", 1)
    far_q = q[:, 3 * PAIR * QW :]
    for _ in range(lax.axis_size("segment") - 1):
        far_q = along(far_q, "segment", -1)

    wanted = random_blocks[0].reshape(BLOCKS * RAND)
    owners = wanted // BLOCKS
    near = jnp.clip(global_blocks[0] - me * BLOCKS, 0, BLOCKS - 1)
    message = exchange(first_message(owners, wanted % BLOCKS, near, keys, values))
    asked = message[:, CHUNKS * PIECE, 0].astype(jnp.int32)
    holder = global_blocks[0] // BLOCKS
    pieces = lax.dynamic_index_in_dim(
        message, jnp.where(me < DEVS // GLOB, holder[0], holder[1]), axis=0, keepdims=False
    )
    flags = jnp.stack([me > 0, me < DEVS - 1]).astype(jnp.int32)

    def piece(c):
        return pieces[c * PIECE : (c + 1) * PIECE]

    low = jnp.concatenate([keys[:, :half], values[:, :half]], axis=1)
    before = along(low[ROWS - BLOCK :], "seq", 1)
    after = along(low[:BLOCK], "seq", -1)

    got = []
    for c in range(2):
        got.append(exchange(pack(asked, keys, c, values, c, piece(c))))

    notes = jnp.concatenate([asked, owners, jnp.zeros((HEAD - 56,), jnp.int32)]).astype(BF)
    tail = jnp.concatenate(
        [
            piece(2),
            piece(3),
            jnp.broadcast_to(notes[None], (PIECE, HEAD)),
            jnp.zeros((PIECE, 5 * HEAD), BF),
        ],
        axis=1,
    )
    high = jnp.concatenate([keys[:, half:], values[:, half:]], axis=1)
    moved = along(jnp.concatenate([high, tail], axis=0), "segment", 1)
    notes_e = moved[ROWS, 2 * HEAD : 3 * HEAD].astype(jnp.int32)
    asked_e, owners_e = notes_e[:DEVS], notes_e[DEVS : DEVS + BLOCKS * RAND]
    before_e = along(moved[ROWS - BLOCK : ROWS], "seq", 1)
    after_e = along(moved[:BLOCK], "seq", -1)

    sent = []
    for c in range(2):
        res = attention(
            owners, flags, q, PAIR * c, keys, PAIR * c, values, PAIR * c,
            before, after, PAIR * c, 2 * PAIR + PAIR * c, got[c],
        )
        sent.append(along(res, "segment", 1))

    out = None
    for c in range(2):
        packed = pack(asked_e, moved, c, moved, 2 + c, moved[ROWS:, c * HEAD : (c + 1) * HEAD])
        got_e = exchange(packed)
        out = attention(
            owners_e, flags, (near_q, far_q)[c], 0, moved, PAIR * c, moved, 2 * PAIR + PAIR * c,
            before_e, after_e, PAIR * c, 2 * PAIR + PAIR * c, got_e,
            out=out, out_at=2 * PAIR + PAIR * c, width=q.shape[1],
        )
    for c in range(2):
        out = place(sent[c], out, c)
    return out[None]


def solution(mesh):
    in_specs = (
        P("segment", "seq", None),
        P("segment", "seq", None),
        P("segment", "seq", None),
        P("segment", "seq", None),
        P("segment", None),
    )
    out_specs = P("segment", "seq", None)
    return jax.shard_map(
        per_device, mesh=mesh, in_specs=in_specs, out_specs=out_specs, check_vma=False
    )
```

time: 540 us -> 266 us (0.49)
  waiting for transfers between devices: 329 us -> 149 us
  local copies, waits for them, and re-layouts: 88.2 us -> 15.5 us
  Pallas kernels: 0 us -> 48.4 us
  matrix products: 43.6 us -> 0 us
  other arithmetic: 38.9 us -> 3.29 us
  starting transfers between devices: 20.9 us -> 47 us
  between operations: 14.1 us -> 1.44 us
    ppermute x3 -> x11, waiting for transfers between devices: 258 us -> 102 us  [along(): return lax.ppermute(x, axis, [(i, (i + by) % n) for i in range(n)])]
    psum x1 -> x0, waiting for transfers between devices: 67.2 us -> none  [per_device(): global_kv = lax.psum(contrib.astype(jnp.bfloat16), 'seq')]
    pallas_call x0 -> x11, Pallas kernels: none -> 48.4 us  [the longest x4 35 us: attention(): pl.pallas_call(body, grid_spec=pltpu.PrefetchScalarGridSpec(num_scalar_pr...]
    all_to_all x2 -> x5, waiting for transfers between devices: 3.69 us -> 47.4 us  [exchange(): return lax.all_to_all(x, 'seq', split_axis=0, concat_axis=0, tiled=True)]
    dot_general x16 -> x0, matrix products: 43.6 us -> none  [the longest x8 23.8 us: per_device(): jnp.einsum('xuys,xsi->xyui', attention_probs, value_portion, preferred_el...]
    sub x8 -> x0, other arithmetic: 25.1 us -> none  [per_device(): expo = jnp.exp(scores - top)]
    unnamed x39 -> x17, local copies, waits for them, and re-layouts: 30.1 us -> 8.69 us
    all_to_all x2 -> x5, starting transfers between devices: 13.7 us -> 34.1 us  [exchange(): return lax.all_to_all(x, 'seq', split_axis=0, concat_axis=0, tiled=True)]
  transfers between devices with their start and end apart: 6 -> 16, of which waited for: 4 -> 10; matrix products, arithmetic and copies ran while one was open for 7% -> 3% of each run, Pallas kernels for 0% -> 16%
where the time goes in v1:
time: 266 us; the launch traced here: 265 us
  waiting for transfers between devices  149 us (56%)
  Pallas kernels  48.4 us (18%)
  starting transfers between devices  47 us (18%)
  local copies, waits for them, and re-layouts  15.5 us (6%)
  other arithmetic  3.29 us (1%)
    ppermute x11, waiting for transfers between devices, along(): return lax.ppermute(x, axis, [(i, (i + by) % n) for i in range(n)])  102 us
    all_to_all x5, waiting for transfers between devices, exchange(): return lax.all_to_all(x, 'seq', split_axis=0, concat_axis=0, tiled=True)  47.4 us
    pallas_call x4, Pallas kernels, attention(): pl.pallas_call(body, grid_spec=pltpu.PrefetchScalarGridSpec(num_scalar_pr...  35 us
    all_to_all x5, starting transfers between devices, exchange(): return lax.all_to_all(x, 'seq', split_axis=0, concat_axis=0, tiled=True)  34.1 us
    ppermute x11, starting transfers between devices, along(): return lax.ppermute(x, axis, [(i, (i + by) % n) for i in range(n)])  12.9 us
    unnamed x17, local copies, waits for them, and re-layouts  8.69 us
    pallas_call x2, Pallas kernels, place(): pl.pallas_call(body, grid=(4,), in_specs=[pl.BlockSpec((step, part.shape[...  7.55 us
  transfers between devices with their start and end apart: 16, of which 10 were waited for; matrix products, arithmetic and copies ran while one was open for 3% of the time, Pallas kernels for 16%

profile of v1, /device:TPU:8, one launch (start us, length us, event | category | flops | bytes accessed | tf_op | source)
XLA Modules:
  0.0 265.0 jit_solution(2909421434329453505)
XLA Ops:
  0.0 0.8 copy.10
  0.8 0.1 reshape_squeeze.3
  0.9 0.7 and_select_fusion
  1.5 1.2 copy-done
  2.8 1.2 copy-done.2
  4.0 1.5 shard_map.55
  5.5 7.5 %all-to-all-start = ((bf16[32,80,128]{2,1,0:T(8,128)(2,1)}), bf16[32,80,128]{2,1,0:T(8,128)(2,1)S(1)}, u32[]{:S(2)}, u32[]{:S(2)}) async-start(bf16[32,80,128]{2,1,0:T(8,128)(2,1)} %shard_map.55), calls=%async_computation | async-start | bytes 1310720 | tf_op jit(solution)/shard_map/all_to_all | solution.py:36
  13.0 0.6 fusion.8
  14.9 9.6 %all-to-all-done = bf16[32,80,128]{2,1,0:T(8,128)(2,1)S(1)} async-done(((bf16[32,80,128]{2,1,0:T(8,128)(2,1)}), bf16[32,80,128]{2,1,0:T(8,128)(2,1)S(1)}, u32[]{:S(2)}, u32[]{:S(2)}) %all-to-all-start) | async-done | bytes 655392 | tf_op jit(solution)/shard_map/all_to_all | solution.py:36
  24.5 0.7 fusion.ask
  25.1 0.0 copy-done.1
  25.2 0.0 copy-done.3
  25.2 1.1 shard_map.58
  26.3 1.4 copy-done.7
  27.7 5.7 %all-to-all-start.2 = ((bf16[32,272,128]{2,1,0:T(8,128)(2,1)}), bf16[32,272,128]{2,1,0:T(8,128)(2,1)}, u32[]{:S(2)}, u32[]{:S(2)}) async-start(bf16[32,272,128]{2,1,0:T(8,128)(2,1)} %copy-done.7), calls=%async_computation.2 | async-start | bytes 4456448 | tf_op jit(solution)/shard_map/all_to_all | solution.py:36
  33.4 4.9 %fusion.3 = (bf16[512,2048]{1,0:T(8,128)(2,1)}, bf16[512,2048]{1,0:T(8,128)(2,1)}) fusion(bf16[512,8192]{1,0:T(8,128)(2,1)} %bitcast.45), kind=kLoop, calls=%fused_computation.27 | loop fusion | bytes 8388608 | tf_op jit(solution)/shard_map/slice | solution.py:219
  38.2 4.0 %collective-permute-start.5 = (bf16[512,2048]{1,0:T(8,128)(2,1)}, bf16[512,2048]{1,0:T(8,128)(2,1)}, u32[]{:S(2)}, u32[]{:S(2)}) collective-permute-start(bf16[512,2048]{1,0:T(8,128)(2,1)} %get-tuple-element.8), channel_id=1, source_target_pairs={{0,96},{32,0},{64,32},{96,64},{1,97},{33,1},{65,33},{97,65},{2,98}... | collective-permute-start | bytes 6291464 | tf_op jit(solution)/shard_map/ppermute | solution.py:32
  42.3 1.1 shard_map.56
  43.4 0.0 copy-start.5
  43.4 1.4 copy-done.5
  44.8 17.3 %all-to-all-done.2.rk.rv.gl = bf16[32,272,128]{2,1,0:T(8,128)(2,1)} async-done(((bf16[32,272,128]{2,1,0:T(8,128)(2,1)}), bf16[32,272,128]{2,1,0:T(8,128)(2,1)}, u32[]{:S(2)}, u32[]{:S(2)}) %all-to-all-start.2) | async-done | bytes 2228256 | tf_op jit(solution)/shard_map/all_to_all | solution.py:36
  62.0 6.5 %all-to-all-start.1 = ((bf16[32,272,128]{2,1,0:T(8,128)(2,1)}), bf16[32,272,128]{2,1,0:T(8,128)(2,1)}, u32[]{:S(2)}, u32[]{:S(2)}) async-start(bf16[32,272,128]{2,1,0:T(8,128)(2,1)} %copy-done.5), calls=%async_computation.1 | async-start | bytes 4456448 | tf_op jit(solution)/shard_map/all_to_all | solution.py:36
  68.5 1.1 fusion.6
  69.7 0.1 pad_maximum_fusion.2
  69.8 0.1 maximum_maximum_fusion
  69.9 2.0 collective-permute-start.4
  71.9 26.3 %collective-permute-done.4.k_ref.v_ref = bf16[528,1024]{1,0:T(8,128)(2,1)S(1)} collective-permute-done((bf16[528,1024]{1,0:T(8,128)(2,1)S(1)}, bf16[528,1024]{1,0:T(8,128)(2,1)S(1)}, u32[]{:S(2)}, u32[]{:S(2)}) %collective-permute-start.4) | collective-permute-done | bytes 1081376 | tf_op jit(solution)/shard_map/ppermute | solution.py:32
  98.2 1.1 shard_map.61
  99.4 1.4 copy-done.6
  100.8 0.0 all-to-all-done.1.rk.rv.gl
  100.8 7.5 %all-to-all-start.4 = ((bf16[32,272,128]{2,1,0:T(8,128)(2,1)}), bf16[32,272,128]{2,1,0:T(8,128)(2,1)}, u32[]{:S(2)}, u32[]{:S(2)}) async-start(bf16[32,272,128]{2,1,0:T(8,128)(2,1)} %copy-done.6), calls=%async_computation.4 | async-start | bytes 4456448 | tf_op jit(solution)/shard_map/all_to_all | solution.py:36
  108.3 0.0 collective-permute-done.5
  108.3 1.8 collective-permute-start.6
  110.1 1.6 pad_maximum_fusion
  111.8 0.0 collective-permute-start
  111.8 1.7 collective-permute-start.1
  113.5 0.3 collective-permute-start.10
  113.8 1.1 shard_map.60
  114.9 1.3 copy-done.4
  116.3 20.5 %all-to-all-done.4.rk.rv.gl = bf16[32,272,128]{2,1,0:T(8,128)(2,1)} async-done(((bf16[32,272,128]{2,1,0:T(8,128)(2,1)}), bf16[32,272,128]{2,1,0:T(8,128)(2,1)}, u32[]{:S(2)}, u32[]{:S(2)}) %all-to-all-start.4) | async-done | bytes 2228256 | tf_op jit(solution)/shard_map/all_to_all | solution.py:36
  136.8 6.8 %all-to-all-start.3 = ((bf16[32,272,128]{2,1,0:T(8,128)(2,1)}), bf16[32,272,128]{2,1,0:T(8,128)(2,1)}, u32[]{:S(2)}, u32[]{:S(2)}) async-start(bf16[32,272,128]{2,1,0:T(8,128)(2,1)} %copy-done.4), calls=%async_computation.3 | async-start | bytes 4456448 | tf_op jit(solution)/shard_map/all_to_all | solution.py:36
  143.6 0.1 add_convert_fusion.flag
  143.7 12.7 %collective-permute-done.6 = bf16[512,2048]{1,0:T(8,128)(2,1)} collective-permute-done((bf16[512,2048]{1,0:T(8,128)(2,1)}, bf16[512,2048]{1,0:T(8,128)(2,1)}, u32[]{:S(2)}, u32[]{:S(2)}) %collective-permute-start.6) | collective-permute-done | bytes 2097184 | tf_op jit(solution)/shard_map/ppermute | solution.py:32
  156.4 2.9 %collective-permute-start.7 = (bf16[512,2048]{1,0:T(8,128)(2,1)}, bf16[512,2048]{1,0:T(8,128)(2,1)}, u32[]{:S(2)}, u32[]{:S(2)}) collective-permute-start(bf16[512,2048]{1,0:T(8,128)(2,1)} %collective-permute-done.6), channel_id=1, source_target_pairs={{0,96},{32,0},{64,32},{96,64},{1,97},{33,1},{65,33},{97,65},{2,98}... | collective-permute-start | bytes 6291464 | tf_op jit(solution)/shard_map/ppermute | solution.py:32
  159.3 0.0 collective-permute-done.kb.vb
  159.4 0.0 collective-permute-done.1.ka.va
  159.4 8.8 %shard_map.59 = bf16[512,2048]{1,0:T(8,128)(2,1)} custom-call(s32[24]{0:T(128)S(1)} %get-tuple-element.6.own.slot, s32[2]{0:T(128)S(1)} %add_convert_fusion.flag, bf16[512,8192]{1,0:T(8,128)(2,1)} %bitcast.46, bf16[512,1024]{1,0:T(8,128)(2,1)S(1)} %bitcast.36, bf16[512,1024]{1,0:T(8,128)(2,1)S(1)} %bitcast.43, ...), custom_call_target="tpu_custom_call" | custom-call | tf_op jit(solution)/shard_map/pallas_call | solution.py:174
  168.1 0.0 collective-permute-start.3
  168.1 8.7 %shard_map.57 = bf16[512,2048]{1,0:T(8,128)(2,1)} custom-call(s32[24]{0:T(128)S(1)} %get-tuple-element.6.own.slot, s32[2]{0:T(128)S(1)} %add_convert_fusion.flag, bf16[512,8192]{1,0:T(8,128)(2,1)} %bitcast.47, bf16[512,1024]{1,0:T(8,128)(2,1)S(1)} %bitcast.37, bf16[512,1024]{1,0:T(8,128)(2,1)S(1)} %bitcast.44, ...), custom_call_target="tpu_custom_call" | custom-call | tf_op jit(solution)/shard_map/pallas_call | solution.py:174
  176.9 0.0 collective-permute-start.2
  176.9 0.1 collective-permute-start.8
  177.0 4.4 %collective-permute-done.8.kb.vb = bf16[64,1024]{1,0:T(8,128)(2,1)S(1)} collective-permute-done((bf16[64,1024]{1,0:T(8,128)(2,1)S(1)}, bf16[64,1024]{1,0:T(8,128)(2,1)S(1)}, u32[]{:S(2)}, u32[]{:S(2)}) %collective-permute-start.8) | collective-permute-done | bytes 131104 | tf_op jit(solution)/shard_map/ppermute | solution.py:32
  181.4 0.0 collective-permute-start.9
  181.4 0.1 slice_bitcast_fusion.1.slot
  181.4 2.5 collective-permute-done.9.ka.va
  183.9 0.0 collective-permute-done.10.q_ref
  183.9 8.7 %shard_map.62.rest_0_ = bf16[512,8192]{1,0:T(8,128)(2,1)} custom-call(s32[24]{0:T(128)S(1)} %slice_bitcast_fusion.1.slot, s32[2]{0:T(128)S(1)} %add_convert_fusion.flag, bf16[512,2048]{1,0:T(8,128)(2,1)} %collective-permute-done.10.q_ref, bf16[528,1024]{1,0:T(8,128)(2,1)S(1)} %collective-permute-done.4.k_ref.v_ref, ...), custom_call_target="tpu_custom_call" | custom-call | tf_op jit(solution)/shard_map/pallas_call | solution.py:174
  192.6 0.0 all-to-all-done.3.rk.rv.gl
  192.6 11.4 %collective-permute-done.7.q_ref = bf16[512,2048]{1,0:T(8,128)(2,1)} collective-permute-done((bf16[512,2048]{1,0:T(8,128)(2,1)}, bf16[512,2048]{1,0:T(8,128)(2,1)}, u32[]{:S(2)}, u32[]{:S(2)}) %collective-permute-start.7) | collective-permute-done | bytes 2097184 | tf_op jit(solution)/shard_map/ppermute | solution.py:32
  204.0 8.7 %shard_map.63._ = bf16[512,8192]{1,0:T(8,128)(2,1)} custom-call(s32[24]{0:T(128)S(1)} %slice_bitcast_fusion.1.slot, s32[2]{0:T(128)S(1)} %add_convert_fusion.flag, bf16[512,2048]{1,0:T(8,128)(2,1)} %collective-permute-done.7.q_ref, bf16[528,1024]{1,0:T(8,128)(2,1)S(1)} %collective-permute-done.4.k_ref.v_ref, ...), custom_call_target="tpu_custom_call", output_to_operand_aliasing={{}: (12, {})} | custom-call | tf_op jit(solution)/shard_map/pallas_call | solution.py:174
  212.7 5.5 %collective-permute-done.3.p_ref = bf16[512,2048]{1,0:T(8,128)(2,1)} collective-permute-done((bf16[512,2048]{1,0:T(8,128)(2,1)}, bf16[512,2048]{1,0:T(8,128)(2,1)}, u32[]{:S(2)}, u32[]{:S(2)}) %collective-permute-start.3) | collective-permute-done | bytes 2097184 | tf_op jit(solution)/shard_map/ppermute | solution.py:32
  218.2 3.8 %shard_map.64._ = bf16[512,8192]{1,0:T(8,128)(2,1)} custom-call(bf16[512,2048]{1,0:T(8,128)(2,1)} %collective-permute-done.3.p_ref, bf16[512,8192]{1,0:T(8,128)(2,1)} %shard_map.63._), custom_call_target="tpu_custom_call", output_to_operand_aliasing={{}: (1, {})} | custom-call | tf_op jit(solution)/shard_map/pallas_call | solution.py:200
  222.0 39.2 %collective-permute-done.2.p_ref = bf16[512,2048]{1,0:T(8,128)(2,1)} collective-permute-done((bf16[512,2048]{1,0:T(8,128)(2,1)}, bf16[512,2048]{1,0:T(8,128)(2,1)}, u32[]{:S(2)}, u32[]{:S(2)}) %collective-permute-start.2) | collective-permute-done | bytes 2097184 | tf_op jit(solution)/shard_map/ppermute | solution.py:32
  261.2 3.8 %shard_map.65 = bf16[512,8192]{1,0:T(8,128)(2,1)} custom-call(bf16[512,2048]{1,0:T(8,128)(2,1)} %collective-permute-done.2.p_ref, bf16[512,8192]{1,0:T(8,128)(2,1)} %shard_map.64._), custom_call_target="tpu_custom_call", output_to_operand_aliasing={{}: (1, {})} | custom-call | tf_op jit(solution)/shard_map/pallas_call | solution.py:200
  (17 shorter events, 0.1 us)
Async XLA Ops:
  1.5 1.2 copy-start
  2.7 1.2 copy-start.2
  4.0 21.2 %copy-start.1 = (bf16[1,512,1024]{2,1,0:T(8,128)(2,1)S(1)}, bf16[1,512,1024]{2,1,0:T(8,128)(2,1)}, u32[]{:S(2)}) copy-start(bf16[1,512,1024]{2,1,0:T(8,128)(2,1)} %param.6) | copy-start | bytes 3145732
  4.0 21.2 %copy-start.3 = (bf16[1,512,1024]{2,1,0:T(8,128)(2,1)S(1)}, bf16[1,512,1024]{2,1,0:T(8,128)(2,1)}, u32[]{:S(2)}) copy-start(bf16[1,512,1024]{2,1,0:T(8,128)(2,1)} %param.7) | copy-start | bytes 3145732
  5.5 19.0 %all-to-all-start = ((bf16[32,80,128]{2,1,0:T(8,128)(2,1)}), bf16[32,80,128]{2,1,0:T(8,128)(2,1)S(1)}, u32[]{:S(2)}, u32[]{:S(2)}) async-start(bf16[32,80,128]{2,1,0:T(8,128)(2,1)} %shard_map.55), calls=%async_computation | async-start | bytes 1310720 | tf_op jit(solution)/shard_map/all_to_all | solution.py:36
  26.3 1.4 copy-start.7
  27.7 34.4 %all-to-all-start.2 = ((bf16[32,272,128]{2,1,0:T(8,128)(2,1)}), bf16[32,272,128]{2,1,0:T(8,128)(2,1)}, u32[]{:S(2)}, u32[]{:S(2)}) async-start(bf16[32,272,128]{2,1,0:T(8,128)(2,1)} %copy-done.7), calls=%async_computation.2 | async-start | bytes 4456448 | tf_op jit(solution)/shard_map/all_to_all | solution.py:36
  38.2 70.1 %collective-permute-start.5 = (bf16[512,2048]{1,0:T(8,128)(2,1)}, bf16[512,2048]{1,0:T(8,128)(2,1)}, u32[]{:S(2)}, u32[]{:S(2)}) collective-permute-start(bf16[512,2048]{1,0:T(8,128)(2,1)} %get-tuple-element.8), channel_id=1, source_target_pairs={{0,96},{32,0},{64,32},{96,64},{1,97},{33,1},{65,33},{97,65},{2,98}... | collective-permute-start | bytes 6291464 | tf_op jit(solution)/shard_map/ppermute | solution.py:32
  43.4 1.4 copy-start.5
  62.0 38.7 %all-to-all-start.1 = ((bf16[32,272,128]{2,1,0:T(8,128)(2,1)}), bf16[32,272,128]{2,1,0:T(8,128)(2,1)}, u32[]{:S(2)}, u32[]{:S(2)}) async-start(bf16[32,272,128]{2,1,0:T(8,128)(2,1)} %copy-done.5), calls=%async_computation.1 | async-start | bytes 4456448 | tf_op jit(solution)/shard_map/all_to_all | solution.py:36
  69.9 28.3 %collective-permute-start.4 = (bf16[528,1024]{1,0:T(8,128)(2,1)S(1)}, bf16[528,1024]{1,0:T(8,128)(2,1)S(1)}, u32[]{:S(2)}, u32[]{:S(2)}) collective-permute-start(bf16[528,1024]{1,0:T(8,128)(2,1)S(1)} %maximum_maximum_fusion), channel_id=1, source_target_pairs={{0,32},{32,64},{64,96},{96,0},{1,33},{33,65},{65,97},{97,1},{2,34}... | collective-permute-start | bytes 3244040 | tf_op jit(solution)/shard_map/ppermute | solution.py:32
  99.3 1.4 copy-start.6
  100.8 36.0 %all-to-all-start.4 = ((bf16[32,272,128]{2,1,0:T(8,128)(2,1)}), bf16[32,272,128]{2,1,0:T(8,128)(2,1)}, u32[]{:S(2)}, u32[]{:S(2)}) async-start(bf16[32,272,128]{2,1,0:T(8,128)(2,1)} %copy-done.6), calls=%async_computation.4 | async-start | bytes 4456448 | tf_op jit(solution)/shard_map/all_to_all | solution.py:36
  108.3 48.1 %collective-permute-start.6 = (bf16[512,2048]{1,0:T(8,128)(2,1)}, bf16[512,2048]{1,0:T(8,128)(2,1)}, u32[]{:S(2)}, u32[]{:S(2)}) collective-permute-start(bf16[512,2048]{1,0:T(8,128)(2,1)} %collective-permute-done.5), channel_id=1, source_target_pairs={{0,96},{32,0},{64,32},{96,64},{1,97},{33,1},{65,33},{97,65},{2,98}... | collective-permute-start | bytes 6291464 | tf_op jit(solution)/shard_map/ppermute | solution.py:32
  111.8 47.6 %collective-permute-start = (bf16[64,1024]{1,0:T(8,128)(2,1)}, bf16[64,1024]{1,0:T(8,128)(2,1)S(1)}, u32[]{:S(2)}, u32[]{:S(2)}) collective-permute-start(bf16[64,1024]{1,0:T(8,128)(2,1)} %get-tuple-element.18), channel_id=1, source_target_pairs={{0,1},{1,2},{2,3},{3,4},{4,5},{5,6},{6,7},{7,8},{8,9},{9,10},{10,1... | collective-permute-start | bytes 393224 | tf_op jit(solution)/shard_map/ppermute | solution.py:32
  111.8 47.6 %collective-permute-start.1 = (bf16[64,1024]{1,0:T(8,128)(2,1)}, bf16[64,1024]{1,0:T(8,128)(2,1)S(1)}, u32[]{:S(2)}, u32[]{:S(2)}) collective-permute-start(bf16[64,1024]{1,0:T(8,128)(2,1)} %get-tuple-element.17), channel_id=1, source_target_pairs={{0,31},{1,0},{2,1},{3,2},{4,3},{5,4},{6,5},{7,6},{8,7},{9,8},{10,9... | collective-permute-start | bytes 393224 | tf_op jit(solution)/shard_map/ppermute | solution.py:32
  113.5 70.4 %collective-permute-start.10 = (bf16[512,2048]{1,0:T(8,128)(2,1)}, bf16[512,2048]{1,0:T(8,128)(2,1)}, u32[]{:S(2)}, u32[]{:S(2)}) collective-permute-start(bf16[512,2048]{1,0:T(8,128)(2,1)} %get-tuple-element.7), channel_id=1, source_target_pairs={{0,32},{32,64},{64,96},{96,0},{1,33},{33,65},{65,97},{97,1},{2,34}... | collective-permute-start | bytes 6291464 | tf_op jit(solution)/shard_map/ppermute | solution.py:32
  114.9 1.3 copy-start.4
  136.8 55.8 %all-to-all-start.3 = ((bf16[32,272,128]{2,1,0:T(8,128)(2,1)}), bf16[32,272,128]{2,1,0:T(8,128)(2,1)}, u32[]{:S(2)}, u32[]{:S(2)}) async-start(bf16[32,272,128]{2,1,0:T(8,128)(2,1)} %copy-done.4), calls=%async_computation.3 | async-start | bytes 4456448 | tf_op jit(solution)/shard_map/all_to_all | solution.py:36
  156.4 47.6 %collective-permute-start.7 = (bf16[512,2048]{1,0:T(8,128)(2,1)}, bf16[512,2048]{1,0:T(8,128)(2,1)}, u32[]{:S(2)}, u32[]{:S(2)}) collective-permute-start(bf16[512,2048]{1,0:T(8,128)(2,1)} %collective-permute-done.6), channel_id=1, source_target_pairs={{0,96},{32,0},{64,32},{96,64},{1,97},{33,1},{65,33},{97,65},{2,98}... | collective-permute-start | bytes 6291464 | tf_op jit(solution)/shard_map/ppermute | solution.py:32
  168.1 50.1 %collective-permute-start.3 = (bf16[512,2048]{1,0:T(8,128)(2,1)}, bf16[512,2048]{1,0:T(8,128)(2,1)}, u32[]{:S(2)}, u32[]{:S(2)}) collective-permute-start(bf16[512,2048]{1,0:T(8,128)(2,1)} %shard_map.59), channel_id=1, source_target_pairs={{0,32},{32,64},{64,96},{96,0},{1,33},{33,65},{65,97},{97,1},{2,34}... | collective-permute-start | bytes 6291464 | tf_op jit(solution)/shard_map/ppermute | solution.py:32
  176.9 84.3 %collective-permute-start.2 = (bf16[512,2048]{1,0:T(8,128)(2,1)}, bf16[512,2048]{1,0:T(8,128)(2,1)}, u32[]{:S(2)}, u32[]{:S(2)}) collective-permute-start(bf16[512,2048]{1,0:T(8,128)(2,1)} %shard_map.57), channel_id=1, source_target_pairs={{0,32},{32,64},{64,96},{96,0},{1,33},{33,65},{65,97},{97,1},{2,34}... | collective-permute-start | bytes 6291464 | tf_op jit(solution)/shard_map/ppermute | solution.py:32
  176.9 4.5 %collective-permute-start.8 = (bf16[64,1024]{1,0:T(8,128)(2,1)S(1)}, bf16[64,1024]{1,0:T(8,128)(2,1)S(1)}, u32[]{:S(2)}, u32[]{:S(2)}) collective-permute-start(bf16[64,1024]{1,0:T(8,128)(2,1)S(1)} %get-tuple-element.12), channel_id=1, source_target_pairs={{0,1},{1,2},{2,3},{3,4},{4,5},{5,6},{6,7},{7,8},{8,9},{9,10},{10,1... | collective-permute-start | bytes 393224 | tf_op jit(solution)/shard_map/ppermute | solution.py:32
  181.4 2.5 collective-permute-start.9

commit v2 on v1

v2 whole, which is shorter than its diff:
```python
import math

import jax
import jax.numpy as jnp
from jax import lax
from jax.experimental import pallas as pl
from jax.experimental.pallas import tpu as pltpu
from jax.sharding import PartitionSpec as P

HEAD = 128
BLOCK = 64
GLOB = 2
RAND = 3
ROWS = 512
BLOCKS = ROWS // BLOCK
GROUP = 8
HEADS_KV = 8
PAIRS = HEADS_KV // 2
LATE = 3
FAR = 2
DEVS = 32
PIECE = 16
KEYS = 512
WEIGHT = 20
QW = GROUP * HEAD
BF = jnp.bfloat16
SCALE = math.log2(math.e) / math.sqrt(HEAD)
VMEM_BYTES = 63 << 20
CHEAP = pl.CostEstimate(flops=0, bytes_accessed=0, transcendentals=0)


def attention_cost(heads):
    scores = heads * GROUP * ROWS * KEYS
    return pl.CostEstimate(
        flops=WEIGHT * 4 * scores * HEAD, bytes_accessed=WEIGHT * 4 * heads * ROWS * QW, transcendentals=scores
    )


def along(x, axis, by):
    n = lax.axis_size(axis)
    return lax.ppermute(x, axis, [(i, (i + by) % n) for i in range(n)])


def exchange(x):
    return lax.all_to_all(x, "seq", split_axis=0, concat_axis=0, tiled=True)


def params():
    return pltpu.CompilerParams(vmem_limit_bytes=VMEM_BYTES)


def opening(random_blocks, global_blocks, q, keys, values):
    cut = LATE * HEAD
    rest = keys.shape[1] - cut
    message_shape = (DEVS, (PAIRS + 1) * PIECE, HEAD)
    shapes = [message_shape, (ROWS, 2 * rest), (ROWS, QW)]

    def body(rb, gb, q_ref, k_ref, v_ref, out_hbm, high_hbm, far_hbm, out, high, far, glob, sems, glob_sems):
        base = lax.axis_index("seq") * BLOCKS
        globs = []
        for g in range(GLOB):
            at = jnp.minimum(jnp.maximum(gb[g] - base, 0), BLOCKS - 1) * BLOCK
            rows = pl.ds(pl.multiple_of(at, BLOCK), BLOCK)
            for n, src in enumerate((k_ref, v_ref)):
                globs.append(pltpu.make_async_copy(src.at[rows], glob.at[n, g], glob_sems.at[2 * n + g]))
        loads = [
            pltpu.make_async_copy(k_ref.at[:, pl.ds(cut, rest)], high.at[:, pl.ds(0, rest)], sems.at[0]),
            pltpu.make_async_copy(v_ref.at[:, pl.ds(cut, rest)], high.at[:, pl.ds(rest, rest)], sems.at[1]),
            pltpu.make_async_copy(q_ref.at[:, pl.ds((HEADS_KV - FAR) * QW, QW)], far, sems.at[2]),
        ]
        stores = [
            pltpu.make_async_copy(high, high_hbm, sems.at[3]),
            pltpu.make_async_copy(far, far_hbm, sems.at[4]),
            pltpu.make_async_copy(out, out_hbm, sems.at[5]),
        ]
        for c in loads + globs:
            c.start()
        out[:, PAIRS * PIECE :] = jnp.zeros((DEVS, PIECE, HEAD), BF)
        for r in range(RAND):
            for j in range(BLOCKS):
                wanted = rb[r, j]
                out[lax.shift_right_logical(wanted, 3), PAIRS * PIECE :] = jnp.full(
                    (PIECE, HEAD), wanted & (BLOCKS - 1), jnp.int32
                ).astype(jnp.float32).astype(BF)
        loads[0].wait()
        loads[1].wait()
        stores[0].start()
        loads[2].wait()
        stores[1].start()
        for c in globs:
            c.wait()
        for i in range(DEVS):
            g, t, part = i // 16, (i % 16) // 4, i % 4
            for c in range(PAIRS):
                head = 2 * c + t % 2
                out[i, c * PIECE : (c + 1) * PIECE] = glob[
                    t // 2, g, part * PIECE : (part + 1) * PIECE, head * HEAD : (head + 1) * HEAD
                ]
        stores[2].start()
        for c in stores:
            c.wait()

    here = pl.BlockSpec(memory_space=pltpu.HBM)
    return pl.pallas_call(
        body,
        grid_spec=pltpu.PrefetchScalarGridSpec(
            num_scalar_prefetch=2,
            grid=(1,),
            in_specs=[here] * 3,
            out_specs=[here] * 3,
            scratch_shapes=[pltpu.VMEM(x, BF) for x in shapes]
            + [
                pltpu.VMEM((2, GLOB, BLOCK, keys.shape[1]), BF),
                pltpu.SemaphoreType.DMA((6,)),
                pltpu.SemaphoreType.DMA((2 * GLOB,)),
            ],
        ),
        out_shape=[jax.ShapeDtypeStruct(x, BF) for x in shapes],
        compiler_params=params(),
        cost_estimate=CHEAP,
    )(random_blocks, global_blocks, q, keys, values)


def pack(asked, sources, pieces):
    step = 8
    arrays = []
    for x, _ in sources:
        if not any(x is y for y in arrays):
            arrays.append(x)
    tiles = [([x is y for y in arrays].index(True), at * HEAD) for x, at in sources]
    widths = [max(at for m, at in tiles if m == n) + HEAD for n in range(len(arrays))]
    extra = pieces.shape[0]
    slot_rows = len(tiles) * BLOCK + extra

    def body(ask, *refs):
        p_ref, out = refs[-2:]
        base = pl.program_id(0) * step
        for d in range(step):
            rows = pl.ds(pl.multiple_of(ask[base + d] * BLOCK, BLOCK), BLOCK)
            for t, (n, at) in enumerate(tiles):
                out[d, t * BLOCK : (t + 1) * BLOCK] = refs[n][rows, at : at + HEAD]
            out[d, len(tiles) * BLOCK :] = p_ref[...]

    def whole(*shape):
        return pl.BlockSpec(shape, lambda i, *_: (0, 0))

    return pl.pallas_call(
        body,
        grid_spec=pltpu.PrefetchScalarGridSpec(
            num_scalar_prefetch=1,
            grid=(DEVS // step,),
            in_specs=[whole(ROWS, w) for w in widths] + [whole(*pieces.shape)],
            out_specs=pl.BlockSpec((step, slot_rows, HEAD), lambda i, *_: (i, 0, 0)),
        ),
        out_shape=jax.ShapeDtypeStruct((DEVS, slot_rows, HEAD), BF),
        compiler_params=params(),
        cost_estimate=CHEAP,
    )(asked, *arrays, pieces)


def pack_first(holder, keys, values, message, owners):
    step = 8
    tiles = 2 * LATE
    cut = LATE * HEAD
    kept = (LATE + 1) // 2 * PIECE
    split = LATE // 2 * PIECE
    pieces = PAIRS * PIECE
    slot_rows = tiles * BLOCK + kept

    def body(held, k_ref, v_ref, ask_ref, p_ref, own_ref, out, notes):
        base = pl.program_id(0) * step
        ask = ask_ref[pl.ds(base, step), 0:1, :].astype(jnp.float32).astype(jnp.int32)
        for d in range(step):
            rows = pl.ds(pl.multiple_of(ask[d, 0, 0] * BLOCK, BLOCK), BLOCK)
            for t in range(tiles):
                src, at = (k_ref, v_ref)[t // LATE], t % LATE * HEAD
                out[d, t * BLOCK : (t + 1) * BLOCK] = src[rows, at : at + HEAD]
            out[d, tiles * BLOCK :] = p_ref[0, :kept]

        @pl.when(pl.program_id(0) == 0)
        def _():
            notes[: pieces - split] = p_ref[0, split:]
            notes[pieces - split : pieces - split + DEVS] = ask_ref[:, 0, :]
            notes[pieces - split + DEVS :] = own_ref[...]

    notes_rows = pieces - split + DEVS + PIECE
    return pl.pallas_call(
        body,
        grid_spec=pltpu.PrefetchScalarGridSpec(
            num_scalar_prefetch=1,
            grid=(DEVS // step,),
            in_specs=[
                pl.BlockSpec((ROWS, cut), lambda i, *_: (0, 0)),
                pl.BlockSpec((ROWS, cut), lambda i, *_: (0, 0)),
                pl.BlockSpec((DEVS, PIECE, HEAD), lambda i, *_: (0, PAIRS, 0)),
                pl.BlockSpec((1, pieces, HEAD), lambda i, held: (held[0], 0, 0)),
                pl.BlockSpec((PIECE, HEAD), lambda i, *_: (0, 0)),
            ],
            out_specs=[
                pl.BlockSpec((step, slot_rows, HEAD), lambda i, *_: (i, 0, 0)),
                pl.BlockSpec((notes_rows, HEAD), lambda i, *_: (0, 0)),
            ],
        ),
        out_shape=[
            jax.ShapeDtypeStruct((DEVS, slot_rows, HEAD), BF),
            jax.ShapeDtypeStruct((notes_rows, HEAD), BF),
        ],
        compiler_params=params(),
        cost_estimate=CHEAP,
    )(holder, keys, values, message, message, owners)


def attention(slots, flags, heads, first, qs, k, k_at, v, v_at, before, after, halo_at, got, got_first, got_heads, width=None, out=None):
    hk_at, hv_at = halo_at
    cuts = 1
    half = BLOCKS // cuts
    part_rows = half * BLOCK
    counts = [n for _, _, n in qs]
    starts = [sum(counts[:i]) for i in range(len(qs))]

    def body(slot, flag, *refs):
        q_refs = refs[: len(qs)]
        k_ref, v_ref, kb, vb, ka, va, rk, rv, gl, *rest = refs[len(qs) :]
        o_ref, kpad, vpad, kcat, vcat, *q_scratch = rest[-5 - (len(qs) > 1) :] if len(qs) > 1 else rest[-5:]
        h, part = pl.program_id(0), pl.program_id(1)
        if len(qs) > 1:
            q_ref = q_scratch[0]
            for i, some in enumerate(q_refs):
                @pl.when((h >= starts[i]) & (h < starts[i] + counts[i]))
                def _(some=some):
                    q_ref[...] = some[...]
        else:
            q_ref = q_refs[0]

        @pl.when(part == 0)
        def _():
            odd = lax.rem(first + h, 2)
            for pad, own, b, a in ((kpad, k_ref, kb, ka), (vpad, v_ref, vb, va)):
                pad[0:BLOCK] = b[...]
                pad[BLOCK : BLOCK + ROWS] = own[...]
                pad[BLOCK + ROWS :] = a[...]
            for buf in range(2):
                for g in range(GLOB):
                    for i in range(4):
                        at = 3 * BLOCK + g * BLOCK + i * PIECE
                        kcat[buf, at : at + PIECE] = gl[g * 16 + odd * 4 + i]
                        vcat[buf, at : at + PIECE, 0:HEAD] = gl[g * 16 + (2 + odd) * 4 + i]
                vcat[buf, :, HEAD:] = jnp.ones((KEYS, HEAD), BF)

        for j in range(half):
            buf = j % 2
            window = pl.ds(pl.multiple_of(part * part_rows + j * BLOCK, BLOCK), 3 * BLOCK)
            kcat[buf, 0 : 3 * BLOCK] = kpad[window]
            vcat[buf, 0 : 3 * BLOCK, 0:HEAD] = vpad[window]
            for r in range(RAND):
                s = slot[(part * half + j) * RAND + r]
                at = (3 + GLOB + r) * BLOCK
                kcat[buf, at : at + BLOCK] = rk[s]
                vcat[buf, at : at + BLOCK, 0:HEAD] = rv[s]
            rows = slice(j * BLOCK, (j + 1) * BLOCK)
            part_heads = 2
            for u in range(GROUP // part_heads):
                mine = range(u * part_heads, (u + 1) * part_heads)
                qq = jnp.concatenate([q_ref[rows, g * HEAD : (g + 1) * HEAD] for g in mine], axis=0)
                s = lax.dot_general(
                    qq, kcat[buf], (((1,), (1,)), ((), ())), preferred_element_type=jnp.float32
                )
                if j == 0 or j == half - 1:
                    col = lax.broadcasted_iota(jnp.int32, (1, KEYS), 1)
                    if j == 0:
                        hide = (col < BLOCK) & (flag[0] == 0) & (part == 0)
                    else:
                        hide = (col >= 2 * BLOCK) & (col < 3 * BLOCK) & (flag[1] == 0) & (part == cuts - 1)
                    s = jnp.where(hide, -jnp.inf, s)
                top = jnp.max(s, axis=-1, keepdims=True)
                e = jnp.exp2((s - top) * SCALE).astype(BF)
                o = lax.dot_general(
                    e, vcat[buf], (((1,), (0,)), ((), ())), preferred_element_type=jnp.float32
                )
                o = (o[:, :HEAD] / o[:, HEAD:]).astype(BF)
                for n, g in enumerate(mine):
                    o_ref[rows, g * HEAD : (g + 1) * HEAD] = o[n * BLOCK : (n + 1) * BLOCK]

    def col(shape, at):
        return pl.BlockSpec(shape, lambda h, *_: (0, at + h))

    def q_spec(i):
        _, at, n = qs[i]
        lo = starts[i]

        def index(h, p, *_):
            here = (h >= lo) & (h < lo + n)
            row = jnp.where(here, p, jnp.where(h < lo, 0, cuts - 1))
            return row, at + jnp.minimum(jnp.maximum(h - lo, 0), n - 1)

        return pl.BlockSpec((part_rows, QW), index)

    at = first - got_first
    glob_at = 2 * got_heads * BLOCK // PIECE - got_first // 2
    in_specs = [q_spec(i) for i in range(len(qs))] + [
        col((ROWS, HEAD), k_at),
        col((ROWS, HEAD), v_at),
        col((BLOCK, HEAD), hk_at),
        col((BLOCK, HEAD), hv_at),
        col((BLOCK, HEAD), hk_at),
        col((BLOCK, HEAD), hv_at),
        pl.BlockSpec((DEVS, BLOCK, HEAD), lambda h, *_: (0, at + h, 0)),
        pl.BlockSpec((DEVS, BLOCK, HEAD), lambda h, *_: (0, got_heads + at + h, 0)),
        pl.BlockSpec((DEVS, PIECE, HEAD), lambda h, *_: (0, glob_at + lax.div(first + h, 2), 0)),
    ]
    operands = [slots, flags, *[x for x, _, _ in qs], k, v, before, before, after, after, got, got, got]
    aliases = {}
    if out is not None:
        in_specs.append(pl.BlockSpec(memory_space=pl.ANY))
        aliases = {len(operands): 0}
        operands.append(out)
    out_at = first if width else 0
    scratch = [
        pltpu.VMEM((ROWS + 2 * BLOCK, HEAD), BF),
        pltpu.VMEM((ROWS + 2 * BLOCK, HEAD), BF),
        pltpu.VMEM((2, KEYS, HEAD), BF),
        pltpu.VMEM((2, KEYS, 2 * HEAD), BF),
    ]
    if len(qs) > 1:
        scratch.append(pltpu.VMEM((part_rows, QW), BF))
    return pl.pallas_call(
        body,
        grid_spec=pltpu.PrefetchScalarGridSpec(
            num_scalar_prefetch=2,
            grid=(heads, cuts),
            in_specs=in_specs,
            out_specs=pl.BlockSpec((part_rows, QW), lambda h, p, *_: (p, out_at + h)),
            scratch_shapes=scratch,
        ),
        out_shape=jax.ShapeDtypeStruct((ROWS, width or heads * QW), BF),
        input_output_aliases=aliases,
        compiler_params=params(),
        cost_estimate=attention_cost(heads),
    )(*operands)


def place(part, out, at, width=None):
    step = ROWS // 2

    def body(p_ref, *refs):
        refs[-1][...] = p_ref[...]

    in_specs = [pl.BlockSpec((step, part.shape[1]), lambda i: (i, 0))]
    operands = [part]
    if out is not None:
        in_specs.append(pl.BlockSpec(memory_space=pl.ANY))
        operands.append(out)
        width = out.shape[1]
    return pl.pallas_call(
        body,
        grid=(2,),
        in_specs=in_specs,
        out_specs=pl.BlockSpec((step, part.shape[1]), lambda i: (i, at)),
        out_shape=jax.ShapeDtypeStruct((ROWS, width), BF),
        input_output_aliases={} if out is None else {1: 0},
        compiler_params=params(),
        cost_estimate=CHEAP,
    )(*operands)


def tied(x, *others):
    return lax.optimization_barrier((x, *others))[0]


def per_device(queries, keys_in, values_in, random_blocks, global_blocks):
    q, keys, values = queries[0], keys_in[0], values_in[0]
    me = lax.axis_index("seq")
    early_heads = HEADS_KV - LATE
    cut = LATE * HEAD
    near_cols = slice(LATE * QW, (HEADS_KV - FAR) * QW)
    always = me >= 0
    holder = jnp.where(me < DEVS // GLOB, global_blocks[0, :1], global_blocks[0, 1:]) // BLOCKS
    owners = random_blocks[0].reshape(BLOCKS * RAND) // BLOCKS
    flags = jnp.stack([me > 0, me < DEVS - 1]).astype(jnp.int32)

    first, high, far_a = opening(random_blocks[0].T, global_blocks[0], q, keys, values)
    high = along(high, "segment", 1)
    far_a = along(far_a, "segment", -1)

    def ask(first, q):
        return exchange(first), q[:, near_cols], q[:, (HEADS_KV - 1) * QW :]

    def no_ask(first, q):
        near = jnp.zeros((ROWS, near_cols.stop - near_cols.start), BF)
        return jnp.zeros_like(first), near, jnp.zeros((ROWS, QW), BF)

    message, near_q, far_b = lax.cond(always, ask, no_ask, first, q)
    message, far_a = lax.optimization_barrier((message, far_a))
    own_row = jnp.concatenate([owners, jnp.zeros((HEAD - BLOCKS * RAND,), jnp.int32)]).astype(BF)
    packed, notes = pack_first(
        holder, keys, values, message, jnp.broadcast_to(own_row[None], (PIECE, HEAD))
    )
    notes = along(notes, "segment", 1)
    near_q = along(tied(near_q, notes), "segment", 1)
    far_b = along(far_b, "segment", -1)
    packed, high, notes, far_a = lax.optimization_barrier((packed, high, notes, far_a))
    asked_at = notes.shape[0] - PIECE - DEVS
    asked_e = notes[asked_at:-PIECE, 0].astype(jnp.int32)
    owners_e = notes[-PIECE, : BLOCKS * RAND].astype(jnp.int32)

    def edge(rows):
        return jnp.concatenate([keys[rows, :cut], values[rows, :cut], high[rows]], axis=1)

    def middle(packed, far, asked_e, pieces_e):
        got = exchange(packed)
        far = along(far, "segment", -1)
        before = along(edge(slice(ROWS - BLOCK, ROWS)), "seq", 1)
        after = along(edge(slice(0, BLOCK)), "seq", -1)
        packed_e = pack(asked_e, [(high, c) for c in range(2 * early_heads)], pieces_e)
        return got, far, before, after, packed_e

    def no_middle(packed, far, asked_e, pieces_e):
        side = jnp.zeros((BLOCK, 2 * keys.shape[1]), BF)
        packed_e = jnp.zeros((DEVS, 2 * early_heads * BLOCK + pieces_e.shape[0], HEAD), BF)
        return jnp.zeros_like(packed), jnp.zeros_like(far), side, side, packed_e

    got, far_a, before, after, packed = lax.cond(
        always, middle, no_middle, packed, far_a, asked_e, notes[:asked_at]
    )
    got_e = exchange(packed)

    sent = []
    slots = owners
    far_a = along(far_a, "segment", -1)
    far_b = along(tied(far_b, got), "segment", -1)
    for h in range(LATE):
        if h == 1:
            slots, near_q, far_b = lax.optimization_barrier((slots, near_q, far_b))
        res = attention(
            slots, flags, 1, h, [(q, h, 1)], keys, h, values, h, before, after, (h, LATE + h), got, 0, LATE
        )
        slots = tied(owners, res)
        sent.append(along(res, "segment", 1))
    far_b = along(tied(far_b, res), "segment", -1)

    out = place(tied(sent[0], res), None, 0, q.shape[1])
    out = place(tied(sent[1], res), out, 1)
    parts = [(near_q, 0, early_heads - FAR), (far_a, 0, 1), (far_b, 0, 1)]
    out = attention(
        owners_e, flags, early_heads, LATE, parts, high, 0, high, early_heads, before, after,
        (2 * LATE, 2 * LATE + early_heads), got_e, LATE, early_heads, width=q.shape[1], out=out,
    )
    for h in range(2, LATE):
        out = place(sent[h], out, h)
    return out[None]


def solution(mesh):
    in_specs = (
        P("segment", "seq", None),
        P("segment", "seq", None),
        P("segment", "seq", None),
        P("segment", "seq", None),
        P("segment", None),
    )
    out_specs = P("segment", "seq", None)
    return jax.shard_map(
        per_device, mesh=mesh, in_specs=in_specs, out_specs=out_specs, check_vma=False
    )
```

time: 266 us -> 202 us (0.76)
  waiting for transfers between devices: 149 us -> 89.1 us
  Pallas kernels: 48.4 us -> 56.4 us
  starting transfers between devices: 47 us -> 40.7 us
  local copies, waits for them, and re-layouts: 15.5 us -> 11.1 us
    all_to_all x5 -> x3, waiting for transfers between devices: 47.4 us -> 11.9 us  [exchange(): return lax.all_to_all(x, 'seq', split_axis=0, concat_axis=0, tiled=True)]
    ppermute x11 -> x14, waiting for transfers between devices: 102 us -> 77.2 us  [along(): return lax.ppermute(x, axis, [(i, (i + by) % n) for i in range(n)])]
    all_to_all x5 -> x3, starting transfers between devices: 34.1 us -> 22.4 us  [exchange(): return lax.all_to_all(x, 'seq', split_axis=0, concat_axis=0, tiled=True)]
    unnamed x17 -> x6, local copies, waits for them, and re-layouts: 8.69 us -> 1.36 us
    ppermute x11 -> x14, starting transfers between devices: 12.9 us -> 18.3 us  [along(): return lax.ppermute(x, axis, [(i, (i + by) % n) for i in range(n)])]
    pallas_call x3 -> x5, Pallas kernels: 9.07 us -> 13.7 us  [the longest x3 6.14 us: place(): pl.pallas_call(body, grid=(2,), in_specs=in_specs, out_specs=pl.BlockSpec...]
    slice x8 -> x6, local copies, waits for them, and re-layouts: 6.68 us -> 9.09 us  [the longest x2 5.99 us: ask(): return (exchange(first), q[:, near_cols], q[:, (HEADS_KV - 1) * QW:])]
  transfers between devices with their start and end apart: 16 -> 17, of which waited for: 10 -> 9; matrix products, arithmetic and copies ran while one was open for 3% -> 6% of each run, Pallas kernels for 16% -> 25%
where the time goes in v2:
time: 202 us; the launch traced here: 201 us
  waiting for transfers between devices  89.1 us (44%)
  Pallas kernels  56.4 us (28%)
  starting transfers between devices  40.7 us (20%)
  local copies, waits for them, and re-layouts  11.1 us (5%)
  other arithmetic  2.39 us (1%)
    ppermute x14, waiting for transfers between devices, along(): return lax.ppermute(x, axis, [(i, (i + by) % n) for i in range(n)])  77.2 us
    pallas_call x4, Pallas kernels, attention(): pl.pallas_call(body, grid_spec=pltpu.PrefetchScalarGridSpec(num_scalar_pr...  37.5 us
    all_to_all x3, starting transfers between devices, exchange(): return lax.all_to_all(x, 'seq', split_axis=0, concat_axis=0, tiled=True)  22.4 us
    ppermute x14, starting transfers between devices, along(): return lax.ppermute(x, axis, [(i, (i + by) % n) for i in range(n)])  18.3 us
    all_to_all x3, waiting for transfers between devices, exchange(): return lax.all_to_all(x, 'seq', split_axis=0, concat_axis=0, tiled=True)  11.9 us
    pallas_call x3, Pallas kernels, place(): pl.pallas_call(body, grid=(2,), in_specs=in_specs, out_specs=pl.BlockSpec...  6.14 us
    slice x2, local copies, waits for them, and re-layouts, ask(): return (exchange(first), q[:, near_cols], q[:, (HEADS_KV - 1) * QW:])  5.99 us
    pallas_call x1, Pallas kernels, pack(): pl.pallas_call(body, grid_spec=pltpu.PrefetchScalarGridSpec(num_scalar_pr...  5.2 us
  transfers between devices with their start and end apart: 17, of which 9 were waited for; matrix products, arithmetic and copies ran while one was open for 6% of the time, Pallas kernels for 25%

profile of v2, /device:TPU:8, one launch (start us, length us, event | category | flops | bytes accessed | tf_op | source)
XLA Modules:
  0.0 201.1 jit_solution(105662059645422534)
XLA Ops:
  0.0 1.3 copy.13
  1.3 0.0 copy-start.1
  1.3 0.0 copy-start
  1.3 3.9 %shard_map.55 = (bf16[32,80,128]{2,1,0:T(8,128)(2,1)}, bf16[512,1280]{1,0:T(8,128)(2,1)}, bf16[512,1024]{1,0:T(8,128)(2,1)}) custom-call(s32[3,8]{1,0:T(4,128)} %bitcast.35, s32[2]{0:T(128)} %bitcast.36, bf16[512,8192]{1,0:T(8,128)(2,1)} %bitcast.18, bf16[512,1024]{1,0:T(8,128)(2,1)} %bitcast.23, bf16[512,1024]{1,0:T(8,128)(2,1)} %bitcast.29), custom_call_target="tpu_custom_call" | custom-call | tf_op jit(solution)/shard_map/pallas_call | solution.py:104
  5.2 4.4 %collective-permute-start.3 = (bf16[512,1024]{1,0:T(8,128)(2,1)}, bf16[512,1024]{1,0:T(8,128)(2,1)}, u32[]{:S(2)}, u32[]{:S(2)}) collective-permute-start(bf16[512,1024]{1,0:T(8,128)(2,1)} %get-tuple-element.65), channel_id=1, source_target_pairs={{0,96},{32,0},{64,32},{96,64},{1,97},{33,1},{65,33},{97,65},{2,98}... | collective-permute-start | bytes 3145736 | tf_op jit(solution)/shard_map/ppermute | solution.py:41
  9.6 0.0 collective-permute-start.4
  9.6 0.0 copy-done.1
  9.6 0.6 fusion.4
  11.5 0.0 copy-done
  11.5 0.1 copy.10
  11.6 0.1 reshape_squeeze.3
  11.7 0.6 fusion
  12.2 19.1 %conditional.2 = (bf16[32,80,128]{2,1,0:T(8,128)(2,1)}, bf16[512,3072]{1,0:T(8,128)(2,1)}, bf16[512,1024]{1,0:T(8,128)(2,1)}) conditional(s32[]{:T(128)} %convert_element_type.21, () %tuple.32, (bf16[32,80,128]{2,1,0:T(8,128)(2,1)}, bf16[512,8192]{1,0:T(8,128)(2,1)}) %tuple.56), branch_computations={%region_0.1_spmd, %region_1.2_spmd} | conditional | bytes 10354744 | solution.py:392
  12.2 7.6 %all-to-all-start = ((bf16[32,80,128]{2,1,0:T(8,128)(2,1)}), bf16[32,80,128]{2,1,0:T(8,128)(2,1)}, u32[]{:S(2)}, u32[]{:S(2)}) async-start(bf16[32,80,128]{2,1,0:T(8,128)(2,1)} %get-tuple-element.26), calls=%async_computation | async-start | bytes 1310720 | tf_op jit(solution)/shard_map/cond/branch_1_fun/all_to_all | solution.py:45
  19.8 2.3 %slice.29 = bf16[512,1024]{1,0:T(8,128)(2,1)} slice(bf16[512,8192]{1,0:T(8,128)(2,1)} %get-tuple-element.27), slice={[0:512], [7168:8192]} | slice | bytes 2097152 | tf_op jit(solution)/shard_map/cond/branch_1_fun/slice | solution.py:386
  22.1 3.7 %slice.28 = bf16[512,3072]{1,0:T(8,128)(2,1)} slice(bf16[512,8192]{1,0:T(8,128)(2,1)} %get-tuple-element.27), slice={[0:512], [3072:6144]} | slice | bytes 6291456 | tf_op jit(solution)/shard_map/cond/branch_1_fun/slice | solution.py:386
  25.8 5.5 %all-to-all-done = bf16[32,80,128]{2,1,0:T(8,128)(2,1)} async-done(((bf16[32,80,128]{2,1,0:T(8,128)(2,1)}), bf16[32,80,128]{2,1,0:T(8,128)(2,1)}, u32[]{:S(2)}, u32[]{:S(2)}) %all-to-all-start) | async-done | bytes 655392 | tf_op jit(solution)/shard_map/cond/branch_1_fun/all_to_all | solution.py:45
  31.3 1.0 collective-permute-done.3
  32.3 0.6 broadcast_in_dim.4.own_ref
  32.9 3.7 %shard_map.56 = (bf16[32,416,128]{2,1,0:T(8,128)(2,1)}, bf16[96,128]{1,0:T(8,128)(2,1)}) custom-call(s32[1]{0:T(128)S(6)} %select_n.21.held, bf16[512,1024]{1,0:T(8,128)(2,1)} %bitcast.24, bf16[512,1024]{1,0:T(8,128)(2,1)} %bitcast.30, bf16[32,80,128]{2,1,0:T(8,128)(2,1)} %get-tuple-element.66.ask_ref.p_ref, ...), custom_call_target="tpu_custom_call" | custom-call | tf_op jit(solution)/shard_map/pallas_call | solution.py:187
  36.6 0.5 collective-permute-start.5
  37.1 5.2 %collective-permute-done.5 = bf16[96,128]{1,0:T(8,128)(2,1)S(1)} collective-permute-done((bf16[96,128]{1,0:T(8,128)(2,1)}, bf16[96,128]{1,0:T(8,128)(2,1)S(1)}, u32[]{:S(2)}, u32[]{:S(2)}) %collective-permute-start.5) | collective-permute-done | bytes 24608 | tf_op jit(solution)/shard_map/ppermute | solution.py:41
  42.3 0.0 collective-permute-start.6
  42.3 3.2 %collective-permute-start.7 = (bf16[512,1024]{1,0:T(8,128)(2,1)}, bf16[512,1024]{1,0:T(8,128)(2,1)}, u32[]{:S(2)}, u32[]{:S(2)}) collective-permute-start(bf16[512,1024]{1,0:T(8,128)(2,1)} %get-tuple-element.81), channel_id=1, source_target_pairs={{0,96},{32,0},{64,32},{96,64},{1,97},{33,1},{65,33},{97,65},{2,98}... | collective-permute-start | bytes 3145736 | tf_op jit(solution)/shard_map/ppermute | solution.py:41
  45.5 0.6 add_convert_fusion.flag
  46.1 0.0 collective-permute-done.4.refs_3_.refs_4_
  46.1 50.8 %conditional.3 = (bf16[32,416,128]{2,1,0:T(8,128)(2,1)}, bf16[512,1024]{1,0:T(8,128)(2,1)}, bf16[64,2048]{1,0:T(8,128)(2,1)}, bf16[64,2048]{1,0:T(8,128)(2,1)}, bf16[32,688,128]{2,1,0:T(8,128)(2,1)}) conditional(s32[]{:T(128)} %convert_element_type.21, () %tuple.31, (bf16[32,416,128]{2,1,0:T(8,128)(2,1)}, bf16[512,1024]{1,0:T(8,128)(2,1)}, ...), branch_computations={%region_2.3_spmd, %region_3.4_spmd} | conditional | flops 1572896 | bytes 18637184 | solution.py:422
  46.1 7.6 %all-to-all-start.1 = ((bf16[32,416,128]{2,1,0:T(8,128)(2,1)}), bf16[32,416,128]{2,1,0:T(8,128)(2,1)}, u32[]{:S(2)}, u32[]{:S(2)}) async-start(bf16[32,416,128]{2,1,0:T(8,128)(2,1)} %get-tuple-element.28), calls=%async_computation.1 | async-start | bytes 6815744 | tf_op jit(solution)/shard_map/cond/branch_1_fun/all_to_all | solution.py:45
  53.7 0.9 collective-permute-start
  54.6 1.0 fusion.1
  55.6 0.9 fusion.2
  56.5 0.1 collective-permute-start.1
  56.7 1.8 collective-permute-start.2
  58.5 0.6 slice.37.refs_1_
  59.1 0.6 convert_reduce_fusion.ask
  59.7 5.2 %branch_1_fun.1 = bf16[32,688,128]{2,1,0:T(8,128)(2,1)} custom-call(s32[32]{0:T(128)} %convert_reduce_fusion.ask, bf16[512,1280]{1,0:T(8,128)(2,1)} %get-tuple-element.32.refs_0_, bf16[48,128]{1,0:T(8,128)(2,1)} %slice.37.refs_1_), custom_call_target="tpu_custom_call" | custom-call | tf_op jit(solution)/shard_map/cond/branch_1_fun/pallas_call | solution.py:147
  64.9 30.9 %collective-permute-done.1 = bf16[64,2048]{1,0:T(8,128)(2,1)} collective-permute-done((bf16[64,2048]{1,0:T(8,128)(2,1)S(1)}, bf16[64,2048]{1,0:T(8,128)(2,1)}, u32[]{:S(2)}, u32[]{:S(2)}) %collective-permute-start.1) | collective-permute-done | bytes 262176 | tf_op jit(solution)/shard_map/cond/branch_1_fun/ppermute | solution.py:41
  95.8 0.0 collective-permute-done.2
  95.8 0.0 collective-permute-done
  95.8 1.1 all-to-all-done.1
  96.9 0.0 collective-permute-done.7
  96.9 7.2 %all-to-all-start.2 = ((bf16[32,688,128]{2,1,0:T(8,128)(2,1)}), bf16[32,688,128]{2,1,0:T(8,128)(2,1)}, u32[]{:S(2)}, u32[]{:S(2)}) async-start(bf16[32,688,128]{2,1,0:T(8,128)(2,1)} %get-tuple-element.89), calls=%async_computation.2 | async-start | bytes 11272192 | tf_op jit(solution)/shard_map/all_to_all | solution.py:45
  104.2 0.9 collective-permute-start.8
  105.1 6.1 %shard_map.57 = bf16[512,1024]{1,0:T(8,128)(2,1)} custom-call(s32[24]{0:T(128)} %get-tuple-element.84.slot, s32[2]{0:T(128)} %add_convert_fusion.flag, bf16[512,8192]{1,0:T(8,128)(2,1)} %bitcast.20, bf16[512,1024]{1,0:T(8,128)(2,1)} %bitcast.26, bf16[512,1024]{1,0:T(8,128)(2,1)} %bitcast.32, ...), custom_call_target="tpu_custom_call" | custom-call | flops 21474836480 | bytes 41943040 | tf_op jit(solution)/shard_map/pallas_call | solution.py:326
  111.2 1.2 collective-permute-start.13
  112.4 2.0 %collective-permute-start.10 = (bf16[512,1024]{1,0:T(8,128)(2,1)}, bf16[512,1024]{1,0:T(8,128)(2,1)}, u32[]{:S(2)}, u32[]{:S(2)}) collective-permute-start(bf16[512,1024]{1,0:T(8,128)(2,1)} %get-tuple-element.86), channel_id=1, source_target_pairs={{0,96},{32,0},{64,32},{96,64},{1,97},{33,1},{65,33},{97,65},{2,98}... | collective-permute-start | bytes 3145736 | tf_op jit(solution)/shard_map/ppermute | solution.py:41
  114.5 16.1 %collective-permute-done.8 = bf16[512,1024]{1,0:T(8,128)(2,1)} collective-permute-done((bf16[512,1024]{1,0:T(8,128)(2,1)}, bf16[512,1024]{1,0:T(8,128)(2,1)}, u32[]{:S(2)}, u32[]{:S(2)}) %collective-permute-start.8) | collective-permute-done | bytes 1048608 | tf_op jit(solution)/shard_map/ppermute | solution.py:41
  130.6 0.0 collective-permute-done.6.refs_0_
  130.6 6.2 %shard_map.58 = bf16[512,1024]{1,0:T(8,128)(2,1)} custom-call(s32[24]{0:T(128)} %get-tuple-element.84.slot, s32[2]{0:T(128)} %add_convert_fusion.flag, bf16[512,8192]{1,0:T(8,128)(2,1)} %bitcast.21, bf16[512,1024]{1,0:T(8,128)(2,1)} %bitcast.27, bf16[512,1024]{1,0:T(8,128)(2,1)} %bitcast.33, ...), custom_call_target="tpu_custom_call" | custom-call | flops 21474836480 | bytes 41943040 | tf_op jit(solution)/shard_map/pallas_call | solution.py:326
  136.7 0.0 collective-permute-start.12
  136.7 6.2 %shard_map.59 = bf16[512,1024]{1,0:T(8,128)(2,1)} custom-call(s32[24]{0:T(128)} %get-tuple-element.84.slot, s32[2]{0:T(128)} %add_convert_fusion.flag, bf16[512,8192]{1,0:T(8,128)(2,1)} %bitcast.22, bf16[512,1024]{1,0:T(8,128)(2,1)} %bitcast.28, bf16[512,1024]{1,0:T(8,128)(2,1)} %bitcast.34, ...), custom_call_target="tpu_custom_call" | custom-call | flops 21474836480 | bytes 41943040 | tf_op jit(solution)/shard_map/pallas_call | solution.py:326
  142.9 3.2 %collective-permute-start.11 = (bf16[512,1024]{1,0:T(8,128)(2,1)}, bf16[512,1024]{1,0:T(8,128)(2,1)}, u32[]{:S(2)}, u32[]{:S(2)}) collective-permute-start(bf16[512,1024]{1,0:T(8,128)(2,1)} %collective-permute-done.8), channel_id=1, source_target_pairs={{0,96},{32,0},{64,32},{96,64},{1,97},{33,1},{65,33},{97,65},{2,98}... | collective-permute-start | bytes 3145736 | tf_op jit(solution)/shard_map/ppermute | solution.py:41
  146.1 0.5 bitcast_convert_fusion.slot
  146.7 0.0 collective-permute-start.9
  146.7 0.0 collective-permute-done.13.p_ref
  146.7 2.0 %shard_map.60.refs_0_ = bf16[512,8192]{1,0:T(8,128)(2,1)} custom-call(bf16[512,1024]{1,0:T(8,128)(2,1)} %collective-permute-done.13.p_ref), custom_call_target="tpu_custom_call" | custom-call | tf_op jit(solution)/shard_map/pallas_call | solution.py:354
  148.7 15.6 %collective-permute-done.12.p_ref = bf16[512,1024]{1,0:T(8,128)(2,1)} collective-permute-done((bf16[512,1024]{1,0:T(8,128)(2,1)}, bf16[512,1024]{1,0:T(8,128)(2,1)}, u32[]{:S(2)}, u32[]{:S(2)}) %collective-permute-start.12) | collective-permute-done | bytes 1048608 | tf_op jit(solution)/shard_map/ppermute | solution.py:41
  164.3 2.0 %shard_map.61.refs_12_ = bf16[512,8192]{1,0:T(8,128)(2,1)} custom-call(bf16[512,1024]{1,0:T(8,128)(2,1)} %collective-permute-done.12.p_ref, bf16[512,8192]{1,0:T(8,128)(2,1)} %shard_map.60.refs_0_), custom_call_target="tpu_custom_call", output_to_operand_aliasing={{}: (1, {})} | custom-call | tf_op jit(solution)/shard_map/pallas_call | solution.py:354
  166.4 0.0 collective-permute-done.10.refs_1_
  166.4 8.3 %collective-permute-done.11.refs_2_ = bf16[512,1024]{1,0:T(8,128)(2,1)} collective-permute-done((bf16[512,1024]{1,0:T(8,128)(2,1)}, bf16[512,1024]{1,0:T(8,128)(2,1)}, u32[]{:S(2)}, u32[]{:S(2)}) %collective-permute-start.11) | collective-permute-done | bytes 1048608 | tf_op jit(solution)/shard_map/ppermute | solution.py:41
  174.7 5.3 %all-to-all-done.2.refs_9_.refs_10_.refs_11_ = bf16[32,688,128]{2,1,0:T(8,128)(2,1)} async-done(((bf16[32,688,128]{2,1,0:T(8,128)(2,1)}), bf16[32,688,128]{2,1,0:T(8,128)(2,1)}, u32[]{:S(2)}, u32[]{:S(2)}) %all-to-all-start.2) | async-done | bytes 5636128 | tf_op jit(solution)/shard_map/all_to_all | solution.py:45
  180.0 19.0 %shard_map.62.refs_0_ = bf16[512,8192]{1,0:T(8,128)(2,1)} custom-call(s32[24]{0:T(128)} %bitcast_convert_fusion.slot, s32[2]{0:T(128)} %add_convert_fusion.flag, bf16[512,3072]{1,0:T(8,128)(2,1)} %collective-permute-done.6.refs_0_, bf16[512,1024]{1,0:T(8,128)(2,1)} %collective-permute-done.10.refs_1_, ...), custom_call_target="tpu_custom_call", output_to_operand_aliasing={{}: (14, {})} | custom-call | flops 107374182400 | bytes 209715200 | tf_op jit(solution)/shard_map/pallas_call | solution.py:326
  199.0 0.0 collective-permute-done.9.p_ref
  199.0 2.1 %shard_map.63 = bf16[512,8192]{1,0:T(8,128)(2,1)} custom-call(bf16[512,1024]{1,0:T(8,128)(2,1)} %collective-permute-done.9.p_ref, bf16[512,8192]{1,0:T(8,128)(2,1)} %shard_map.62.refs_0_), custom_call_target="tpu_custom_call", output_to_operand_aliasing={{}: (1, {})} | custom-call | tf_op jit(solution)/shard_map/pallas_call | solution.py:354
  (3 shorter events, 0.0 us)
Async XLA Ops:
  1.3 8.3 %copy-start.1 = (s32[1,2]{1,0:T(1,128)S(1)}, s32[1,2]{1,0:T(1,128)}, u32[]{:S(2)}) copy-start(s32[1,2]{1,0:T(1,128)} %param.13) | copy-start | bytes 28
  1.3 10.2 %copy-start = (s32[1,8,3]{1,0,2:T(1,128)S(1)}, s32[1,8,3]{1,0,2:T(1,128)}, u32[]{:S(2)}) copy-start(s32[1,8,3]{1,0,2:T(1,128)} %param.12) | copy-start | bytes 292
  5.2 27.1 %collective-permute-start.3 = (bf16[512,1024]{1,0:T(8,128)(2,1)}, bf16[512,1024]{1,0:T(8,128)(2,1)}, u32[]{:S(2)}, u32[]{:S(2)}) collective-permute-start(bf16[512,1024]{1,0:T(8,128)(2,1)} %get-tuple-element.65), channel_id=1, source_target_pairs={{0,96},{32,0},{64,32},{96,64},{1,97},{33,1},{65,33},{97,65},{2,98}... | collective-permute-start | bytes 3145736 | tf_op jit(solution)/shard_map/ppermute | solution.py:41
  9.6 36.5 %collective-permute-start.4 = (bf16[512,1280]{1,0:T(8,128)(2,1)}, bf16[512,1280]{1,0:T(8,128)(2,1)}, u32[]{:S(2)}, u32[]{:S(2)}) collective-permute-start(bf16[512,1280]{1,0:T(8,128)(2,1)} %get-tuple-element.68), channel_id=1, source_target_pairs={{0,32},{32,64},{64,96},{96,0},{1,33},{33,65},{65,97},{97,1},{2,34}... | collective-permute-start | bytes 3932168 | tf_op jit(solution)/shard_map/ppermute | solution.py:41
  12.2 19.1 %all-to-all-start = ((bf16[32,80,128]{2,1,0:T(8,128)(2,1)}), bf16[32,80,128]{2,1,0:T(8,128)(2,1)}, u32[]{:S(2)}, u32[]{:S(2)}) async-start(bf16[32,80,128]{2,1,0:T(8,128)(2,1)} %get-tuple-element.26), calls=%async_computation | async-start | bytes 1310720 | tf_op jit(solution)/shard_map/cond/branch_1_fun/all_to_all | solution.py:45
  36.6 5.7 %collective-permute-start.5 = (bf16[96,128]{1,0:T(8,128)(2,1)}, bf16[96,128]{1,0:T(8,128)(2,1)S(1)}, u32[]{:S(2)}, u32[]{:S(2)}) collective-permute-start(bf16[96,128]{1,0:T(8,128)(2,1)} %get-tuple-element.69), channel_id=1, source_target_pairs={{0,32},{32,64},{64,96},{96,0},{1,33},{33,65},{65,97},{97,1},{2,34}... | collective-permute-start | bytes 73736 | tf_op jit(solution)/shard_map/ppermute | solution.py:41
  42.3 88.3 %collective-permute-start.6 = (bf16[512,3072]{1,0:T(8,128)(2,1)}, bf16[512,3072]{1,0:T(8,128)(2,1)}, u32[]{:S(2)}, u32[]{:S(2)}) collective-permute-start(bf16[512,3072]{1,0:T(8,128)(2,1)} %get-tuple-element.80), channel_id=1, source_target_pairs={{0,32},{32,64},{64,96},{96,0},{1,33},{33,65},{65,97},{97,1},{2,34}... | collective-permute-start | bytes 9437192 | tf_op jit(solution)/shard_map/ppermute | solution.py:41
  42.3 54.7 %collective-permute-start.7 = (bf16[512,1024]{1,0:T(8,128)(2,1)}, bf16[512,1024]{1,0:T(8,128)(2,1)}, u32[]{:S(2)}, u32[]{:S(2)}) collective-permute-start(bf16[512,1024]{1,0:T(8,128)(2,1)} %get-tuple-element.81), channel_id=1, source_target_pairs={{0,96},{32,0},{64,32},{96,64},{1,97},{33,1},{65,33},{97,65},{2,98}... | collective-permute-start | bytes 3145736 | tf_op jit(solution)/shard_map/ppermute | solution.py:41
  46.1 50.8 %all-to-all-start.1 = ((bf16[32,416,128]{2,1,0:T(8,128)(2,1)}), bf16[32,416,128]{2,1,0:T(8,128)(2,1)}, u32[]{:S(2)}, u32[]{:S(2)}) async-start(bf16[32,416,128]{2,1,0:T(8,128)(2,1)} %get-tuple-element.28), calls=%async_computation.1 | async-start | bytes 6815744 | tf_op jit(solution)/shard_map/cond/branch_1_fun/all_to_all | solution.py:45
  53.7 42.1 %collective-permute-start = (bf16[512,1024]{1,0:T(8,128)(2,1)}, bf16[512,1024]{1,0:T(8,128)(2,1)}, u32[]{:S(2)}, u32[]{:S(2)}) collective-permute-start(bf16[512,1024]{1,0:T(8,128)(2,1)} %get-tuple-element.29), channel_id=1, source_target_pairs={{0,96},{32,0},{64,32},{96,64},{1,97},{33,1},{65,33},{97,65},{2,98}... | collective-permute-start | bytes 3145736 | tf_op jit(solution)/shard_map/cond/branch_1_fun/ppermute | solution.py:41
  56.5 39.3 %collective-permute-start.1 = (bf16[64,2048]{1,0:T(8,128)(2,1)S(1)}, bf16[64,2048]{1,0:T(8,128)(2,1)}, u32[]{:S(2)}, u32[]{:S(2)}) collective-permute-start(bf16[64,2048]{1,0:T(8,128)(2,1)S(1)} %pad_maximum_fusion), channel_id=1, source_target_pairs={{0,1},{1,2},{2,3},{3,4},{4,5},{5,6},{6,7},{7,8},{8,9},{9,10},{10,1... | collective-permute-start | bytes 786440 | tf_op jit(solution)/shard_map/cond/branch_1_fun/ppermute | solution.py:41
  56.7 39.1 %collective-permute-start.2 = (bf16[64,2048]{1,0:T(8,128)(2,1)S(1)}, bf16[64,2048]{1,0:T(8,128)(2,1)}, u32[]{:S(2)}, u32[]{:S(2)}) collective-permute-start(bf16[64,2048]{1,0:T(8,128)(2,1)S(1)} %pad_maximum_fusion.1), channel_id=1, source_target_pairs={{0,31},{1,0},{2,1},{3,2},{4,3},{5,4},{6,5},{7,6},{8,7},{9,8},{10,9... | collective-permute-start | bytes 786440 | tf_op jit(solution)/shard_map/cond/branch_1_fun/ppermute | solution.py:41
  96.9 83.1 %all-to-all-start.2 = ((bf16[32,688,128]{2,1,0:T(8,128)(2,1)}), bf16[32,688,128]{2,1,0:T(8,128)(2,1)}, u32[]{:S(2)}, u32[]{:S(2)}) async-start(bf16[32,688,128]{2,1,0:T(8,128)(2,1)} %get-tuple-element.89), calls=%async_computation.2 | async-start | bytes 11272192 | tf_op jit(solution)/shard_map/all_to_all | solution.py:45
  104.2 26.4 %collective-permute-start.8 = (bf16[512,1024]{1,0:T(8,128)(2,1)}, bf16[512,1024]{1,0:T(8,128)(2,1)}, u32[]{:S(2)}, u32[]{:S(2)}) collective-permute-start(bf16[512,1024]{1,0:T(8,128)(2,1)} %collective-permute-done.7), channel_id=1, source_target_pairs={{0,96},{32,0},{64,32},{96,64},{1,97},{33,1},{65,33},{97,65},{2,98}... | collective-permute-start | bytes 3145736 | tf_op jit(solution)/shard_map/ppermute | solution.py:41
  111.2 35.5 %collective-permute-start.13 = (bf16[512,1024]{1,0:T(8,128)(2,1)}, bf16[512,1024]{1,0:T(8,128)(2,1)}, u32[]{:S(2)}, u32[]{:S(2)}) collective-permute-start(bf16[512,1024]{1,0:T(8,128)(2,1)} %shard_map.57), channel_id=1, source_target_pairs={{0,32},{32,64},{64,96},{96,0},{1,33},{33,65},{65,97},{97,1},{2,34}... | collective-permute-start | bytes 3145736 | tf_op jit(solution)/shard_map/ppermute | solution.py:41
  112.4 54.0 %collective-permute-start.10 = (bf16[512,1024]{1,0:T(8,128)(2,1)}, bf16[512,1024]{1,0:T(8,128)(2,1)}, u32[]{:S(2)}, u32[]{:S(2)}) collective-permute-start(bf16[512,1024]{1,0:T(8,128)(2,1)} %get-tuple-element.86), channel_id=1, source_target_pairs={{0,96},{32,0},{64,32},{96,64},{1,97},{33,1},{65,33},{97,65},{2,98}... | collective-permute-start | bytes 3145736 | tf_op jit(solution)/shard_map/ppermute | solution.py:41
  136.7 27.6 %collective-permute-start.12 = (bf16[512,1024]{1,0:T(8,128)(2,1)}, bf16[512,1024]{1,0:T(8,128)(2,1)}, u32[]{:S(2)}, u32[]{:S(2)}) collective-permute-start(bf16[512,1024]{1,0:T(8,128)(2,1)} %shard_map.58), channel_id=1, source_target_pairs={{0,32},{32,64},{64,96},{96,0},{1,33},{33,65},{65,97},{97,1},{2,34}... | collective-permute-start | bytes 3145736 | tf_op jit(solution)/shard_map/ppermute | solution.py:41
  142.9 31.8 %collective-permute-start.11 = (bf16[512,1024]{1,0:T(8,128)(2,1)}, bf16[512,1024]{1,0:T(8,128)(2,1)}, u32[]{:S(2)}, u32[]{:S(2)}) collective-permute-start(bf16[512,1024]{1,0:T(8,128)(2,1)} %collective-permute-done.8), channel_id=1, source_target_pairs={{0,96},{32,0},{64,32},{96,64},{1,97},{33,1},{65,33},{97,65},{2,98}... | collective-permute-start | bytes 3145736 | tf_op jit(solution)/shard_map/ppermute | solution.py:41
  146.7 52.4 %collective-permute-start.9 = (bf16[512,1024]{1,0:T(8,128)(2,1)}, bf16[512,1024]{1,0:T(8,128)(2,1)}, u32[]{:S(2)}, u32[]{:S(2)}) collective-permute-start(bf16[512,1024]{1,0:T(8,128)(2,1)} %shard_map.59), channel_id=1, source_target_pairs={{0,32},{32,64},{64,96},{96,0},{1,33},{33,65},{65,97},{97,1},{2,34}... | collective-permute-start | bytes 3145736 | tf_op jit(solution)/shard_map/ppermute | solution.py:41

commit v3 on v2

--- a/solution.py
+++ b/solution.py
@@ -374,59 +374,58 @@
     cut = LATE * HEAD
     near_cols = slice(LATE * QW, (HEADS_KV - FAR) * QW)
     always = me >= 0
-    holder = jnp.where(me < DEVS // GLOB, global_blocks[0, :1], global_blocks[0, 1:]) // BLOCKS
-    owners = random_blocks[0].reshape(BLOCKS * RAND) // BLOCKS
-    flags = jnp.stack([me > 0, me < DEVS - 1]).astype(jnp.int32)
 
     first, high, far_a = opening(random_blocks[0].T, global_blocks[0], q, keys, values)
     high = along(high, "segment", 1)
     far_a = along(far_a, "segment", -1)
 
-    def ask(first, q):
-        return exchange(first), q[:, near_cols], q[:, (HEADS_KV - 1) * QW :]
-
-    def no_ask(first, q):
-        near = jnp.zeros((ROWS, near_cols.stop - near_cols.start), BF)
-        return jnp.zeros_like(first), near, jnp.zeros((ROWS, QW), BF)
-
-    message, near_q, far_b = lax.cond(always, ask, no_ask, first, q)
-    message, far_a = lax.optimization_barrier((message, far_a))
-    own_row = jnp.concatenate([owners, jnp.zeros((HEAD - BLOCKS * RAND,), jnp.int32)]).astype(BF)
-    packed, notes = pack_first(
-        holder, keys, values, message, jnp.broadcast_to(own_row[None], (PIECE, HEAD))
+    def edges(*parts):
+        last = jnp.concatenate([x[ROWS - BLOCK :] for x in parts], axis=1)
+        leading = jnp.concatenate([x[:BLOCK] for x in parts], axis=1)
+        return along(last, "seq", 1), along(leading, "seq", -1)
+
+    def ask(first, q, blocks, listed):
+        owners = blocks.reshape(BLOCKS * RAND) // BLOCKS
+        row = jnp.concatenate([owners, jnp.zeros((HEAD - BLOCKS * RAND,), jnp.int32)]).astype(BF)
+        holder = jnp.where(me < DEVS // GLOB, listed[:1], listed[1:]) // BLOCKS
+        flags = jnp.stack([me > 0, me < DEVS - 1]).astype(jnp.int32)
+        return (
+            exchange(first), q[:, near_cols], q[:, (HEADS_KV - 1) * QW :],
+            owners, jnp.broadcast_to(row[None], (PIECE, HEAD)), holder, flags, *edges(keys[:, :cut], values[:, :cut]),
+        )
+
+    def ask_shapes(q):
+        ints = [jnp.zeros((n,), jnp.int32) for n in (BLOCKS * RAND, 1, 2)]
+        return (
+            jnp.zeros(first.shape, BF), q[:, near_cols], q[:, :QW],
+            ints[0], jnp.zeros((PIECE, HEAD), BF), ints[1], ints[2],
+            jnp.zeros((BLOCK, 2 * cut), BF), jnp.zeros((BLOCK, 2 * cut), BF),
+        )
+
+    def no_ask(first, q, blocks, listed):
+        return jax.tree.map(lambda x: jnp.zeros(x.shape, x.dtype), jax.eval_shape(ask_shapes, q))
+
+    message, near_q, far_b, owners, own_tile, holder, flags, before, after = lax.cond(
+        always, ask, no_ask, first, q, random_blocks[0], global_blocks[0]
     )
+    packed, notes = pack_first(holder, keys, values, message, own_tile)
     notes = along(notes, "segment", 1)
+    packed, notes, far_a, high = lax.optimization_barrier((packed, notes, far_a, high))
+    got = exchange(packed)
     near_q = along(tied(near_q, notes), "segment", 1)
-    far_b = along(far_b, "segment", -1)
-    packed, high, notes, far_a = lax.optimization_barrier((packed, high, notes, far_a))
+    far_b = along(tied(far_b, notes), "segment", -1)
+    far_a = along(tied(far_a, notes), "segment", -1)
     asked_at = notes.shape[0] - PIECE - DEVS
     asked_e = notes[asked_at:-PIECE, 0].astype(jnp.int32)
     owners_e = notes[-PIECE, : BLOCKS * RAND].astype(jnp.int32)
 
-    def edge(rows):
-        return jnp.concatenate([keys[rows, :cut], values[rows, :cut], high[rows]], axis=1)
-
-    def middle(packed, far, asked_e, pieces_e):
-        got = exchange(packed)
-        far = along(far, "segment", -1)
-        before = along(edge(slice(ROWS - BLOCK, ROWS)), "seq", 1)
-        after = along(edge(slice(0, BLOCK)), "seq", -1)
-        packed_e = pack(asked_e, [(high, c) for c in range(2 * early_heads)], pieces_e)
-        return got, far, before, after, packed_e
-
-    def no_middle(packed, far, asked_e, pieces_e):
-        side = jnp.zeros((BLOCK, 2 * keys.shape[1]), BF)
-        packed_e = jnp.zeros((DEVS, 2 * early_heads * BLOCK + pieces_e.shape[0], HEAD), BF)
-        return jnp.zeros_like(packed), jnp.zeros_like(far), side, side, packed_e
-
-    got, far_a, before, after, packed = lax.cond(
-        always, middle, no_middle, packed, far_a, asked_e, notes[:asked_at]
-    )
+    before_e, after_e = edges(high)
+    packed = pack(asked_e, [(high, c) for c in range(2 * early_heads)], notes[:asked_at])
     got_e = exchange(packed)
 
     sent = []
     slots = owners
-    far_a = along(far_a, "segment", -1)
+    far_a = along(tied(far_a, got), "segment", -1)
     far_b = along(tied(far_b, got), "segment", -1)
     for h in range(LATE):
         if h == 1:
@@ -439,13 +438,12 @@
     far_b = along(tied(far_b, res), "segment", -1)
 
     out = place(tied(sent[0], res), None, 0, q.shape[1])
-    out = place(tied(sent[1], res), out, 1)
     parts = [(near_q, 0, early_heads - FAR), (far_a, 0, 1), (far_b, 0, 1)]
     out = attention(
-        owners_e, flags, early_heads, LATE, parts, high, 0, high, early_heads, before, after,
-        (2 * LATE, 2 * LATE + early_heads), got_e, LATE, early_heads, width=q.shape[1], out=out,
+        owners_e, flags, early_heads, LATE, parts, high, 0, high, early_heads, before_e, after_e,
+        (0, early_heads), got_e, LATE, early_heads, width=q.shape[1], out=out,
     )
-    for h in range(2, LATE):
+    for h in reversed(range(1, LATE)):
         out = place(sent[h], out, h)
     return out[None]
 

time: 202 us -> 197 us (0.975)
    ppermute x14 -> x16, waiting for transfers between devices: 77.2 us -> 47.3 us  [along(): return lax.ppermute(x, axis, [(i, (i + by) % n) for i in range(n)])]
    all_to_all x3, waiting for transfers between devices: 11.9 us -> 40.2 us  [exchange(): return lax.all_to_all(x, 'seq', split_axis=0, concat_axis=0, tiled=True)]
    ppermute x14 -> x16, starting transfers between devices: 18.3 us -> 18.8 us  [along(): return lax.ppermute(x, axis, [(i, (i + by) % n) for i in range(n)])]
  transfers between devices with their start and end apart: 17 -> 19, of which waited for: 9 -> 10; matrix products, arithmetic and copies ran while one was open for 6% -> 5% of each run, Pallas kernels for 25% -> 25%
where the time goes in v3:
time: 197 us; the launch traced here: 196 us
  waiting for transfers between devices  87.5 us (44%)
  Pallas kernels  55.8 us (28%)
  starting transfers between devices  39.2 us (20%)
  local copies, waits for them, and re-layouts  10.6 us (5%)
    ppermute x16, waiting for transfers between devices, along(): return lax.ppermute(x, axis, [(i, (i + by) % n) for i in range(n)])  47.3 us
    all_to_all x3, waiting for transfers between devices, exchange(): return lax.all_to_all(x, 'seq', split_axis=0, concat_axis=0, tiled=True)  40.2 us
    pallas_call x4, Pallas kernels, attention(): pl.pallas_call(body, grid_spec=pltpu.PrefetchScalarGridSpec(num_scalar_pr...  36.9 us
    all_to_all x3, starting transfers between devices, exchange(): return lax.all_to_all(x, 'seq', split_axis=0, concat_axis=0, tiled=True)  20.4 us
    ppermute x16, starting transfers between devices, along(): return lax.ppermute(x, axis, [(i, (i + by) % n) for i in range(n)])  18.8 us
    pallas_call x3, Pallas kernels, place(): pl.pallas_call(body, grid=(2,), in_specs=in_specs, out_specs=pl.BlockSpec...  6.14 us
    pallas_call x1, Pallas kernels, pack(): pl.pallas_call(body, grid_spec=pltpu.PrefetchScalarGridSpec(num_scalar_pr...  5.2 us
  transfers between devices with their start and end apart: 19, of which 10 were waited for; matrix products, arithmetic and copies ran while one was open for 5% of the time, Pallas kernels for 25%

profile of v3, /device:TPU:8, one launch (start us, length us, event | category | flops | bytes accessed | tf_op | source)
XLA Modules:
  0.0 195.7 jit_solution(3201700832294074187)
XLA Ops:
  0.0 1.3 copy.13
  1.3 3.9 %shard_map.55 = (bf16[32,80,128]{2,1,0:T(8,128)(2,1)}, bf16[512,1280]{1,0:T(8,128)(2,1)}, bf16[512,1024]{1,0:T(8,128)(2,1)}) custom-call(s32[3,8]{1,0:T(4,128)} %bitcast.33, s32[2]{0:T(128)} %bitcast.34, bf16[512,8192]{1,0:T(8,128)(2,1)} %bitcast.16, bf16[512,1024]{1,0:T(8,128)(2,1)} %bitcast.21, bf16[512,1024]{1,0:T(8,128)(2,1)} %bitcast.27), custom_call_target="tpu_custom_call" | custom-call | tf_op jit(solution)/shard_map/pallas_call | solution.py:104
  5.2 2.3 %collective-permute-start.4 = (bf16[512,1280]{1,0:T(8,128)(2,1)}, bf16[512,1280]{1,0:T(8,128)(2,1)}, u32[]{:S(2)}, u32[]{:S(2)}) collective-permute-start(bf16[512,1280]{1,0:T(8,128)(2,1)} %get-tuple-element.67), channel_id=1, source_target_pairs={{0,32},{32,64},{64,96},{96,0},{1,33},{33,65},{65,97},{97,1},{2,34}... | collective-permute-start | bytes 3932168 | tf_op jit(solution)/shard_map/ppermute | solution.py:41
  7.5 2.2 %collective-permute-start.3 = (bf16[512,1024]{1,0:T(8,128)(2,1)}, bf16[512,1024]{1,0:T(8,128)(2,1)}, u32[]{:S(2)}, u32[]{:S(2)}) collective-permute-start(bf16[512,1024]{1,0:T(8,128)(2,1)} %get-tuple-element.66), channel_id=1, source_target_pairs={{0,96},{32,0},{64,32},{96,64},{1,97},{33,1},{65,33},{97,65},{2,98}... | collective-permute-start | bytes 3145736 | tf_op jit(solution)/shard_map/ppermute | solution.py:41
  9.7 0.0 copy-done
  9.7 0.0 copy-done.1
  9.7 18.8 %conditional.1 = (bf16[32,80,128]{2,1,0:T(8,128)(2,1)}, bf16[512,3072]{1,0:T(8,128)(2,1)}, bf16[512,1024]{1,0:T(8,128)(2,1)}, s32[24]{0:T(128)S(1)}, bf16[16,128...) conditional(s32[]{:T(128)} %convert_element_type.17, () %tuple.24, ...), branch_computations={%region_0.0_spmd, %region_1.2_spmd} | conditional | flops 393623 | bytes 11933234 | solution.py:408
  9.7 7.3 %all-to-all-start = ((bf16[32,80,128]{2,1,0:T(8,128)(2,1)}), bf16[32,80,128]{2,1,0:T(8,128)(2,1)}, u32[]{:S(2)}, u32[]{:S(2)}) async-start(bf16[32,80,128]{2,1,0:T(8,128)(2,1)} %get-tuple-element.19), calls=%async_computation | async-start | bytes 1310720 | tf_op jit(solution)/shard_map/cond/branch_1_fun/all_to_all | solution.py:45
  17.0 0.9 fusion.1
  17.9 0.2 collective-permute-start
  18.1 1.7 collective-permute-start.1
  19.8 0.6 fusion.3
  21.6 2.3 %slice.33 = bf16[512,1024]{1,0:T(8,128)(2,1)} slice(bf16[512,8192]{1,0:T(8,128)(2,1)} %get-tuple-element.20), slice={[0:512], [7168:8192]} | slice | bytes 2097152 | tf_op jit(solution)/shard_map/cond/branch_1_fun/slice | solution.py:393
  24.0 3.7 %slice.32 = bf16[512,3072]{1,0:T(8,128)(2,1)} slice(bf16[512,8192]{1,0:T(8,128)(2,1)} %get-tuple-element.20), slice={[0:512], [3072:6144]} | slice | bytes 6291456 | tf_op jit(solution)/shard_map/cond/branch_1_fun/slice | solution.py:393
  27.7 0.1 copy.10
  27.8 0.1 reshape_squeeze.2
  27.9 0.1 add_convert_fusion
  27.9 0.0 collective-permute-done
  27.9 0.0 collective-permute-done.1
  27.9 0.5 all-to-all-done
  28.5 3.6 %shard_map.56 = (bf16[32,416,128]{2,1,0:T(8,128)(2,1)}, bf16[96,128]{1,0:T(8,128)(2,1)}) custom-call(s32[1]{0:T(128)} %get-tuple-element.61.held, bf16[512,1024]{1,0:T(8,128)(2,1)} %bitcast.23, bf16[512,1024]{1,0:T(8,128)(2,1)} %bitcast.29, bf16[32,80,128]{2,1,0:T(8,128)(2,1)} %get-tuple-element.62.ask_ref.p_ref, ...), custom_call_target="tpu_custom_call" | custom-call | tf_op jit(solution)/shard_map/pallas_call | solution.py:187
  32.1 0.0 collective-permute-start.2
  32.1 7.0 %collective-permute-done.2 = bf16[96,128]{1,0:T(8,128)(2,1)S(1)} collective-permute-done((bf16[96,128]{1,0:T(8,128)(2,1)}, bf16[96,128]{1,0:T(8,128)(2,1)S(1)}, u32[]{:S(2)}, u32[]{:S(2)}) %collective-permute-start.2) | collective-permute-done | bytes 24608 | tf_op jit(solution)/shard_map/ppermute | solution.py:41
  39.1 0.0 collective-permute-done.3
  39.1 0.0 collective-permute-done.4.refs_0_.refs_3_.refs_4_
  39.1 7.3 %all-to-all-start.1 = ((bf16[32,416,128]{2,1,0:T(8,128)(2,1)}), bf16[32,416,128]{2,1,0:T(8,128)(2,1)}, u32[]{:S(2)}, u32[]{:S(2)}) async-start(bf16[32,416,128]{2,1,0:T(8,128)(2,1)} %get-tuple-element.68), calls=%async_computation.1 | async-start | bytes 6815744 | tf_op jit(solution)/shard_map/all_to_all | solution.py:45
  46.4 0.1 collective-permute-start.5
  46.5 3.2 %collective-permute-start.6 = (bf16[512,1024]{1,0:T(8,128)(2,1)}, bf16[512,1024]{1,0:T(8,128)(2,1)}, u32[]{:S(2)}, u32[]{:S(2)}) collective-permute-start(bf16[512,1024]{1,0:T(8,128)(2,1)} %get-tuple-element.74), channel_id=1, source_target_pairs={{0,96},{32,0},{64,32},{96,64},{1,97},{33,1},{65,33},{97,65},{2,98}... | collective-permute-start | bytes 3145736 | tf_op jit(solution)/shard_map/ppermute | solution.py:41
  49.7 0.6 slice.49.refs_1_
  50.3 0.5 collective-permute-start.10
  50.8 0.6 convert_reduce_fusion.ask
  51.5 5.2 %shard_map.60 = bf16[32,688,128]{2,1,0:T(8,128)(2,1)} custom-call(s32[32]{0:T(128)} %convert_reduce_fusion.ask, bf16[512,1280]{1,0:T(8,128)(2,1)} %collective-permute-done.4.refs_0_.refs_3_.refs_4_, bf16[48,128]{1,0:T(8,128)(2,1)} %slice.49.refs_1_), custom_call_target="tpu_custom_call" | custom-call | tf_op jit(solution)/shard_map/pallas_call | solution.py:147
  56.7 33.0 %all-to-all-done.1.refs_7_.refs_8_.refs_9_ = bf16[32,416,128]{2,1,0:T(8,128)(2,1)} async-done(((bf16[32,416,128]{2,1,0:T(8,128)(2,1)}), bf16[32,416,128]{2,1,0:T(8,128)(2,1)}, u32[]{:S(2)}, u32[]{:S(2)}) %all-to-all-start.1) | async-done | bytes 3407904 | tf_op jit(solution)/shard_map/all_to_all | solution.py:45
  89.6 5.8 %all-to-all-start.2 = ((bf16[32,688,128]{2,1,0:T(8,128)(2,1)}), bf16[32,688,128]{2,1,0:T(8,128)(2,1)}, u32[]{:S(2)}, u32[]{:S(2)}) async-start(bf16[32,688,128]{2,1,0:T(8,128)(2,1)} %shard_map.60), calls=%async_computation.2 | async-start | bytes 11272192 | tf_op jit(solution)/shard_map/all_to_all | solution.py:45
  95.5 0.0 collective-permute-done.6
  95.5 1.8 collective-permute-start.7
  97.3 6.0 %shard_map.57 = bf16[512,1024]{1,0:T(8,128)(2,1)} custom-call(s32[24]{0:T(128)S(1)} %get-tuple-element.77.slot, s32[2]{0:T(128)S(1)} %get-tuple-element.58.flag, bf16[512,8192]{1,0:T(8,128)(2,1)} %bitcast.18, bf16[512,1024]{1,0:T(8,128)(2,1)} %bitcast.24, bf16[512,1024]{1,0:T(8,128)(2,1)} %bitcast.30, bf16[64,768]{1,0:T(8,128)(2,1)} %get-tuple-element.59.refs_3_.refs_4_, ...), custom_call_target="tpu_custom_call" | custom-call | flops 21474836480 | bytes 41943040 | tf_op jit(solution)/shard_map/pallas_call | solution.py:326
  103.3 0.3 collective-permute-start.15
  103.6 0.0 collective-permute-done.10
  103.6 3.0 %collective-permute-start.11 = (bf16[512,1024]{1,0:T(8,128)(2,1)}, bf16[512,1024]{1,0:T(8,128)(2,1)}, u32[]{:S(2)}, u32[]{:S(2)}) collective-permute-start(bf16[512,1024]{1,0:T(8,128)(2,1)} %collective-permute-done.10), channel_id=1, source_target_pairs={{0,96},{32,0},{64,32},{96,64},{1,97},{33,1},{65,33},{97,65},{2,98}... | collective-permute-start | bytes 3145736 | tf_op jit(solution)/shard_map/ppermute | solution.py:41
  106.6 12.4 %collective-permute-done.5.refs_0_ = bf16[512,3072]{1,0:T(8,128)(2,1)} collective-permute-done((bf16[512,3072]{1,0:T(8,128)(2,1)}, bf16[512,3072]{1,0:T(8,128)(2,1)}, u32[]{:S(2)}, u32[]{:S(2)}) %collective-permute-start.5) | collective-permute-done | bytes 3145760 | tf_op jit(solution)/shard_map/ppermute | solution.py:41
  119.0 2.9 %collective-permute-done.7 = bf16[512,1024]{1,0:T(8,128)(2,1)} collective-permute-done((bf16[512,1024]{1,0:T(8,128)(2,1)}, bf16[512,1024]{1,0:T(8,128)(2,1)}, u32[]{:S(2)}, u32[]{:S(2)}) %collective-permute-start.7) | collective-permute-done | bytes 1048608 | tf_op jit(solution)/shard_map/ppermute | solution.py:41
  121.9 6.0 %shard_map.58 = bf16[512,1024]{1,0:T(8,128)(2,1)} custom-call(s32[24]{0:T(128)S(1)} %get-tuple-element.77.slot, s32[2]{0:T(128)S(1)} %get-tuple-element.58.flag, bf16[512,8192]{1,0:T(8,128)(2,1)} %bitcast.19, bf16[512,1024]{1,0:T(8,128)(2,1)} %bitcast.25, bf16[512,1024]{1,0:T(8,128)(2,1)} %bitcast.31, bf16[64,768]{1,0:T(8,128)(2,1)} %get-tuple-element.59.refs_3_.refs_4_, ...), custom_call_target="tpu_custom_call" | custom-call | flops 21474836480 | bytes 41943040 | tf_op jit(solution)/shard_map/pallas_call | solution.py:326
  127.9 6.0 %shard_map.59 = bf16[512,1024]{1,0:T(8,128)(2,1)} custom-call(s32[24]{0:T(128)S(1)} %get-tuple-element.77.slot, s32[2]{0:T(128)S(1)} %get-tuple-element.58.flag, bf16[512,8192]{1,0:T(8,128)(2,1)} %bitcast.20, bf16[512,1024]{1,0:T(8,128)(2,1)} %bitcast.26, bf16[512,1024]{1,0:T(8,128)(2,1)} %bitcast.32, bf16[64,768]{1,0:T(8,128)(2,1)} %get-tuple-element.59.refs_3_.refs_4_, ...), custom_call_target="tpu_custom_call" | custom-call | flops 21474836480 | bytes 41943040 | tf_op jit(solution)/shard_map/pallas_call | solution.py:326
  133.9 2.9 %collective-permute-start.12 = (bf16[512,1024]{1,0:T(8,128)(2,1)}, bf16[512,1024]{1,0:T(8,128)(2,1)}, u32[]{:S(2)}, u32[]{:S(2)}) collective-permute-start(bf16[512,1024]{1,0:T(8,128)(2,1)} %collective-permute-done.7), channel_id=1, source_target_pairs={{0,96},{32,0},{64,32},{96,64},{1,97},{33,1},{65,33},{97,65},{2,98}... | collective-permute-start | bytes 3145736 | tf_op jit(solution)/shard_map/ppermute | solution.py:41
  136.9 1.0 fusion.4
  137.9 0.1 collective-permute-start.14
  138.0 0.5 collective-permute-start.13
  138.5 0.5 bitcast_convert_fusion.slot
  139.0 1.6 collective-permute-done.15.p_ref
  140.6 0.0 collective-permute-start.9
  140.6 2.0 %shard_map.61.refs_12_ = bf16[512,8192]{1,0:T(8,128)(2,1)} custom-call(bf16[512,1024]{1,0:T(8,128)(2,1)} %collective-permute-done.15.p_ref), custom_call_target="tpu_custom_call" | custom-call | tf_op jit(solution)/shard_map/pallas_call | solution.py:354
  142.7 16.3 %collective-permute-done.14.refs_7_.refs_8_ = bf16[64,1280]{1,0:T(8,128)(2,1)S(1)} collective-permute-done((bf16[64,1280]{1,0:T(8,128)(2,1)S(1)}, bf16[64,1280]{1,0:T(8,128)(2,1)S(1)}, u32[]{:S(2)}, u32[]{:S(2)}) %collective-permute-start.14) | collective-permute-done | bytes 163872 | tf_op jit(solution)/shard_map/ppermute | solution.py:41
  159.0 0.0 collective-permute-start.8
  159.0 3.5 %collective-permute-done.13.refs_5_.refs_6_ = bf16[64,1280]{1,0:T(8,128)(2,1)S(1)} collective-permute-done((bf16[64,1280]{1,0:T(8,128)(2,1)S(1)}, bf16[64,1280]{1,0:T(8,128)(2,1)S(1)}, u32[]{:S(2)}, u32[]{:S(2)}) %collective-permute-start.13) | collective-permute-done | bytes 163872 | tf_op jit(solution)/shard_map/ppermute | solution.py:41
  162.5 0.0 collective-permute-done.11.refs_1_
  162.5 3.6 %collective-permute-done.12.refs_2_ = bf16[512,1024]{1,0:T(8,128)(2,1)} collective-permute-done((bf16[512,1024]{1,0:T(8,128)(2,1)}, bf16[512,1024]{1,0:T(8,128)(2,1)}, u32[]{:S(2)}, u32[]{:S(2)}) %collective-permute-start.12) | collective-permute-done | bytes 1048608 | tf_op jit(solution)/shard_map/ppermute | solution.py:41
  166.0 6.7 %all-to-all-done.2.refs_9_.refs_10_.refs_11_ = bf16[32,688,128]{2,1,0:T(8,128)(2,1)} async-done(((bf16[32,688,128]{2,1,0:T(8,128)(2,1)}), bf16[32,688,128]{2,1,0:T(8,128)(2,1)}, u32[]{:S(2)}, u32[]{:S(2)}) %all-to-all-start.2) | async-done | bytes 5636128 | tf_op jit(solution)/shard_map/all_to_all | solution.py:45
  172.7 0.0 copy-done.2
  172.7 18.9 %shard_map.62.refs_0_ = bf16[512,8192]{1,0:T(8,128)(2,1)} custom-call(s32[24]{0:T(128)} %bitcast_convert_fusion.slot, s32[2]{0:T(128)S(1)} %get-tuple-element.58.flag, bf16[512,3072]{1,0:T(8,128)(2,1)} %collective-permute-done.5.refs_0_, bf16[512,1024]{1,0:T(8,128)(2,1)} %collective-permute-done.11.refs_1_, ...), custom_call_target="tpu_custom_call", output_to_operand_aliasing={{}: (14, {})} | custom-call | flops 107374182400 | bytes 209715200 | tf_op jit(solution)/shard_map/pallas_call | solution.py:326
  191.6 0.0 collective-permute-done.9.p_ref
  191.6 2.1 %shard_map.63.refs_0_ = bf16[512,8192]{1,0:T(8,128)(2,1)} custom-call(bf16[512,1024]{1,0:T(8,128)(2,1)} %collective-permute-done.9.p_ref, bf16[512,8192]{1,0:T(8,128)(2,1)} %shard_map.62.refs_0_), custom_call_target="tpu_custom_call", output_to_operand_aliasing={{}: (1, {})} | custom-call | tf_op jit(solution)/shard_map/pallas_call | solution.py:354
  193.7 0.0 collective-permute-done.8.p_ref
  193.7 2.0 %shard_map.64 = bf16[512,8192]{1,0:T(8,128)(2,1)} custom-call(bf16[512,1024]{1,0:T(8,128)(2,1)} %collective-permute-done.8.p_ref, bf16[512,8192]{1,0:T(8,128)(2,1)} %shard_map.63.refs_0_), custom_call_target="tpu_custom_call", output_to_operand_aliasing={{}: (1, {})} | custom-call | tf_op jit(solution)/shard_map/pallas_call | solution.py:354
  (10 shorter events, 0.1 us)
Async XLA Ops:
  1.3 8.4 %copy-start = (s32[1,8,3]{1,0,2:T(1,128)S(1)}, s32[1,8,3]{1,0,2:T(1,128)}, u32[]{:S(2)}) copy-start(s32[1,8,3]{1,0,2:T(1,128)} %param.10) | copy-start | bytes 292
  1.3 8.4 %copy-start.1 = (s32[1,2]{1,0:T(1,128)S(1)}, s32[1,2]{1,0:T(1,128)}, u32[]{:S(2)}) copy-start(s32[1,2]{1,0:T(1,128)} %param.11) | copy-start | bytes 28
  5.2 33.9 %collective-permute-start.4 = (bf16[512,1280]{1,0:T(8,128)(2,1)}, bf16[512,1280]{1,0:T(8,128)(2,1)}, u32[]{:S(2)}, u32[]{:S(2)}) collective-permute-start(bf16[512,1280]{1,0:T(8,128)(2,1)} %get-tuple-element.67), channel_id=1, source_target_pairs={{0,32},{32,64},{64,96},{96,0},{1,33},{33,65},{65,97},{97,1},{2,34}... | collective-permute-start | bytes 3932168 | tf_op jit(solution)/shard_map/ppermute | solution.py:41
  7.5 31.6 %collective-permute-start.3 = (bf16[512,1024]{1,0:T(8,128)(2,1)}, bf16[512,1024]{1,0:T(8,128)(2,1)}, u32[]{:S(2)}, u32[]{:S(2)}) collective-permute-start(bf16[512,1024]{1,0:T(8,128)(2,1)} %get-tuple-element.66), channel_id=1, source_target_pairs={{0,96},{32,0},{64,32},{96,64},{1,97},{33,1},{65,33},{97,65},{2,98}... | collective-permute-start | bytes 3145736 | tf_op jit(solution)/shard_map/ppermute | solution.py:41
  9.7 18.8 %all-to-all-start = ((bf16[32,80,128]{2,1,0:T(8,128)(2,1)}), bf16[32,80,128]{2,1,0:T(8,128)(2,1)}, u32[]{:S(2)}, u32[]{:S(2)}) async-start(bf16[32,80,128]{2,1,0:T(8,128)(2,1)} %get-tuple-element.19), calls=%async_computation | async-start | bytes 1310720 | tf_op jit(solution)/shard_map/cond/branch_1_fun/all_to_all | solution.py:45
  17.9 10.0 %collective-permute-start = (bf16[64,768]{1,0:T(8,128)(2,1)S(1)}, bf16[64,768]{1,0:T(8,128)(2,1)}, u32[]{:S(2)}, u32[]{:S(2)}) collective-permute-start(bf16[64,768]{1,0:T(8,128)(2,1)S(1)} %pad_maximum_fusion), channel_id=1, source_target_pairs={{0,1},{1,2},{2,3},{3,4},{4,5},{5,6},{6,7},{7,8},{8,9},{9,10},{10,1... | collective-permute-start | bytes 294920 | tf_op jit(solution)/shard_map/cond/branch_1_fun/ppermute | solution.py:41
  18.1 9.8 %collective-permute-start.1 = (bf16[64,768]{1,0:T(8,128)(2,1)S(1)}, bf16[64,768]{1,0:T(8,128)(2,1)}, u32[]{:S(2)}, u32[]{:S(2)}) collective-permute-start(bf16[64,768]{1,0:T(8,128)(2,1)S(1)} %pad_maximum_fusion.1), channel_id=1, source_target_pairs={{0,31},{1,0},{2,1},{3,2},{4,3},{5,4},{6,5},{7,6},{8,7},{9,8},{10,9... | collective-permute-start | bytes 294920 | tf_op jit(solution)/shard_map/cond/branch_1_fun/ppermute | solution.py:41
  32.1 7.0 %collective-permute-start.2 = (bf16[96,128]{1,0:T(8,128)(2,1)}, bf16[96,128]{1,0:T(8,128)(2,1)S(1)}, u32[]{:S(2)}, u32[]{:S(2)}) collective-permute-start(bf16[96,128]{1,0:T(8,128)(2,1)} %get-tuple-element.65), channel_id=1, source_target_pairs={{0,32},{32,64},{64,96},{96,0},{1,33},{33,65},{65,97},{97,1},{2,34}... | collective-permute-start | bytes 73736 | tf_op jit(solution)/shard_map/ppermute | solution.py:41
  39.1 50.5 %all-to-all-start.1 = ((bf16[32,416,128]{2,1,0:T(8,128)(2,1)}), bf16[32,416,128]{2,1,0:T(8,128)(2,1)}, u32[]{:S(2)}, u32[]{:S(2)}) async-start(bf16[32,416,128]{2,1,0:T(8,128)(2,1)} %get-tuple-element.68), calls=%async_computation.1 | async-start | bytes 6815744 | tf_op jit(solution)/shard_map/all_to_all | solution.py:45
  46.4 72.5 %collective-permute-start.5 = (bf16[512,3072]{1,0:T(8,128)(2,1)}, bf16[512,3072]{1,0:T(8,128)(2,1)}, u32[]{:S(2)}, u32[]{:S(2)}) collective-permute-start(bf16[512,3072]{1,0:T(8,128)(2,1)} %get-tuple-element.72), channel_id=1, source_target_pairs={{0,32},{32,64},{64,96},{96,0},{1,33},{33,65},{65,97},{97,1},{2,34}... | collective-permute-start | bytes 9437192 | tf_op jit(solution)/shard_map/ppermute | solution.py:41
  46.5 49.0 %collective-permute-start.6 = (bf16[512,1024]{1,0:T(8,128)(2,1)}, bf16[512,1024]{1,0:T(8,128)(2,1)}, u32[]{:S(2)}, u32[]{:S(2)}) collective-permute-start(bf16[512,1024]{1,0:T(8,128)(2,1)} %get-tuple-element.74), channel_id=1, source_target_pairs={{0,96},{32,0},{64,32},{96,64},{1,97},{33,1},{65,33},{97,65},{2,98}... | collective-permute-start | bytes 3145736 | tf_op jit(solution)/shard_map/ppermute | solution.py:41
  50.3 53.3 %collective-permute-start.10 = (bf16[512,1024]{1,0:T(8,128)(2,1)}, bf16[512,1024]{1,0:T(8,128)(2,1)}, u32[]{:S(2)}, u32[]{:S(2)}) collective-permute-start(bf16[512,1024]{1,0:T(8,128)(2,1)} %collective-permute-done.3), channel_id=1, source_target_pairs={{0,96},{32,0},{64,32},{96,64},{1,97},{33,1},{65,33},{97,65},{2,98}... | collective-permute-start | bytes 3145736 | tf_op jit(solution)/shard_map/ppermute | solution.py:41
  89.6 83.1 %all-to-all-start.2 = ((bf16[32,688,128]{2,1,0:T(8,128)(2,1)}), bf16[32,688,128]{2,1,0:T(8,128)(2,1)}, u32[]{:S(2)}, u32[]{:S(2)}) async-start(bf16[32,688,128]{2,1,0:T(8,128)(2,1)} %shard_map.60), calls=%async_computation.2 | async-start | bytes 11272192 | tf_op jit(solution)/shard_map/all_to_all | solution.py:45
  95.5 26.4 %collective-permute-start.7 = (bf16[512,1024]{1,0:T(8,128)(2,1)}, bf16[512,1024]{1,0:T(8,128)(2,1)}, u32[]{:S(2)}, u32[]{:S(2)}) collective-permute-start(bf16[512,1024]{1,0:T(8,128)(2,1)} %collective-permute-done.6), channel_id=1, source_target_pairs={{0,96},{32,0},{64,32},{96,64},{1,97},{33,1},{65,33},{97,65},{2,98}... | collective-permute-start | bytes 3145736 | tf_op jit(solution)/shard_map/ppermute | solution.py:41
  103.3 37.3 %collective-permute-start.15 = (bf16[512,1024]{1,0:T(8,128)(2,1)}, bf16[512,1024]{1,0:T(8,128)(2,1)}, u32[]{:S(2)}, u32[]{:S(2)}) collective-permute-start(bf16[512,1024]{1,0:T(8,128)(2,1)} %shard_map.57), channel_id=1, source_target_pairs={{0,32},{32,64},{64,96},{96,0},{1,33},{33,65},{65,97},{97,1},{2,34}... | collective-permute-start | bytes 3145736 | tf_op jit(solution)/shard_map/ppermute | solution.py:41
  103.6 58.9 %collective-permute-start.11 = (bf16[512,1024]{1,0:T(8,128)(2,1)}, bf16[512,1024]{1,0:T(8,128)(2,1)}, u32[]{:S(2)}, u32[]{:S(2)}) collective-permute-start(bf16[512,1024]{1,0:T(8,128)(2,1)} %collective-permute-done.10), channel_id=1, source_target_pairs={{0,96},{32,0},{64,32},{96,64},{1,97},{33,1},{65,33},{97,65},{2,98}... | collective-permute-start | bytes 3145736 | tf_op jit(solution)/shard_map/ppermute | solution.py:41
  133.9 32.1 %collective-permute-start.12 = (bf16[512,1024]{1,0:T(8,128)(2,1)}, bf16[512,1024]{1,0:T(8,128)(2,1)}, u32[]{:S(2)}, u32[]{:S(2)}) collective-permute-start(bf16[512,1024]{1,0:T(8,128)(2,1)} %collective-permute-done.7), channel_id=1, source_target_pairs={{0,96},{32,0},{64,32},{96,64},{1,97},{33,1},{65,33},{97,65},{2,98}... | collective-permute-start | bytes 3145736 | tf_op jit(solution)/shard_map/ppermute | solution.py:41
  137.9 21.1 %collective-permute-start.14 = (bf16[64,1280]{1,0:T(8,128)(2,1)S(1)}, bf16[64,1280]{1,0:T(8,128)(2,1)S(1)}, u32[]{:S(2)}, u32[]{:S(2)}) collective-permute-start(bf16[64,1280]{1,0:T(8,128)(2,1)S(1)} %get-tuple-element.110), channel_id=1, source_target_pairs={{0,31},{1,0},{2,1},{3,2},{4,3},{5,4},{6,5},{7,6},{8,7},{9,8},{10,9... | collective-permute-start | bytes 491528 | tf_op jit(solution)/shard_map/ppermute | solution.py:41
  138.0 24.5 %collective-permute-start.13 = (bf16[64,1280]{1,0:T(8,128)(2,1)S(1)}, bf16[64,1280]{1,0:T(8,128)(2,1)S(1)}, u32[]{:S(2)}, u32[]{:S(2)}) collective-permute-start(bf16[64,1280]{1,0:T(8,128)(2,1)S(1)} %get-tuple-element.111), channel_id=1, source_target_pairs={{0,1},{1,2},{2,3},{3,4},{4,5},{5,6},{6,7},{7,8},{8,9},{9,10},{10,1... | collective-permute-start | bytes 491528 | tf_op jit(solution)/shard_map/ppermute | solution.py:41
  140.6 51.0 %collective-permute-start.9 = (bf16[512,1024]{1,0:T(8,128)(2,1)}, bf16[512,1024]{1,0:T(8,128)(2,1)}, u32[]{:S(2)}, u32[]{:S(2)}) collective-permute-start(bf16[512,1024]{1,0:T(8,128)(2,1)} %shard_map.59), channel_id=1, source_target_pairs={{0,32},{32,64},{64,96},{96,0},{1,33},{33,65},{65,97},{97,1},{2,34}... | collective-permute-start | bytes 3145736 | tf_op jit(solution)/shard_map/ppermute | solution.py:41
  159.0 13.8 %copy-start.2 = (bf16[64,1280]{1,0:T(8,128)(2,1)}, bf16[64,1280]{1,0:T(8,128)(2,1)S(1)}, u32[]{:S(2)}) copy-start(bf16[64,1280]{1,0:T(8,128)(2,1)S(1)} %collective-permute-done.14.refs_7_.refs_8_) | copy-start | bytes 491524
  159.0 34.7 %collective-permute-start.8 = (bf16[512,1024]{1,0:T(8,128)(2,1)}, bf16[512,1024]{1,0:T(8,128)(2,1)}, u32[]{:S(2)}, u32[]{:S(2)}) collective-permute-start(bf16[512,1024]{1,0:T(8,128)(2,1)} %shard_map.58), channel_id=1, source_target_pairs={{0,32},{32,64},{64,96},{96,0},{1,33},{33,65},{65,97},{97,1},{2,34}... | collective-permute-start | bytes 3145736 | tf_op jit(solution)/shard_map/ppermute | solution.py:41
  162.5 10.3 %copy-start.3 = (bf16[64,1280]{1,0:T(8,128)(2,1)}, bf16[64,1280]{1,0:T(8,128)(2,1)S(1)}, u32[]{:S(2)}) copy-start(bf16[64,1280]{1,0:T(8,128)(2,1)S(1)} %collective-permute-done.13.refs_5_.refs_6_) | copy-start | bytes 491524

commit v4 on v3

--- a/solution.py
+++ b/solution.py
@@ -63,30 +63,41 @@
             rows = pl.ds(pl.multiple_of(at, BLOCK), BLOCK)
             for n, src in enumerate((k_ref, v_ref)):
                 globs.append(pltpu.make_async_copy(src.at[rows], glob.at[n, g], glob_sems.at[2 * n + g]))
-        loads = [
-            pltpu.make_async_copy(k_ref.at[:, pl.ds(cut, rest)], high.at[:, pl.ds(0, rest)], sems.at[0]),
-            pltpu.make_async_copy(v_ref.at[:, pl.ds(cut, rest)], high.at[:, pl.ds(rest, rest)], sems.at[1]),
-            pltpu.make_async_copy(q_ref.at[:, pl.ds((HEADS_KV - FAR) * QW, QW)], far, sems.at[2]),
-        ]
-        stores = [
-            pltpu.make_async_copy(high, high_hbm, sems.at[3]),
-            pltpu.make_async_copy(far, far_hbm, sems.at[4]),
-            pltpu.make_async_copy(out, out_hbm, sems.at[5]),
-        ]
-        for c in loads + globs:
+        half = [pl.ds(i * ROWS // 2, ROWS // 2) for i in range(2)]
+        high_loads, far_loads, high_stores, far_stores = [], [], [], []
+        for i, rows in enumerate(half):
+            high_loads += [
+                pltpu.make_async_copy(
+                    k_ref.at[rows, pl.ds(cut, rest)], high.at[rows, pl.ds(0, rest)], sems.at[i]
+                ),
+                pltpu.make_async_copy(
+                    v_ref.at[rows, pl.ds(cut, rest)], high.at[rows, pl.ds(rest, rest)], sems.at[2 + i]
+                ),
+            ]
+            far_loads.append(
+                pltpu.make_async_copy(
+                    q_ref.at[rows, pl.ds((HEADS_KV - FAR) * QW, QW)], far.at[rows], sems.at[4 + i]
+                )
+            )
+            high_stores.append(pltpu.make_async_copy(high.at[rows], high_hbm.at[rows], sems.at[6 + i]))
+            far_stores.append(pltpu.make_async_copy(far.at[rows], far_hbm.at[rows], sems.at[8 + i]))
+        last_store = pltpu.make_async_copy(out, out_hbm, sems.at[10])
+        for c in high_loads + far_loads + globs:
             c.start()
         out[:, PAIRS * PIECE :] = jnp.zeros((DEVS, PIECE, HEAD), BF)
         for r in range(RAND):
             for j in range(BLOCKS):
-                wanted = rb[r, j]
+                wanted = rb[r, 0, j]
                 out[lax.shift_right_logical(wanted, 3), PAIRS * PIECE :] = jnp.full(
                     (PIECE, HEAD), wanted & (BLOCKS - 1), jnp.int32
                 ).astype(jnp.float32).astype(BF)
-        loads[0].wait()
-        loads[1].wait()
-        stores[0].start()
-        loads[2].wait()
-        stores[1].start()
+        for i in range(2):
+            high_loads[2 * i].wait()
+            high_loads[2 * i + 1].wait()
+            high_stores[i].start()
+        for i in range(2):
+            far_loads[i].wait()
+            far_stores[i].start()
         for c in globs:
             c.wait()
         for i in range(DEVS):
@@ -96,8 +107,8 @@
                 out[i, c * PIECE : (c + 1) * PIECE] = glob[
                     t // 2, g, part * PIECE : (part + 1) * PIECE, head * HEAD : (head + 1) * HEAD
                 ]
-        stores[2].start()
-        for c in stores:
+        last_store.start()
+        for c in high_stores + far_stores + [last_store]:
             c.wait()
 
     here = pl.BlockSpec(memory_space=pltpu.HBM)
@@ -111,7 +122,7 @@
             scratch_shapes=[pltpu.VMEM(x, BF) for x in shapes]
             + [
                 pltpu.VMEM((2, GLOB, BLOCK, keys.shape[1]), BF),
-                pltpu.SemaphoreType.DMA((6,)),
+                pltpu.SemaphoreType.DMA((11,)),
                 pltpu.SemaphoreType.DMA((2 * GLOB,)),
             ],
         ),
@@ -340,23 +351,41 @@
 
 
 def place(part, out, at, width=None):
-    step = ROWS // 2
+    cuts = 8
+    step = ROWS // cuts
 
     def body(p_ref, *refs):
-        refs[-1][...] = p_ref[...]
-
-    in_specs = [pl.BlockSpec((step, part.shape[1]), lambda i: (i, 0))]
+        o_ref, stage, load_sems, store_sems = refs[-4:]
+        loads, stores = [], []
+        for i in range(cuts):
+            rows = pl.ds(i * step, step)
+            loads.append(pltpu.make_async_copy(p_ref.at[rows], stage.at[rows], load_sems.at[i]))
+            stores.append(
+                pltpu.make_async_copy(stage.at[rows], o_ref.at[rows, pl.ds(at * QW, QW)], store_sems.at[i])
+            )
+        for c in loads:
+            c.start()
+        for x, y in zip(loads, stores):
+            x.wait()
+            y.start()
+        for c in stores:
+            c.wait()
+
+    here = pl.BlockSpec(memory_space=pltpu.HBM)
     operands = [part]
     if out is not None:
-        in_specs.append(pl.BlockSpec(memory_space=pl.ANY))
         operands.append(out)
         width = out.shape[1]
     return pl.pallas_call(
         body,
-        grid=(2,),
-        in_specs=in_specs,
-        out_specs=pl.BlockSpec((step, part.shape[1]), lambda i: (i, at)),
+        in_specs=[here] * len(operands),
+        out_specs=here,
         out_shape=jax.ShapeDtypeStruct((ROWS, width), BF),
+        scratch_shapes=[
+            pltpu.VMEM((ROWS, QW), BF),
+            pltpu.SemaphoreType.DMA((cuts,)),
+            pltpu.SemaphoreType.DMA((cuts,)),
+        ],
         input_output_aliases={} if out is None else {1: 0},
         compiler_params=params(),
         cost_estimate=CHEAP,
@@ -375,7 +404,7 @@
     near_cols = slice(LATE * QW, (HEADS_KV - FAR) * QW)
     always = me >= 0
 
-    first, high, far_a = opening(random_blocks[0].T, global_blocks[0], q, keys, values)
+    first, high, far_a = opening(random_blocks.transpose(2, 0, 1), global_blocks[0], q, keys, values)
     high = along(high, "segment", 1)
     far_a = along(far_a, "segment", -1)
 
@@ -430,21 +459,23 @@
     for h in range(LATE):
         if h == 1:
             slots, near_q, far_b = lax.optimization_barrier((slots, near_q, far_b))
+        if h == 2:
+            slots, far_a = lax.optimization_barrier((slots, far_a))
         res = attention(
             slots, flags, 1, h, [(q, h, 1)], keys, h, values, h, before, after, (h, LATE + h), got, 0, LATE
         )
         slots = tied(owners, res)
         sent.append(along(res, "segment", 1))
-    far_b = along(tied(far_b, res), "segment", -1)
+    far_b = along(far_b, "segment", -1)
 
     out = place(tied(sent[0], res), None, 0, q.shape[1])
+    out = place(tied(sent[1], res), out, 1)
     parts = [(near_q, 0, early_heads - FAR), (far_a, 0, 1), (far_b, 0, 1)]
     out = attention(
         owners_e, flags, early_heads, LATE, parts, high, 0, high, early_heads, before_e, after_e,
         (0, early_heads), got_e, LATE, early_heads, width=q.shape[1], out=out,
     )
-    for h in reversed(range(1, LATE)):
-        out = place(sent[h], out, h)
+    out = place(sent[2], out, 2)
     return out[None]
 
 

time: 197 us -> 194 us (0.985)
  waiting for transfers between devices: 87.5 us -> 85.5 us
    all_to_all x3, waiting for transfers between devices: 40.2 us -> 34 us  [exchange(): return lax.all_to_all(x, 'seq', split_axis=0, concat_axis=0, tiled=True)]
    ppermute x16, waiting for transfers between devices: 47.3 us -> 51.5 us  [along(): return lax.ppermute(x, axis, [(i, (i + by) % n) for i in range(n)])]
  transfers between devices with their start and end apart: 19 -> 19, of which waited for: 10 -> 9; matrix products, arithmetic and copies ran while one was open for 5% -> 5% of each run, Pallas kernels for 25% -> 26%
where the time goes in v4:
time: 194 us; the launch traced here: 193 us
  waiting for transfers between devices  85.5 us (44%)
  Pallas kernels  55.8 us (29%)
  starting transfers between devices  39.5 us (20%)
  local copies, waits for them, and re-layouts  9.28 us (5%)
    ppermute x16, waiting for transfers between devices, along(): return lax.ppermute(x, axis, [(i, (i + by) % n) for i in range(n)])  51.5 us
    pallas_call x4, Pallas kernels, attention(): pl.pallas_call(body, grid_spec=pltpu.PrefetchScalarGridSpec(num_scalar_pr...  37 us
    all_to_all x3, waiting for transfers between devices, exchange(): return lax.all_to_all(x, 'seq', split_axis=0, concat_axis=0, tiled=True)  34 us
    all_to_all x3, starting transfers between devices, exchange(): return lax.all_to_all(x, 'seq', split_axis=0, concat_axis=0, tiled=True)  22.2 us
    ppermute x16, starting transfers between devices, along(): return lax.ppermute(x, axis, [(i, (i + by) % n) for i in range(n)])  17.3 us
    pallas_call x3, Pallas kernels, place(): pl.pallas_call(body, in_specs=[here] * len(operands), out_specs=here, out...  6.26 us
    pallas_call x1, Pallas kernels, pack(): pl.pallas_call(body, grid_spec=pltpu.PrefetchScalarGridSpec(num_scalar_pr...  5.2 us
  transfers between devices with their start and end apart: 19, of which 9 were waited for; matrix products, arithmetic and copies ran while one was open for 5% of the time, Pallas kernels for 26%

profile of v4, /device:TPU:8, one launch (start us, length us, event | category | flops | bytes accessed | tf_op | source)
XLA Modules:
  0.0 193.0 jit_solution(16817369948708220619)
XLA Ops:
  0.0 3.7 %shard_map.55 = (bf16[32,80,128]{2,1,0:T(8,128)(2,1)}, bf16[512,1280]{1,0:T(8,128)(2,1)}, bf16[512,1024]{1,0:T(8,128)(2,1)}) custom-call(s32[3,1,8]{2,1,0:T(1,128)} %bitcast.29, s32[2]{0:T(128)} %bitcast.30, bf16[512,8192]{1,0:T(8,128)(2,1)} %bitcast.12, bf16[512,1024]{1,0:T(8,128)(2,1)} %bitcast.17, bf16[512,1024]{1,0:T(8,128)(2,1)} %bitcast.23), custom_call_target="tpu_custom_call" | custom-call | tf_op jit(solution)/shard_map/pallas_call | solution.py:115
  3.7 2.5 %collective-permute-start.4 = (bf16[512,1280]{1,0:T(8,128)(2,1)}, bf16[512,1280]{1,0:T(8,128)(2,1)}, u32[]{:S(2)}, u32[]{:S(2)}) collective-permute-start(bf16[512,1280]{1,0:T(8,128)(2,1)} %get-tuple-element.69), channel_id=1, source_target_pairs={{0,32},{32,64},{64,96},{96,0},{1,33},{33,65},{65,97},{97,1},{2,34}... | collective-permute-start | bytes 3932168 | tf_op jit(solution)/shard_map/ppermute | solution.py:41
  6.2 1.7 collective-permute-start.3
  7.9 0.0 copy-done
  7.9 0.0 copy-done.1
  7.9 19.6 %conditional.1 = (bf16[32,80,128]{2,1,0:T(8,128)(2,1)}, bf16[512,3072]{1,0:T(8,128)(2,1)}, bf16[512,1024]{1,0:T(8,128)(2,1)}, s32[24]{0:T(128)S(1)}, bf16[16,128...) conditional(s32[]{:T(128)} %convert_element_type.17, () %tuple.25, ...), branch_computations={%region_0.0_spmd, %region_1.2_spmd} | conditional | flops 393623 | bytes 11933234 | solution.py:437
  7.9 8.2 %all-to-all-start = ((bf16[32,80,128]{2,1,0:T(8,128)(2,1)}), bf16[32,80,128]{2,1,0:T(8,128)(2,1)}, u32[]{:S(2)}, u32[]{:S(2)}) async-start(bf16[32,80,128]{2,1,0:T(8,128)(2,1)} %get-tuple-element.19), calls=%async_computation | async-start | bytes 1310720 | tf_op jit(solution)/shard_map/cond/branch_1_fun/all_to_all | solution.py:45
  16.1 0.9 fusion.1
  17.0 0.2 collective-permute-start
  17.2 1.7 collective-permute-start.1
  18.9 0.6 fusion.3
  20.8 3.7 %slice.32 = bf16[512,3072]{1,0:T(8,128)(2,1)} slice(bf16[512,8192]{1,0:T(8,128)(2,1)} %get-tuple-element.20), slice={[0:512], [3072:6144]} | slice | bytes 6291456 | tf_op jit(solution)/shard_map/cond/branch_1_fun/slice | solution.py:422
  24.5 2.3 %slice.33 = bf16[512,1024]{1,0:T(8,128)(2,1)} slice(bf16[512,8192]{1,0:T(8,128)(2,1)} %get-tuple-element.20), slice={[0:512], [7168:8192]} | slice | bytes 2097152 | tf_op jit(solution)/shard_map/cond/branch_1_fun/slice | solution.py:422
  26.8 0.1 copy.10
  26.9 0.1 reshape_squeeze.2
  27.0 0.1 add_convert_fusion
  27.1 0.0 collective-permute-done
  27.1 0.0 collective-permute-done.1
  27.1 0.5 all-to-all-done
  27.6 3.6 %shard_map.56 = (bf16[32,416,128]{2,1,0:T(8,128)(2,1)}, bf16[96,128]{1,0:T(8,128)(2,1)}) custom-call(s32[1]{0:T(128)} %get-tuple-element.63.held, bf16[512,1024]{1,0:T(8,128)(2,1)} %bitcast.19, bf16[512,1024]{1,0:T(8,128)(2,1)} %bitcast.25, bf16[32,80,128]{2,1,0:T(8,128)(2,1)} %get-tuple-element.64.ask_ref.p_ref, ...), custom_call_target="tpu_custom_call" | custom-call | tf_op jit(solution)/shard_map/pallas_call | solution.py:198
  31.2 0.0 collective-permute-start.2
  31.2 6.2 %collective-permute-done.2 = bf16[96,128]{1,0:T(8,128)(2,1)S(1)} collective-permute-done((bf16[96,128]{1,0:T(8,128)(2,1)}, bf16[96,128]{1,0:T(8,128)(2,1)S(1)}, u32[]{:S(2)}, u32[]{:S(2)}) %collective-permute-start.2) | collective-permute-done | bytes 24608 | tf_op jit(solution)/shard_map/ppermute | solution.py:41
  37.3 0.0 collective-permute-done.3
  37.3 0.0 collective-permute-done.4.refs_0_.refs_3_.refs_4_
  37.3 8.1 %all-to-all-start.1 = ((bf16[32,416,128]{2,1,0:T(8,128)(2,1)}), bf16[32,416,128]{2,1,0:T(8,128)(2,1)}, u32[]{:S(2)}, u32[]{:S(2)}) async-start(bf16[32,416,128]{2,1,0:T(8,128)(2,1)} %get-tuple-element.70), calls=%async_computation.1 | async-start | bytes 6815744 | tf_op jit(solution)/shard_map/all_to_all | solution.py:45
  45.5 0.1 collective-permute-start.5
  45.6 3.2 %collective-permute-start.6 = (bf16[512,1024]{1,0:T(8,128)(2,1)}, bf16[512,1024]{1,0:T(8,128)(2,1)}, u32[]{:S(2)}, u32[]{:S(2)}) collective-permute-start(bf16[512,1024]{1,0:T(8,128)(2,1)} %get-tuple-element.76), channel_id=1, source_target_pairs={{0,96},{32,0},{64,32},{96,64},{1,97},{33,1},{65,33},{97,65},{2,98}... | collective-permute-start | bytes 3145736 | tf_op jit(solution)/shard_map/ppermute | solution.py:41
  48.8 0.6 slice.49.refs_1_
  49.4 0.5 collective-permute-start.8
  49.9 1.0 fusion.4
  51.0 0.1 collective-permute-start.12
  51.0 1.7 collective-permute-start.13
  52.8 0.7 convert_reduce_fusion.ask
  53.5 5.2 %shard_map.60 = bf16[32,688,128]{2,1,0:T(8,128)(2,1)} custom-call(s32[32]{0:T(128)} %convert_reduce_fusion.ask, bf16[512,1280]{1,0:T(8,128)(2,1)} %collective-permute-done.4.refs_0_.refs_3_.refs_4_, bf16[48,128]{1,0:T(8,128)(2,1)} %slice.49.refs_1_), custom_call_target="tpu_custom_call" | custom-call | tf_op jit(solution)/shard_map/pallas_call | solution.py:158
  58.7 0.5 bitcast_convert_fusion.slot
  59.2 29.5 %all-to-all-done.1.refs_7_.refs_8_.refs_9_ = bf16[32,416,128]{2,1,0:T(8,128)(2,1)} async-done(((bf16[32,416,128]{2,1,0:T(8,128)(2,1)}), bf16[32,416,128]{2,1,0:T(8,128)(2,1)}, u32[]{:S(2)}, u32[]{:S(2)}) %all-to-all-start.1) | async-done | bytes 3407904 | tf_op jit(solution)/shard_map/all_to_all | solution.py:45
  88.7 5.9 %all-to-all-start.2 = ((bf16[32,688,128]{2,1,0:T(8,128)(2,1)}), bf16[32,688,128]{2,1,0:T(8,128)(2,1)}, u32[]{:S(2)}, u32[]{:S(2)}) async-start(bf16[32,688,128]{2,1,0:T(8,128)(2,1)} %shard_map.60), calls=%async_computation.2 | async-start | bytes 11272192 | tf_op jit(solution)/shard_map/all_to_all | solution.py:45
  94.6 0.0 collective-permute-done.6
  94.6 1.8 collective-permute-start.7
  96.5 6.0 %shard_map.57 = bf16[512,1024]{1,0:T(8,128)(2,1)} custom-call(s32[24]{0:T(128)S(1)} %get-tuple-element.83.slot, s32[2]{0:T(128)S(1)} %get-tuple-element.60.flag, bf16[512,8192]{1,0:T(8,128)(2,1)} %bitcast.14, bf16[512,1024]{1,0:T(8,128)(2,1)} %bitcast.20, bf16[512,1024]{1,0:T(8,128)(2,1)} %bitcast.26, bf16[64,768]{1,0:T(8,128)(2,1)} %get-tuple-element.61.refs_3_.refs_4_, ...), custom_call_target="tpu_custom_call" | custom-call | flops 21474836480 | bytes 41943040 | tf_op jit(solution)/shard_map/pallas_call | solution.py:337
  102.5 0.0 collective-permute-done.8
  102.5 0.3 collective-permute-start.15
  102.8 15.3 %collective-permute-done.5.refs_0_ = bf16[512,3072]{1,0:T(8,128)(2,1)} collective-permute-done((bf16[512,3072]{1,0:T(8,128)(2,1)}, bf16[512,3072]{1,0:T(8,128)(2,1)}, u32[]{:S(2)}, u32[]{:S(2)}) %collective-permute-start.5) | collective-permute-done | bytes 3145760 | tf_op jit(solution)/shard_map/ppermute | solution.py:41
  118.0 0.5 collective-permute-start.9
  118.6 2.4 %collective-permute-done.7 = bf16[512,1024]{1,0:T(8,128)(2,1)} collective-permute-done((bf16[512,1024]{1,0:T(8,128)(2,1)}, bf16[512,1024]{1,0:T(8,128)(2,1)}, u32[]{:S(2)}, u32[]{:S(2)}) %collective-permute-start.7) | collective-permute-done | bytes 1048608 | tf_op jit(solution)/shard_map/ppermute | solution.py:41
  120.9 6.0 %shard_map.58 = bf16[512,1024]{1,0:T(8,128)(2,1)} custom-call(s32[24]{0:T(128)S(1)} %get-tuple-element.83.slot, s32[2]{0:T(128)S(1)} %get-tuple-element.60.flag, bf16[512,8192]{1,0:T(8,128)(2,1)} %bitcast.15, bf16[512,1024]{1,0:T(8,128)(2,1)} %bitcast.21, bf16[512,1024]{1,0:T(8,128)(2,1)} %bitcast.27, bf16[64,768]{1,0:T(8,128)(2,1)} %get-tuple-element.61.refs_3_.refs_4_, ...), custom_call_target="tpu_custom_call" | custom-call | flops 21474836480 | bytes 41943040 | tf_op jit(solution)/shard_map/pallas_call | solution.py:337
  126.9 0.0 collective-permute-start.14
  127.0 15.8 %collective-permute-done.9.refs_1_ = bf16[512,1024]{1,0:T(8,128)(2,1)} collective-permute-done((bf16[512,1024]{1,0:T(8,128)(2,1)}, bf16[512,1024]{1,0:T(8,128)(2,1)}, u32[]{:S(2)}, u32[]{:S(2)}) %collective-permute-start.9) | collective-permute-done | bytes 1048608 | tf_op jit(solution)/shard_map/ppermute | solution.py:41
  142.7 2.9 %collective-permute-start.11 = (bf16[512,1024]{1,0:T(8,128)(2,1)}, bf16[512,1024]{1,0:T(8,128)(2,1)}, u32[]{:S(2)}, u32[]{:S(2)}) collective-permute-start(bf16[512,1024]{1,0:T(8,128)(2,1)} %collective-permute-done.7), channel_id=1, source_target_pairs={{0,96},{32,0},{64,32},{96,64},{1,97},{33,1},{65,33},{97,65},{2,98}... | collective-permute-start | bytes 3145736 | tf_op jit(solution)/shard_map/ppermute | solution.py:41
  145.7 6.1 %shard_map.59 = bf16[512,1024]{1,0:T(8,128)(2,1)} custom-call(s32[24]{0:T(128)S(1)} %get-tuple-element.83.slot, s32[2]{0:T(128)S(1)} %get-tuple-element.60.flag, bf16[512,8192]{1,0:T(8,128)(2,1)} %bitcast.16, bf16[512,1024]{1,0:T(8,128)(2,1)} %bitcast.22, bf16[512,1024]{1,0:T(8,128)(2,1)} %bitcast.28, bf16[64,768]{1,0:T(8,128)(2,1)} %get-tuple-element.61.refs_3_.refs_4_, ...), custom_call_target="tpu_custom_call" | custom-call | flops 21474836480 | bytes 41943040 | tf_op jit(solution)/shard_map/pallas_call | solution.py:337
  151.7 0.0 collective-permute-done.15.p_ref
  151.7 0.0 collective-permute-start.10
  151.7 2.1 %shard_map.61.refs_0_ = bf16[512,8192]{1,0:T(8,128)(2,1)} custom-call(bf16[512,1024]{1,0:T(8,128)(2,1)} %collective-permute-done.15.p_ref), custom_call_target="tpu_custom_call" | custom-call | tf_op jit(solution)/shard_map/pallas_call | solution.py:379
  153.8 9.2 %collective-permute-done.14.p_ref = bf16[512,1024]{1,0:T(8,128)(2,1)} collective-permute-done((bf16[512,1024]{1,0:T(8,128)(2,1)}, bf16[512,1024]{1,0:T(8,128)(2,1)}, u32[]{:S(2)}, u32[]{:S(2)}) %collective-permute-start.14) | collective-permute-done | bytes 1048608 | tf_op jit(solution)/shard_map/ppermute | solution.py:41
  163.0 2.1 %shard_map.62.refs_12_ = bf16[512,8192]{1,0:T(8,128)(2,1)} custom-call(bf16[512,1024]{1,0:T(8,128)(2,1)} %collective-permute-done.14.p_ref, bf16[512,8192]{1,0:T(8,128)(2,1)} %shard_map.61.refs_0_), custom_call_target="tpu_custom_call", output_to_operand_aliasing={{}: (1, {})} | custom-call | tf_op jit(solution)/shard_map/pallas_call | solution.py:379
  165.1 0.0 collective-permute-done.12.refs_5_.refs_6_
  165.1 0.0 copy-start.2
  165.1 0.0 collective-permute-done.13.refs_7_.refs_8_
  165.1 2.8 %collective-permute-done.11.refs_2_ = bf16[512,1024]{1,0:T(8,128)(2,1)} collective-permute-done((bf16[512,1024]{1,0:T(8,128)(2,1)}, bf16[512,1024]{1,0:T(8,128)(2,1)}, u32[]{:S(2)}, u32[]{:S(2)}) %collective-permute-start.11) | collective-permute-done | bytes 1048608 | tf_op jit(solution)/shard_map/ppermute | solution.py:41
  167.9 4.0 %all-to-all-done.2.refs_9_.refs_10_.refs_11_ = bf16[32,688,128]{2,1,0:T(8,128)(2,1)} async-done(((bf16[32,688,128]{2,1,0:T(8,128)(2,1)}), bf16[32,688,128]{2,1,0:T(8,128)(2,1)}, u32[]{:S(2)}, u32[]{:S(2)}) %all-to-all-start.2) | async-done | bytes 5636128 | tf_op jit(solution)/shard_map/all_to_all | solution.py:45
  171.9 0.0 copy-done.2
  171.9 18.9 %shard_map.63.refs_0_ = bf16[512,8192]{1,0:T(8,128)(2,1)} custom-call(s32[24]{0:T(128)} %bitcast_convert_fusion.slot, s32[2]{0:T(128)S(1)} %get-tuple-element.60.flag, bf16[512,3072]{1,0:T(8,128)(2,1)} %collective-permute-done.5.refs_0_, bf16[512,1024]{1,0:T(8,128)(2,1)} %collective-permute-done.9.refs_1_, ...), custom_call_target="tpu_custom_call", output_to_operand_aliasing={{}: (14, {})} | custom-call | flops 107374182400 | bytes 209715200 | tf_op jit(solution)/shard_map/pallas_call | solution.py:337
  190.8 0.0 collective-permute-done.10.p_ref
  190.8 2.1 %shard_map.64 = bf16[512,8192]{1,0:T(8,128)(2,1)} custom-call(bf16[512,1024]{1,0:T(8,128)(2,1)} %collective-permute-done.10.p_ref, bf16[512,8192]{1,0:T(8,128)(2,1)} %shard_map.63.refs_0_), custom_call_target="tpu_custom_call", output_to_operand_aliasing={{}: (1, {})} | custom-call | tf_op jit(solution)/shard_map/pallas_call | solution.py:379
  (9 shorter events, 0.1 us)
Async XLA Ops:
  0.0 7.9 %copy-start = (s32[1,8,3]{1,0,2:T(1,128)S(1)}, s32[1,8,3]{1,0,2:T(1,128)}, u32[]{:S(2)}) copy-start(s32[1,8,3]{1,0,2:T(1,128)} %param.10) | copy-start | bytes 292
  0.0 7.9 %copy-start.1 = (s32[1,2]{1,0:T(1,128)S(1)}, s32[1,2]{1,0:T(1,128)}, u32[]{:S(2)}) copy-start(s32[1,2]{1,0:T(1,128)} %param.11) | copy-start | bytes 28
  3.7 33.6 %collective-permute-start.4 = (bf16[512,1280]{1,0:T(8,128)(2,1)}, bf16[512,1280]{1,0:T(8,128)(2,1)}, u32[]{:S(2)}, u32[]{:S(2)}) collective-permute-start(bf16[512,1280]{1,0:T(8,128)(2,1)} %get-tuple-element.69), channel_id=1, source_target_pairs={{0,32},{32,64},{64,96},{96,0},{1,33},{33,65},{65,97},{97,1},{2,34}... | collective-permute-start | bytes 3932168 | tf_op jit(solution)/shard_map/ppermute | solution.py:41
  6.2 31.1 %collective-permute-start.3 = (bf16[512,1024]{1,0:T(8,128)(2,1)}, bf16[512,1024]{1,0:T(8,128)(2,1)}, u32[]{:S(2)}, u32[]{:S(2)}) collective-permute-start(bf16[512,1024]{1,0:T(8,128)(2,1)} %get-tuple-element.68), channel_id=1, source_target_pairs={{0,96},{32,0},{64,32},{96,64},{1,97},{33,1},{65,33},{97,65},{2,98}... | collective-permute-start | bytes 3145736 | tf_op jit(solution)/shard_map/ppermute | solution.py:41
  7.9 19.6 %all-to-all-start = ((bf16[32,80,128]{2,1,0:T(8,128)(2,1)}), bf16[32,80,128]{2,1,0:T(8,128)(2,1)}, u32[]{:S(2)}, u32[]{:S(2)}) async-start(bf16[32,80,128]{2,1,0:T(8,128)(2,1)} %get-tuple-element.19), calls=%async_computation | async-start | bytes 1310720 | tf_op jit(solution)/shard_map/cond/branch_1_fun/all_to_all | solution.py:45
  17.0 10.1 %collective-permute-start = (bf16[64,768]{1,0:T(8,128)(2,1)S(1)}, bf16[64,768]{1,0:T(8,128)(2,1)}, u32[]{:S(2)}, u32[]{:S(2)}) collective-permute-start(bf16[64,768]{1,0:T(8,128)(2,1)S(1)} %pad_maximum_fusion), channel_id=1, source_target_pairs={{0,1},{1,2},{2,3},{3,4},{4,5},{5,6},{6,7},{7,8},{8,9},{9,10},{10,1... | collective-permute-start | bytes 294920 | tf_op jit(solution)/shard_map/cond/branch_1_fun/ppermute | solution.py:41
  17.2 9.9 %collective-permute-start.1 = (bf16[64,768]{1,0:T(8,128)(2,1)S(1)}, bf16[64,768]{1,0:T(8,128)(2,1)}, u32[]{:S(2)}, u32[]{:S(2)}) collective-permute-start(bf16[64,768]{1,0:T(8,128)(2,1)S(1)} %pad_maximum_fusion.1), channel_id=1, source_target_pairs={{0,31},{1,0},{2,1},{3,2},{4,3},{5,4},{6,5},{7,6},{8,7},{9,8},{10,9... | collective-permute-start | bytes 294920 | tf_op jit(solution)/shard_map/cond/branch_1_fun/ppermute | solution.py:41
  31.2 6.2 %collective-permute-start.2 = (bf16[96,128]{1,0:T(8,128)(2,1)}, bf16[96,128]{1,0:T(8,128)(2,1)S(1)}, u32[]{:S(2)}, u32[]{:S(2)}) collective-permute-start(bf16[96,128]{1,0:T(8,128)(2,1)} %get-tuple-element.67), channel_id=1, source_target_pairs={{0,32},{32,64},{64,96},{96,0},{1,33},{33,65},{65,97},{97,1},{2,34}... | collective-permute-start | bytes 73736 | tf_op jit(solution)/shard_map/ppermute | solution.py:41
  37.3 51.4 %all-to-all-start.1 = ((bf16[32,416,128]{2,1,0:T(8,128)(2,1)}), bf16[32,416,128]{2,1,0:T(8,128)(2,1)}, u32[]{:S(2)}, u32[]{:S(2)}) async-start(bf16[32,416,128]{2,1,0:T(8,128)(2,1)} %get-tuple-element.70), calls=%async_computation.1 | async-start | bytes 6815744 | tf_op jit(solution)/shard_map/all_to_all | solution.py:45
  45.5 72.5 %collective-permute-start.5 = (bf16[512,3072]{1,0:T(8,128)(2,1)}, bf16[512,3072]{1,0:T(8,128)(2,1)}, u32[]{:S(2)}, u32[]{:S(2)}) collective-permute-start(bf16[512,3072]{1,0:T(8,128)(2,1)} %get-tuple-element.74), channel_id=1, source_target_pairs={{0,32},{32,64},{64,96},{96,0},{1,33},{33,65},{65,97},{97,1},{2,34}... | collective-permute-start | bytes 9437192 | tf_op jit(solution)/shard_map/ppermute | solution.py:41
  45.6 49.1 %collective-permute-start.6 = (bf16[512,1024]{1,0:T(8,128)(2,1)}, bf16[512,1024]{1,0:T(8,128)(2,1)}, u32[]{:S(2)}, u32[]{:S(2)}) collective-permute-start(bf16[512,1024]{1,0:T(8,128)(2,1)} %get-tuple-element.76), channel_id=1, source_target_pairs={{0,96},{32,0},{64,32},{96,64},{1,97},{33,1},{65,33},{97,65},{2,98}... | collective-permute-start | bytes 3145736 | tf_op jit(solution)/shard_map/ppermute | solution.py:41
  49.4 53.1 %collective-permute-start.8 = (bf16[512,1024]{1,0:T(8,128)(2,1)}, bf16[512,1024]{1,0:T(8,128)(2,1)}, u32[]{:S(2)}, u32[]{:S(2)}) collective-permute-start(bf16[512,1024]{1,0:T(8,128)(2,1)} %collective-permute-done.3), channel_id=1, source_target_pairs={{0,96},{32,0},{64,32},{96,64},{1,97},{33,1},{65,33},{97,65},{2,98}... | collective-permute-start | bytes 3145736 | tf_op jit(solution)/shard_map/ppermute | solution.py:41
  51.0 114.1 %collective-permute-start.12 = (bf16[64,1280]{1,0:T(8,128)(2,1)S(1)}, bf16[64,1280]{1,0:T(8,128)(2,1)S(1)}, u32[]{:S(2)}, u32[]{:S(2)}) collective-permute-start(bf16[64,1280]{1,0:T(8,128)(2,1)S(1)} %get-tuple-element.115), channel_id=1, source_target_pairs={{0,1},{1,2},{2,3},{3,4},{4,5},{5,6},{6,7},{7,8},{8,9},{9,10},{10,1... | collective-permute-start | bytes 491528 | tf_op jit(solution)/shard_map/ppermute | solution.py:41
  51.0 114.1 %collective-permute-start.13 = (bf16[64,1280]{1,0:T(8,128)(2,1)S(1)}, bf16[64,1280]{1,0:T(8,128)(2,1)S(1)}, u32[]{:S(2)}, u32[]{:S(2)}) collective-permute-start(bf16[64,1280]{1,0:T(8,128)(2,1)S(1)} %get-tuple-element.114), channel_id=1, source_target_pairs={{0,31},{1,0},{2,1},{3,2},{4,3},{5,4},{6,5},{7,6},{8,7},{9,8},{10,9... | collective-permute-start | bytes 491528 | tf_op jit(solution)/shard_map/ppermute | solution.py:41
  88.7 83.1 %all-to-all-start.2 = ((bf16[32,688,128]{2,1,0:T(8,128)(2,1)}), bf16[32,688,128]{2,1,0:T(8,128)(2,1)}, u32[]{:S(2)}, u32[]{:S(2)}) async-start(bf16[32,688,128]{2,1,0:T(8,128)(2,1)} %shard_map.60), calls=%async_computation.2 | async-start | bytes 11272192 | tf_op jit(solution)/shard_map/all_to_all | solution.py:45
  94.6 26.3 %collective-permute-start.7 = (bf16[512,1024]{1,0:T(8,128)(2,1)}, bf16[512,1024]{1,0:T(8,128)(2,1)}, u32[]{:S(2)}, u32[]{:S(2)}) collective-permute-start(bf16[512,1024]{1,0:T(8,128)(2,1)} %collective-permute-done.6), channel_id=1, source_target_pairs={{0,96},{32,0},{64,32},{96,64},{1,97},{33,1},{65,33},{97,65},{2,98}... | collective-permute-start | bytes 3145736 | tf_op jit(solution)/shard_map/ppermute | solution.py:41
  102.5 49.2 %collective-permute-start.15 = (bf16[512,1024]{1,0:T(8,128)(2,1)}, bf16[512,1024]{1,0:T(8,128)(2,1)}, u32[]{:S(2)}, u32[]{:S(2)}) collective-permute-start(bf16[512,1024]{1,0:T(8,128)(2,1)} %shard_map.57), channel_id=1, source_target_pairs={{0,32},{32,64},{64,96},{96,0},{1,33},{33,65},{65,97},{97,1},{2,34}... | collective-permute-start | bytes 3145736 | tf_op jit(solution)/shard_map/ppermute | solution.py:41
  118.0 24.7 %collective-permute-start.9 = (bf16[512,1024]{1,0:T(8,128)(2,1)}, bf16[512,1024]{1,0:T(8,128)(2,1)}, u32[]{:S(2)}, u32[]{:S(2)}) collective-permute-start(bf16[512,1024]{1,0:T(8,128)(2,1)} %collective-permute-done.8), channel_id=1, source_target_pairs={{0,96},{32,0},{64,32},{96,64},{1,97},{33,1},{65,33},{97,65},{2,98}... | collective-permute-start | bytes 3145736 | tf_op jit(solution)/shard_map/ppermute | solution.py:41
  126.9 36.0 %collective-permute-start.14 = (bf16[512,1024]{1,0:T(8,128)(2,1)}, bf16[512,1024]{1,0:T(8,128)(2,1)}, u32[]{:S(2)}, u32[]{:S(2)}) collective-permute-start(bf16[512,1024]{1,0:T(8,128)(2,1)} %shard_map.58), channel_id=1, source_target_pairs={{0,32},{32,64},{64,96},{96,0},{1,33},{33,65},{65,97},{97,1},{2,34}... | collective-permute-start | bytes 3145736 | tf_op jit(solution)/shard_map/ppermute | solution.py:41
  142.7 25.2 %collective-permute-start.11 = (bf16[512,1024]{1,0:T(8,128)(2,1)}, bf16[512,1024]{1,0:T(8,128)(2,1)}, u32[]{:S(2)}, u32[]{:S(2)}) collective-permute-start(bf16[512,1024]{1,0:T(8,128)(2,1)} %collective-permute-done.7), channel_id=1, source_target_pairs={{0,96},{32,0},{64,32},{96,64},{1,97},{33,1},{65,33},{97,65},{2,98}... | collective-permute-start | bytes 3145736 | tf_op jit(solution)/shard_map/ppermute | solution.py:41
  151.7 39.0 %collective-permute-start.10 = (bf16[512,1024]{1,0:T(8,128)(2,1)}, bf16[512,1024]{1,0:T(8,128)(2,1)}, u32[]{:S(2)}, u32[]{:S(2)}) collective-permute-start(bf16[512,1024]{1,0:T(8,128)(2,1)} %shard_map.59), channel_id=1, source_target_pairs={{0,32},{32,64},{64,96},{96,0},{1,33},{33,65},{65,97},{97,1},{2,34}... | collective-permute-start | bytes 3145736 | tf_op jit(solution)/shard_map/ppermute | solution.py:41
  165.1 6.8 %copy-start.2 = (bf16[64,1280]{1,0:T(8,128)(2,1)}, bf16[64,1280]{1,0:T(8,128)(2,1)S(1)}, u32[]{:S(2)}) copy-start(bf16[64,1280]{1,0:T(8,128)(2,1)S(1)} %collective-permute-done.12.refs_5_.refs_6_) | copy-start | bytes 491524
  165.1 6.8 %copy-start.3 = (bf16[64,1280]{1,0:T(8,128)(2,1)}, bf16[64,1280]{1,0:T(8,128)(2,1)S(1)}, u32[]{:S(2)}) copy-start(bf16[64,1280]{1,0:T(8,128)(2,1)S(1)} %collective-permute-done.13.refs_7_.refs_8_) | copy-start | bytes 491524

commit v5 on v4

--- a/solution.py
+++ b/solution.py
@@ -419,14 +419,14 @@
         holder = jnp.where(me < DEVS // GLOB, listed[:1], listed[1:]) // BLOCKS
         flags = jnp.stack([me > 0, me < DEVS - 1]).astype(jnp.int32)
         return (
-            exchange(first), q[:, near_cols], q[:, (HEADS_KV - 1) * QW :],
+            exchange(first),
             owners, jnp.broadcast_to(row[None], (PIECE, HEAD)), holder, flags, *edges(keys[:, :cut], values[:, :cut]),
         )
 
     def ask_shapes(q):
         ints = [jnp.zeros((n,), jnp.int32) for n in (BLOCKS * RAND, 1, 2)]
         return (
-            jnp.zeros(first.shape, BF), q[:, near_cols], q[:, :QW],
+            jnp.zeros(first.shape, BF),
             ints[0], jnp.zeros((PIECE, HEAD), BF), ints[1], ints[2],
             jnp.zeros((BLOCK, 2 * cut), BF), jnp.zeros((BLOCK, 2 * cut), BF),
         )
@@ -434,12 +434,15 @@
     def no_ask(first, q, blocks, listed):
         return jax.tree.map(lambda x: jnp.zeros(x.shape, x.dtype), jax.eval_shape(ask_shapes, q))
 
-    message, near_q, far_b, owners, own_tile, holder, flags, before, after = lax.cond(
+    message, owners, own_tile, holder, flags, before, after = lax.cond(
         always, ask, no_ask, first, q, random_blocks[0], global_blocks[0]
     )
     packed, notes = pack_first(holder, keys, values, message, own_tile)
     notes = along(notes, "segment", 1)
-    packed, notes, far_a, high = lax.optimization_barrier((packed, notes, far_a, high))
+    near_q, far_b = q[:, near_cols], q[:, (HEADS_KV - 1) * QW :]
+    packed, notes, far_a, high, near_q, far_b = lax.optimization_barrier(
+        (packed, notes, far_a, high, near_q, far_b)
+    )
     got = exchange(packed)
     near_q = along(tied(near_q, notes), "segment", 1)
     far_b = along(tied(far_b, notes), "segment", -1)

time: 194 us -> 194 us (level)
  waiting for transfers between devices: 85.5 us -> 82.9 us
    ppermute x16, waiting for transfers between devices: 51.5 us -> 48.8 us  [along(): return lax.ppermute(x, axis, [(i, (i + by) % n) for i in range(n)])]
    ppermute x16, starting transfers between devices: 17.3 us -> 19.6 us  [along(): return lax.ppermute(x, axis, [(i, (i + by) % n) for i in range(n)])]
  transfers between devices with their start and end apart: 19 -> 19, of which waited for: 9 -> 11; matrix products, arithmetic and copies ran while one was open for 5% -> 5% of each run, Pallas kernels for 26% -> 26%
where the time goes in v5:
time: 194 us; the launch traced here: 193 us
  waiting for transfers between devices  82.9 us (43%)
  Pallas kernels  56.3 us (29%)
  starting transfers between devices  41.4 us (21%)
  local copies, waits for them, and re-layouts  9.26 us (5%)
    ppermute x16, waiting for transfers between devices, along(): return lax.ppermute(x, axis, [(i, (i + by) % n) for i in range(n)])  48.8 us
    pallas_call x4, Pallas kernels, attention(): pl.pallas_call(body, grid_spec=pltpu.PrefetchScalarGridSpec(num_scalar_pr...  37 us
    all_to_all x3, waiting for transfers between devices, exchange(): return lax.all_to_all(x, 'seq', split_axis=0, concat_axis=0, tiled=True)  34.1 us
    all_to_all x3, starting transfers between devices, exchange(): return lax.all_to_all(x, 'seq', split_axis=0, concat_axis=0, tiled=True)  21.9 us
    ppermute x16, starting transfers between devices, along(): return lax.ppermute(x, axis, [(i, (i + by) % n) for i in range(n)])  19.6 us
    pallas_call x3, Pallas kernels, place(): pl.pallas_call(body, in_specs=[here] * len(operands), out_specs=here, out...  6.26 us
    slice x2, local copies, waits for them, and re-layouts, per_device(): near_q, far_b = (q[:, near_cols], q[:, (HEADS_KV - 1) * QW:])  5.97 us
    pallas_call x1, Pallas kernels, pack(): pl.pallas_call(body, grid_spec=pltpu.PrefetchScalarGridSpec(num_scalar_pr...  5.2 us
  transfers between devices with their start and end apart: 19, of which 11 were waited for; matrix products, arithmetic and copies ran while one was open for 5% of the time, Pallas kernels for 26%

profile of v5, /device:TPU:8, one launch (start us, length us, event | category | flops | bytes accessed | tf_op | source)
XLA Modules:
  0.0 192.8 jit_solution(16237811968305786517)
XLA Ops:
  0.0 4.2 %shard_map.55 = (bf16[32,80,128]{2,1,0:T(8,128)(2,1)}, bf16[512,1280]{1,0:T(8,128)(2,1)}, bf16[512,1024]{1,0:T(8,128)(2,1)}) custom-call(s32[3,1,8]{2,1,0:T(1,128)} %bitcast.30, s32[2]{0:T(128)} %bitcast.31, bf16[512,8192]{1,0:T(8,128)(2,1)} %bitcast.12, bf16[512,1024]{1,0:T(8,128)(2,1)} %bitcast.18, bf16[512,1024]{1,0:T(8,128)(2,1)} %bitcast.24), custom_call_target="tpu_custom_call" | custom-call | tf_op jit(solution)/shard_map/pallas_call | solution.py:115
  4.3 2.0 %collective-permute-start.4 = (bf16[512,1280]{1,0:T(8,128)(2,1)}, bf16[512,1280]{1,0:T(8,128)(2,1)}, u32[]{:S(2)}, u32[]{:S(2)}) collective-permute-start(bf16[512,1280]{1,0:T(8,128)(2,1)} %get-tuple-element.66), channel_id=1, source_target_pairs={{0,32},{32,64},{64,96},{96,0},{1,33},{33,65},{65,97},{97,1},{2,34}... | collective-permute-start | bytes 3932168 | tf_op jit(solution)/shard_map/ppermute | solution.py:41
  6.2 1.7 collective-permute-start.3
  7.9 0.0 copy-done.1
  7.9 0.0 copy-done
  7.9 19.5 %conditional.1 = (bf16[32,80,128]{2,1,0:T(8,128)(2,1)}, s32[24]{0:T(128)S(1)}, bf16[16,128]{1,0:T(8,128)(2,1)S(1)}, s32[1]{0:T(128)}, s32[2]{0:T(128)S(1)}, /*in...) conditional(s32[]{:T(128)} %convert_element_type.17, () %tuple.25, (bf16[32,80,128]{2,1,0:T(8,128)(2,1)}, ...), branch_computations={%region_0.0_spmd, %region_1.2_spmd} | conditional | flops 393623 | bytes 3544610 | solution.py:437
  7.9 8.0 %all-to-all-start = ((bf16[32,80,128]{2,1,0:T(8,128)(2,1)}), bf16[32,80,128]{2,1,0:T(8,128)(2,1)}, u32[]{:S(2)}, u32[]{:S(2)}) async-start(bf16[32,80,128]{2,1,0:T(8,128)(2,1)} %get-tuple-element.17), calls=%async_computation | async-start | bytes 1310720 | tf_op jit(solution)/shard_map/cond/branch_1_fun/all_to_all | solution.py:45
  15.9 0.9 fusion.1
  16.8 0.2 collective-permute-start.1
  17.0 0.5 collective-permute-start
  17.5 0.6 fusion.3
  19.3 0.1 copy.10
  19.4 0.1 reshape_squeeze.2
  19.5 0.1 add_convert_fusion
  19.6 2.4 %collective-permute-done.1 = bf16[64,768]{1,0:T(8,128)(2,1)} collective-permute-done((bf16[64,768]{1,0:T(8,128)(2,1)S(1)}, bf16[64,768]{1,0:T(8,128)(2,1)}, u32[]{:S(2)}, u32[]{:S(2)}) %collective-permute-start.1) | collective-permute-done | bytes 98336 | tf_op jit(solution)/shard_map/cond/branch_1_fun/ppermute | solution.py:41
  22.0 3.1 %collective-permute-done = bf16[64,768]{1,0:T(8,128)(2,1)} collective-permute-done((bf16[64,768]{1,0:T(8,128)(2,1)S(1)}, bf16[64,768]{1,0:T(8,128)(2,1)}, u32[]{:S(2)}, u32[]{:S(2)}) %collective-permute-start) | collective-permute-done | bytes 98336 | tf_op jit(solution)/shard_map/cond/branch_1_fun/ppermute | solution.py:41
  25.2 2.2 %all-to-all-done = bf16[32,80,128]{2,1,0:T(8,128)(2,1)} async-done(((bf16[32,80,128]{2,1,0:T(8,128)(2,1)}), bf16[32,80,128]{2,1,0:T(8,128)(2,1)}, u32[]{:S(2)}, u32[]{:S(2)}) %all-to-all-start) | async-done | bytes 655392 | tf_op jit(solution)/shard_map/cond/branch_1_fun/all_to_all | solution.py:45
  27.4 3.6 %shard_map.56 = (bf16[32,416,128]{2,1,0:T(8,128)(2,1)}, bf16[96,128]{1,0:T(8,128)(2,1)}) custom-call(s32[1]{0:T(128)} %get-tuple-element.60.held, bf16[512,1024]{1,0:T(8,128)(2,1)} %bitcast.20, bf16[512,1024]{1,0:T(8,128)(2,1)} %bitcast.26, bf16[32,80,128]{2,1,0:T(8,128)(2,1)} %get-tuple-element.61.ask_ref.p_ref, ...), custom_call_target="tpu_custom_call" | custom-call | tf_op jit(solution)/shard_map/pallas_call | solution.py:198
  31.0 0.0 collective-permute-start.2
  31.0 3.7 %slice.52 = bf16[512,3072]{1,0:T(8,128)(2,1)} slice(bf16[512,8192]{1,0:T(8,128)(2,1)} %bitcast.13), slice={[0:512], [3072:6144]} | slice | bytes 6291456 | tf_op jit(solution)/shard_map/slice | solution.py:442
  34.7 2.3 %slice.53 = bf16[512,1024]{1,0:T(8,128)(2,1)} slice(bf16[512,8192]{1,0:T(8,128)(2,1)} %bitcast.14), slice={[0:512], [7168:8192]} | slice | bytes 2097152 | tf_op jit(solution)/shard_map/slice | solution.py:442
  37.0 0.3 collective-permute-done.2
  37.3 0.0 collective-permute-done.3
  37.3 0.0 collective-permute-done.4.refs_0_.refs_3_.refs_4_
  37.3 8.0 %all-to-all-start.1 = ((bf16[32,416,128]{2,1,0:T(8,128)(2,1)}), bf16[32,416,128]{2,1,0:T(8,128)(2,1)}, u32[]{:S(2)}, u32[]{:S(2)}) async-start(bf16[32,416,128]{2,1,0:T(8,128)(2,1)} %get-tuple-element.67), calls=%async_computation.1 | async-start | bytes 6815744 | tf_op jit(solution)/shard_map/all_to_all | solution.py:45
  45.3 1.3 collective-permute-start.5
  46.6 2.0 %collective-permute-start.6 = (bf16[512,1024]{1,0:T(8,128)(2,1)}, bf16[512,1024]{1,0:T(8,128)(2,1)}, u32[]{:S(2)}, u32[]{:S(2)}) collective-permute-start(bf16[512,1024]{1,0:T(8,128)(2,1)} %slice.53), channel_id=1, source_target_pairs={{0,96},{32,0},{64,32},{96,64},{1,97},{33,1},{65,33},{97,65},{2,98}... | collective-permute-start | bytes 3145736 | tf_op jit(solution)/shard_map/ppermute | solution.py:41
  48.6 0.6 slice.51.refs_1_
  49.2 1.4 collective-permute-start.8
  50.6 1.0 fusion.4
  51.6 0.1 collective-permute-start.12
  51.7 1.7 collective-permute-start.13
  53.4 0.7 convert_reduce_fusion.ask
  54.1 5.2 %shard_map.60 = bf16[32,688,128]{2,1,0:T(8,128)(2,1)} custom-call(s32[32]{0:T(128)} %convert_reduce_fusion.ask, bf16[512,1280]{1,0:T(8,128)(2,1)} %collective-permute-done.4.refs_0_.refs_3_.refs_4_, bf16[48,128]{1,0:T(8,128)(2,1)} %slice.51.refs_1_), custom_call_target="tpu_custom_call" | custom-call | tf_op jit(solution)/shard_map/pallas_call | solution.py:158
  59.3 0.5 bitcast_convert_fusion.slot
  59.9 28.7 %all-to-all-done.1.refs_7_.refs_8_.refs_9_ = bf16[32,416,128]{2,1,0:T(8,128)(2,1)} async-done(((bf16[32,416,128]{2,1,0:T(8,128)(2,1)}), bf16[32,416,128]{2,1,0:T(8,128)(2,1)}, u32[]{:S(2)}, u32[]{:S(2)}) %all-to-all-start.1) | async-done | bytes 3407904 | tf_op jit(solution)/shard_map/all_to_all | solution.py:45
  88.5 5.9 %all-to-all-start.2 = ((bf16[32,688,128]{2,1,0:T(8,128)(2,1)}), bf16[32,688,128]{2,1,0:T(8,128)(2,1)}, u32[]{:S(2)}, u32[]{:S(2)}) async-start(bf16[32,688,128]{2,1,0:T(8,128)(2,1)} %shard_map.60), calls=%async_computation.2 | async-start | bytes 11272192 | tf_op jit(solution)/shard_map/all_to_all | solution.py:45
  94.5 0.0 collective-permute-done.6
  94.5 2.6 %collective-permute-start.7 = (bf16[512,1024]{1,0:T(8,128)(2,1)}, bf16[512,1024]{1,0:T(8,128)(2,1)}, u32[]{:S(2)}, u32[]{:S(2)}) collective-permute-start(bf16[512,1024]{1,0:T(8,128)(2,1)} %collective-permute-done.6), channel_id=1, source_target_pairs={{0,96},{32,0},{64,32},{96,64},{1,97},{33,1},{65,33},{97,65},{2,98}... | collective-permute-start | bytes 3145736 | tf_op jit(solution)/shard_map/ppermute | solution.py:41
  97.1 6.0 %shard_map.57 = bf16[512,1024]{1,0:T(8,128)(2,1)} custom-call(s32[24]{0:T(128)S(1)} %get-tuple-element.80.slot, s32[2]{0:T(128)S(1)} %get-tuple-element.57.flag, bf16[512,8192]{1,0:T(8,128)(2,1)} %bitcast.15, bf16[512,1024]{1,0:T(8,128)(2,1)} %bitcast.21, bf16[512,1024]{1,0:T(8,128)(2,1)} %bitcast.27, bf16[64,768]{1,0:T(8,128)(2,1)} %get-tuple-element.58.refs_3_.refs_4_, ...), custom_call_target="tpu_custom_call" | custom-call | flops 21474836480 | bytes 41943040 | tf_op jit(solution)/shard_map/pallas_call | solution.py:337
  103.1 0.0 collective-permute-done.8
  103.1 0.0 collective-permute-start.15
  103.1 14.8 %collective-permute-done.5.refs_0_ = bf16[512,3072]{1,0:T(8,128)(2,1)} collective-permute-done((bf16[512,3072]{1,0:T(8,128)(2,1)}, bf16[512,3072]{1,0:T(8,128)(2,1)}, u32[]{:S(2)}, u32[]{:S(2)}) %collective-permute-start.5) | collective-permute-done | bytes 3145760 | tf_op jit(solution)/shard_map/ppermute | solution.py:41
  117.9 1.4 collective-permute-start.9
  119.2 1.7 collective-permute-done.7
  120.9 6.0 %shard_map.58 = bf16[512,1024]{1,0:T(8,128)(2,1)} custom-call(s32[24]{0:T(128)S(1)} %get-tuple-element.80.slot, s32[2]{0:T(128)S(1)} %get-tuple-element.57.flag, bf16[512,8192]{1,0:T(8,128)(2,1)} %bitcast.16, bf16[512,1024]{1,0:T(8,128)(2,1)} %bitcast.22, bf16[512,1024]{1,0:T(8,128)(2,1)} %bitcast.28, bf16[64,768]{1,0:T(8,128)(2,1)} %get-tuple-element.58.refs_3_.refs_4_, ...), custom_call_target="tpu_custom_call" | custom-call | flops 21474836480 | bytes 41943040 | tf_op jit(solution)/shard_map/pallas_call | solution.py:337
  126.9 1.2 collective-permute-start.14
  128.1 14.5 %collective-permute-done.9.refs_1_ = bf16[512,1024]{1,0:T(8,128)(2,1)} collective-permute-done((bf16[512,1024]{1,0:T(8,128)(2,1)}, bf16[512,1024]{1,0:T(8,128)(2,1)}, u32[]{:S(2)}, u32[]{:S(2)}) %collective-permute-start.9) | collective-permute-done | bytes 1048608 | tf_op jit(solution)/shard_map/ppermute | solution.py:41
  142.6 3.7 %collective-permute-start.11 = (bf16[512,1024]{1,0:T(8,128)(2,1)}, bf16[512,1024]{1,0:T(8,128)(2,1)}, u32[]{:S(2)}, u32[]{:S(2)}) collective-permute-start(bf16[512,1024]{1,0:T(8,128)(2,1)} %collective-permute-done.7), channel_id=1, source_target_pairs={{0,96},{32,0},{64,32},{96,64},{1,97},{33,1},{65,33},{97,65},{2,98}... | collective-permute-start | bytes 3145736 | tf_op jit(solution)/shard_map/ppermute | solution.py:41
  146.3 6.1 %shard_map.59 = bf16[512,1024]{1,0:T(8,128)(2,1)} custom-call(s32[24]{0:T(128)S(1)} %get-tuple-element.80.slot, s32[2]{0:T(128)S(1)} %get-tuple-element.57.flag, bf16[512,8192]{1,0:T(8,128)(2,1)} %bitcast.17, bf16[512,1024]{1,0:T(8,128)(2,1)} %bitcast.23, bf16[512,1024]{1,0:T(8,128)(2,1)} %bitcast.29, bf16[64,768]{1,0:T(8,128)(2,1)} %get-tuple-element.58.refs_3_.refs_4_, ...), custom_call_target="tpu_custom_call" | custom-call | flops 21474836480 | bytes 41943040 | tf_op jit(solution)/shard_map/pallas_call | solution.py:337
  152.3 0.0 collective-permute-done.15.p_ref
  152.3 0.0 collective-permute-start.10
  152.3 2.1 %shard_map.61.refs_0_ = bf16[512,8192]{1,0:T(8,128)(2,1)} custom-call(bf16[512,1024]{1,0:T(8,128)(2,1)} %collective-permute-done.15.p_ref), custom_call_target="tpu_custom_call" | custom-call | tf_op jit(solution)/shard_map/pallas_call | solution.py:379
  154.4 8.4 %collective-permute-done.14.p_ref = bf16[512,1024]{1,0:T(8,128)(2,1)} collective-permute-done((bf16[512,1024]{1,0:T(8,128)(2,1)}, bf16[512,1024]{1,0:T(8,128)(2,1)}, u32[]{:S(2)}, u32[]{:S(2)}) %collective-permute-start.14) | collective-permute-done | bytes 1048608 | tf_op jit(solution)/shard_map/ppermute | solution.py:41
  162.8 2.1 %shard_map.62.refs_12_ = bf16[512,8192]{1,0:T(8,128)(2,1)} custom-call(bf16[512,1024]{1,0:T(8,128)(2,1)} %collective-permute-done.14.p_ref, bf16[512,8192]{1,0:T(8,128)(2,1)} %shard_map.61.refs_0_), custom_call_target="tpu_custom_call", output_to_operand_aliasing={{}: (1, {})} | custom-call | tf_op jit(solution)/shard_map/pallas_call | solution.py:379
  164.9 0.0 collective-permute-done.12.refs_5_.refs_6_
  164.9 0.0 copy-start.2
  164.9 0.0 collective-permute-done.13.refs_7_.refs_8_
  164.9 0.0 copy-start.3
  164.9 3.6 %collective-permute-done.11.refs_2_ = bf16[512,1024]{1,0:T(8,128)(2,1)} collective-permute-done((bf16[512,1024]{1,0:T(8,128)(2,1)}, bf16[512,1024]{1,0:T(8,128)(2,1)}, u32[]{:S(2)}, u32[]{:S(2)}) %collective-permute-start.11) | collective-permute-done | bytes 1048608 | tf_op jit(solution)/shard_map/ppermute | solution.py:41
  168.5 3.2 %all-to-all-done.2.refs_9_.refs_10_.refs_11_ = bf16[32,688,128]{2,1,0:T(8,128)(2,1)} async-done(((bf16[32,688,128]{2,1,0:T(8,128)(2,1)}), bf16[32,688,128]{2,1,0:T(8,128)(2,1)}, u32[]{:S(2)}, u32[]{:S(2)}) %all-to-all-start.2) | async-done | bytes 5636128 | tf_op jit(solution)/shard_map/all_to_all | solution.py:45
  171.7 18.9 %shard_map.63.refs_0_ = bf16[512,8192]{1,0:T(8,128)(2,1)} custom-call(s32[24]{0:T(128)} %bitcast_convert_fusion.slot, s32[2]{0:T(128)S(1)} %get-tuple-element.57.flag, bf16[512,3072]{1,0:T(8,128)(2,1)} %collective-permute-done.5.refs_0_, bf16[512,1024]{1,0:T(8,128)(2,1)} %collective-permute-done.9.refs_1_, ...), custom_call_target="tpu_custom_call", output_to_operand_aliasing={{}: (14, {})} | custom-call | flops 107374182400 | bytes 209715200 | tf_op jit(solution)/shard_map/pallas_call | solution.py:337
  190.6 0.0 collective-permute-done.10.p_ref
  190.6 2.1 %shard_map.64 = bf16[512,8192]{1,0:T(8,128)(2,1)} custom-call(bf16[512,1024]{1,0:T(8,128)(2,1)} %collective-permute-done.10.p_ref, bf16[512,8192]{1,0:T(8,128)(2,1)} %shard_map.63.refs_0_), custom_call_target="tpu_custom_call", output_to_operand_aliasing={{}: (1, {})} | custom-call | tf_op jit(solution)/shard_map/pallas_call | solution.py:379
  (9 shorter events, 0.1 us)
Async XLA Ops:
  0.0 7.9 %copy-start.1 = (s32[1,2]{1,0:T(1,128)S(1)}, s32[1,2]{1,0:T(1,128)}, u32[]{:S(2)}) copy-start(s32[1,2]{1,0:T(1,128)} %param.11) | copy-start | bytes 28
  0.0 7.9 %copy-start = (s32[1,8,3]{1,0,2:T(1,128)S(1)}, s32[1,8,3]{1,0,2:T(1,128)}, u32[]{:S(2)}) copy-start(s32[1,8,3]{1,0,2:T(1,128)} %param.10) | copy-start | bytes 292
  4.3 33.1 %collective-permute-start.4 = (bf16[512,1280]{1,0:T(8,128)(2,1)}, bf16[512,1280]{1,0:T(8,128)(2,1)}, u32[]{:S(2)}, u32[]{:S(2)}) collective-permute-start(bf16[512,1280]{1,0:T(8,128)(2,1)} %get-tuple-element.66), channel_id=1, source_target_pairs={{0,32},{32,64},{64,96},{96,0},{1,33},{33,65},{65,97},{97,1},{2,34}... | collective-permute-start | bytes 3932168 | tf_op jit(solution)/shard_map/ppermute | solution.py:41
  6.2 31.1 %collective-permute-start.3 = (bf16[512,1024]{1,0:T(8,128)(2,1)}, bf16[512,1024]{1,0:T(8,128)(2,1)}, u32[]{:S(2)}, u32[]{:S(2)}) collective-permute-start(bf16[512,1024]{1,0:T(8,128)(2,1)} %get-tuple-element.65), channel_id=1, source_target_pairs={{0,96},{32,0},{64,32},{96,64},{1,97},{33,1},{65,33},{97,65},{2,98}... | collective-permute-start | bytes 3145736 | tf_op jit(solution)/shard_map/ppermute | solution.py:41
  7.9 19.5 %all-to-all-start = ((bf16[32,80,128]{2,1,0:T(8,128)(2,1)}), bf16[32,80,128]{2,1,0:T(8,128)(2,1)}, u32[]{:S(2)}, u32[]{:S(2)}) async-start(bf16[32,80,128]{2,1,0:T(8,128)(2,1)} %get-tuple-element.17), calls=%async_computation | async-start | bytes 1310720 | tf_op jit(solution)/shard_map/cond/branch_1_fun/all_to_all | solution.py:45
  16.8 5.2 %collective-permute-start.1 = (bf16[64,768]{1,0:T(8,128)(2,1)S(1)}, bf16[64,768]{1,0:T(8,128)(2,1)}, u32[]{:S(2)}, u32[]{:S(2)}) collective-permute-start(bf16[64,768]{1,0:T(8,128)(2,1)S(1)} %pad_maximum_fusion.1), channel_id=1, source_target_pairs={{0,31},{1,0},{2,1},{3,2},{4,3},{5,4},{6,5},{7,6},{8,7},{9,8},{10,9... | collective-permute-start | bytes 294920 | tf_op jit(solution)/shard_map/cond/branch_1_fun/ppermute | solution.py:41
  17.0 8.2 %collective-permute-start = (bf16[64,768]{1,0:T(8,128)(2,1)S(1)}, bf16[64,768]{1,0:T(8,128)(2,1)}, u32[]{:S(2)}, u32[]{:S(2)}) collective-permute-start(bf16[64,768]{1,0:T(8,128)(2,1)S(1)} %pad_maximum_fusion), channel_id=1, source_target_pairs={{0,1},{1,2},{2,3},{3,4},{4,5},{5,6},{6,7},{7,8},{8,9},{9,10},{10,1... | collective-permute-start | bytes 294920 | tf_op jit(solution)/shard_map/cond/branch_1_fun/ppermute | solution.py:41
  31.0 6.3 %collective-permute-start.2 = (bf16[96,128]{1,0:T(8,128)(2,1)}, bf16[96,128]{1,0:T(8,128)(2,1)S(1)}, u32[]{:S(2)}, u32[]{:S(2)}) collective-permute-start(bf16[96,128]{1,0:T(8,128)(2,1)} %get-tuple-element.64), channel_id=1, source_target_pairs={{0,32},{32,64},{64,96},{96,0},{1,33},{33,65},{65,97},{97,1},{2,34}... | collective-permute-start | bytes 73736 | tf_op jit(solution)/shard_map/ppermute | solution.py:41
  37.3 51.2 %all-to-all-start.1 = ((bf16[32,416,128]{2,1,0:T(8,128)(2,1)}), bf16[32,416,128]{2,1,0:T(8,128)(2,1)}, u32[]{:S(2)}, u32[]{:S(2)}) async-start(bf16[32,416,128]{2,1,0:T(8,128)(2,1)} %get-tuple-element.67), calls=%async_computation.1 | async-start | bytes 6815744 | tf_op jit(solution)/shard_map/all_to_all | solution.py:45
  45.3 72.5 %collective-permute-start.5 = (bf16[512,3072]{1,0:T(8,128)(2,1)}, bf16[512,3072]{1,0:T(8,128)(2,1)}, u32[]{:S(2)}, u32[]{:S(2)}) collective-permute-start(bf16[512,3072]{1,0:T(8,128)(2,1)} %slice.52), channel_id=1, source_target_pairs={{0,32},{32,64},{64,96},{96,0},{1,33},{33,65},{65,97},{97,1},{2,34}... | collective-permute-start | bytes 9437192 | tf_op jit(solution)/shard_map/ppermute | solution.py:41
  46.6 47.8 %collective-permute-start.6 = (bf16[512,1024]{1,0:T(8,128)(2,1)}, bf16[512,1024]{1,0:T(8,128)(2,1)}, u32[]{:S(2)}, u32[]{:S(2)}) collective-permute-start(bf16[512,1024]{1,0:T(8,128)(2,1)} %slice.53), channel_id=1, source_target_pairs={{0,96},{32,0},{64,32},{96,64},{1,97},{33,1},{65,33},{97,65},{2,98}... | collective-permute-start | bytes 3145736 | tf_op jit(solution)/shard_map/ppermute | solution.py:41
  49.2 53.9 %collective-permute-start.8 = (bf16[512,1024]{1,0:T(8,128)(2,1)}, bf16[512,1024]{1,0:T(8,128)(2,1)}, u32[]{:S(2)}, u32[]{:S(2)}) collective-permute-start(bf16[512,1024]{1,0:T(8,128)(2,1)} %collective-permute-done.3), channel_id=1, source_target_pairs={{0,96},{32,0},{64,32},{96,64},{1,97},{33,1},{65,33},{97,65},{2,98}... | collective-permute-start | bytes 3145736 | tf_op jit(solution)/shard_map/ppermute | solution.py:41
  51.6 113.3 %collective-permute-start.12 = (bf16[64,1280]{1,0:T(8,128)(2,1)S(1)}, bf16[64,1280]{1,0:T(8,128)(2,1)S(1)}, u32[]{:S(2)}, u32[]{:S(2)}) collective-permute-start(bf16[64,1280]{1,0:T(8,128)(2,1)S(1)} %get-tuple-element.110), channel_id=1, source_target_pairs={{0,1},{1,2},{2,3},{3,4},{4,5},{5,6},{6,7},{7,8},{8,9},{9,10},{10,1... | collective-permute-start | bytes 491528 | tf_op jit(solution)/shard_map/ppermute | solution.py:41
  51.7 113.2 %collective-permute-start.13 = (bf16[64,1280]{1,0:T(8,128)(2,1)S(1)}, bf16[64,1280]{1,0:T(8,128)(2,1)S(1)}, u32[]{:S(2)}, u32[]{:S(2)}) collective-permute-start(bf16[64,1280]{1,0:T(8,128)(2,1)S(1)} %get-tuple-element.109), channel_id=1, source_target_pairs={{0,31},{1,0},{2,1},{3,2},{4,3},{5,4},{6,5},{7,6},{8,7},{9,8},{10,9... | collective-permute-start | bytes 491528 | tf_op jit(solution)/shard_map/ppermute | solution.py:41
  88.5 83.1 %all-to-all-start.2 = ((bf16[32,688,128]{2,1,0:T(8,128)(2,1)}), bf16[32,688,128]{2,1,0:T(8,128)(2,1)}, u32[]{:S(2)}, u32[]{:S(2)}) async-start(bf16[32,688,128]{2,1,0:T(8,128)(2,1)} %shard_map.60), calls=%async_computation.2 | async-start | bytes 11272192 | tf_op jit(solution)/shard_map/all_to_all | solution.py:45
  94.5 26.4 %collective-permute-start.7 = (bf16[512,1024]{1,0:T(8,128)(2,1)}, bf16[512,1024]{1,0:T(8,128)(2,1)}, u32[]{:S(2)}, u32[]{:S(2)}) collective-permute-start(bf16[512,1024]{1,0:T(8,128)(2,1)} %collective-permute-done.6), channel_id=1, source_target_pairs={{0,96},{32,0},{64,32},{96,64},{1,97},{33,1},{65,33},{97,65},{2,98}... | collective-permute-start | bytes 3145736 | tf_op jit(solution)/shard_map/ppermute | solution.py:41
  103.1 49.2 %collective-permute-start.15 = (bf16[512,1024]{1,0:T(8,128)(2,1)}, bf16[512,1024]{1,0:T(8,128)(2,1)}, u32[]{:S(2)}, u32[]{:S(2)}) collective-permute-start(bf16[512,1024]{1,0:T(8,128)(2,1)} %shard_map.57), channel_id=1, source_target_pairs={{0,32},{32,64},{64,96},{96,0},{1,33},{33,65},{65,97},{97,1},{2,34}... | collective-permute-start | bytes 3145736 | tf_op jit(solution)/shard_map/ppermute | solution.py:41
  117.9 24.7 %collective-permute-start.9 = (bf16[512,1024]{1,0:T(8,128)(2,1)}, bf16[512,1024]{1,0:T(8,128)(2,1)}, u32[]{:S(2)}, u32[]{:S(2)}) collective-permute-start(bf16[512,1024]{1,0:T(8,128)(2,1)} %collective-permute-done.8), channel_id=1, source_target_pairs={{0,96},{32,0},{64,32},{96,64},{1,97},{33,1},{65,33},{97,65},{2,98}... | collective-permute-start | bytes 3145736 | tf_op jit(solution)/shard_map/ppermute | solution.py:41
  126.9 35.9 %collective-permute-start.14 = (bf16[512,1024]{1,0:T(8,128)(2,1)}, bf16[512,1024]{1,0:T(8,128)(2,1)}, u32[]{:S(2)}, u32[]{:S(2)}) collective-permute-start(bf16[512,1024]{1,0:T(8,128)(2,1)} %shard_map.58), channel_id=1, source_target_pairs={{0,32},{32,64},{64,96},{96,0},{1,33},{33,65},{65,97},{97,1},{2,34}... | collective-permute-start | bytes 3145736 | tf_op jit(solution)/shard_map/ppermute | solution.py:41
  142.6 25.9 %collective-permute-start.11 = (bf16[512,1024]{1,0:T(8,128)(2,1)}, bf16[512,1024]{1,0:T(8,128)(2,1)}, u32[]{:S(2)}, u32[]{:S(2)}) collective-permute-start(bf16[512,1024]{1,0:T(8,128)(2,1)} %collective-permute-done.7), channel_id=1, source_target_pairs={{0,96},{32,0},{64,32},{96,64},{1,97},{33,1},{65,33},{97,65},{2,98}... | collective-permute-start | bytes 3145736 | tf_op jit(solution)/shard_map/ppermute | solution.py:41
  152.3 38.2 %collective-permute-start.10 = (bf16[512,1024]{1,0:T(8,128)(2,1)}, bf16[512,1024]{1,0:T(8,128)(2,1)}, u32[]{:S(2)}, u32[]{:S(2)}) collective-permute-start(bf16[512,1024]{1,0:T(8,128)(2,1)} %shard_map.59), channel_id=1, source_target_pairs={{0,32},{32,64},{64,96},{96,0},{1,33},{33,65},{65,97},{97,1},{2,34}... | collective-permute-start | bytes 3145736 | tf_op jit(solution)/shard_map/ppermute | solution.py:41
  164.9 6.8 %copy-start.2 = (bf16[64,1280]{1,0:T(8,128)(2,1)}, bf16[64,1280]{1,0:T(8,128)(2,1)S(1)}, u32[]{:S(2)}) copy-start(bf16[64,1280]{1,0:T(8,128)(2,1)S(1)} %collective-permute-done.12.refs_5_.refs_6_) | copy-start | bytes 491524
  164.9 6.8 %copy-start.3 = (bf16[64,1280]{1,0:T(8,128)(2,1)}, bf16[64,1280]{1,0:T(8,128)(2,1)S(1)}, u32[]{:S(2)}) copy-start(bf16[64,1280]{1,0:T(8,128)(2,1)S(1)} %collective-permute-done.13.refs_7_.refs_8_) | copy-start | bytes 491524
